TPU v7x, 512 devices: a whole 4x8x8 slice. The times are simulated.
512 devices in a mesh: gx: 16 (over x, z_hi), gy: 32 (over y, z_lo, core).
Axes of the slice: x: 4, y: 8, z: 8 (z_hi: 4, z_lo: 2; z = z_hi * 2 + z_lo), core: 2. Of those that a mesh axis runs over, the one named last changes fastest.
Arguments:
- velocity: bfloat16 [3, 16, 64, 256, 128], P(None, 'gx', 'gy'), may hold values from -6 to 6
- position_code: int32 [16, 64, 256, 128], P('gx', 'gy'), may hold values from 0 to 511
- occupancy: int32 [16, 64, 256], P('gx', 'gy'), may hold values from 1 to 128
- shifts: int32 [4, 3], replicated, may hold values from 0 to 7
- axis_ids: int32 [4, 16, 64, 256], P(None, 'gx', 'gy'), may hold values from 0 to 31
Outputs:
- velocity_out: bfloat16 [3, 16, 64, 256, 128], P(None, 'gx', 'gy')
- cell_means: float32 [3, 16, 64, 256], P(None, 'gx', 'gy')
All inputs are finite; a program needn't handle non-finite values.
Results may differ from a plain program's by a relative error of at most 0.001.
Values sent between devices are 32-bit elements; how exact they have to be, the bound alone decides.
No kernel may reach another device: no remote copies, remote signals or barrier semaphores. Data moves between devices by JAX's collectives and lax.ppermute only.
A program may use at most 64 MiB of HBM per device.

v0:
```python
import math

import jax
import jax.numpy as jnp
from jax import lax
from jax.sharding import PartitionSpec as P

SUBDIV = 8
NAXES = 32
ITERS = 4


GOLDEN = 2.399963229728653
TURN_COS = math.cos(130.0 * math.pi / 180.0)
TURN_SIN = math.sin(130.0 * math.pi / 180.0)


def shifted(value, axis, steps):
    count = lax.axis_size(axis)
    pairs = [(source, (source + steps) % count) for source in range(count)]
    return lax.ppermute(value, axis, pairs)


def axis_table():
    ordinal = jnp.arange(NAXES).astype(jnp.float32)
    height = 1.0 - (2.0 * ordinal + 1.0) / NAXES
    radius = jnp.sqrt(1.0 - height * height)
    phases = ordinal * GOLDEN
    return jnp.stack([radius * jnp.cos(phases), radius * jnp.sin(phases), height])


def corner_steps(corner):
    return (corner // 4, corner // 2 % 2, corner % 2)


def corner_of(code_block, shift_now):
    sub_x = code_block // (SUBDIV * SUBDIV)
    sub_y = code_block // SUBDIV % SUBDIV
    sub_z = code_block % SUBDIV
    hop_x = (sub_x + shift_now[0] >= SUBDIV).astype(jnp.int32)
    hop_y = (sub_y + shift_now[1] >= SUBDIV).astype(jnp.int32)
    hop_z = (sub_z + shift_now[2] >= SUBDIV).astype(jnp.int32)
    return hop_x * 4 + hop_y * 2 + hop_z


def rotate_relative(velocity_in, mean_vec, normal):
    relative = velocity_in - mean_vec
    crossed = jnp.stack(
        [
            normal[1] * relative[2] - normal[2] * relative[1],
            normal[2] * relative[0] - normal[0] * relative[2],
            normal[0] * relative[1] - normal[1] * relative[0],
        ]
    )
    along_axis = jnp.sum(normal * relative, axis=0)
    return (
        mean_vec
        + TURN_COS * relative
        + TURN_SIN * crossed
        + (1.0 - TURN_COS) * along_axis[None] * normal
    )


def on_device(velocity, position_code, occupancy, shifts, axis_ids):
    rows_x, rows_y, depth_z = occupancy.shape
    slot_index = lax.broadcasted_iota(jnp.int32, position_code.shape, 3)
    filled = (slot_index < occupancy[..., None]).astype(jnp.float32)
    velocities = velocity.astype(jnp.float32) * filled[None]
    directions = axis_table()
    axis_range = lax.broadcasted_iota(jnp.int32, (NAXES, rows_x, rows_y, depth_z), 0)
    means_now = None
    for iteration in range(ITERS):
        corner_idx = corner_of(position_code, shifts[iteration])
        chosen_all = [(corner_idx == corner).astype(jnp.float32) for corner in range(8)]
        deposit_ext = jnp.zeros((4, rows_x + 1, rows_y + 1, depth_z), jnp.float32)
        for corner in range(8):
            step_x, step_y, step_z = corner_steps(corner)
            chosen = chosen_all[corner] * filled
            piece = jnp.concatenate(
                [jnp.sum(velocities * chosen[None], axis=-1), jnp.sum(chosen, axis=-1)[None]],
                axis=0,
            )
            rolled = jnp.roll(piece, step_z, axis=3)
            deposit_ext = deposit_ext + jnp.pad(
                rolled, ((0, 0), (step_x, 1 - step_x), (step_y, 1 - step_y), (0, 0))
            )
        onehot_axes = (axis_range == axis_ids[iteration][None]).astype(jnp.float32)
        normal = jnp.einsum(
            "dk,kxyz->dxyz", directions, onehot_axes, precision=lax.Precision.HIGHEST
        )
        from_prev = shifted(deposit_ext[:, rows_x], "gx", 1)
        deposit_ext = deposit_ext.at[:, 0].add(from_prev)
        from_left = shifted(deposit_ext[:, :rows_x, rows_y], "gy", 1)
        totals = deposit_ext[:, :rows_x, :rows_y].at[:, :, 0].add(from_left)
        means_now = totals[:3] / jnp.maximum(totals[3], 1.0)
        packed = jnp.concatenate([means_now, normal], axis=0)
        next_col = shifted(packed[:, :, 0], "gy", -1)
        packed_wide = jnp.concatenate([packed, next_col[:, :, None]], axis=2)
        next_row = shifted(packed_wide[:, 0], "gx", -1)
        extended = jnp.concatenate([packed_wide, next_row[:, None]], axis=1)
        gathered = jnp.zeros((6,) + position_code.shape, jnp.float32)
        for corner in range(8):
            step_x, step_y, step_z = corner_steps(corner)
            window = extended[:, step_x : step_x + rows_x, step_y : step_y + rows_y]
            window = jnp.roll(window, -step_z, axis=3)
            gathered = gathered + chosen_all[corner][None] * window[..., None]
        velocities = rotate_relative(velocities, gathered[:3], gathered[3:]) * filled[None]
    return (velocities.astype(jnp.bfloat16), means_now)


def solution(mesh):
    in_specs = (
        P(None, "gx", "gy", None, None),
        P("gx", "gy", None, None),
        P("gx", "gy", None),
        P(),
        P(None, "gx", "gy", None),
    )
    out_specs = (P(None, "gx", "gy", None, None), P(None, "gx", "gy", None))
    return jax.shard_map(
        on_device, mesh=mesh, in_specs=in_specs, out_specs=out_specs, check_vma=False
    )
```

profile of v0, /device:TPU:89, one launch (start us, length us, event | category | flops | bytes accessed | tf_op | source)
XLA Modules:
  0.0 155.3 jit_solution(1375910800332317098)
XLA Ops:
  0.6 1.8 %fusion.253 = (s32[1,1]{1,0:T(1,128)}, s32[1,1]{1,0:T(1,128)}, s32[1,1]{1,0:T(1,128)}, s32[1,1]{1,0:T(1,128)}, s32[1,1]{1,0:T(1,128)}, /*index=5*/s32[1,1]{1,0:T...) fusion(s32[4,3]{1,0:T(4,128)} %param.24), kind=kLoop, calls=%fused_computation.643 | loop fusion | bytes 96 | tf_op jit(solution)/shard_map/slice | solution.py:40
  2.4 0.8 fusion.80
  3.3 9.4 %convert_bitcast_fusion.28 = (f32[2,256,128]{2,1,0:T(8,128)S(1)}, pred[1,2,256,128]{3,2,1,0:T(8,128)(4,1)S(1)}, s32[1,2,256,128]{3,2,1,0:T(8,128)S(1)}, f32[2,25...) fusion(s32[]{:T(128)} %bitcast.14, s32[]{:T(128)} %bitcast.13, ...), kind=kLoop, calls=%fused_computation.134 | loop fusion | flops 6029312 | bytes 2621488 | tf_op jit(solution)/shard_map/mul | solution.py:106
  12.7 0.8 convert_bitcast_fusion.20
  13.5 1.3 fusion.16
  14.9 1.8 %multiply_reduce_fusion.35 = (f32[3,2,256]{2,1,0:T(2,128)S(1)}, f32[3,2,256]{2,1,0:T(2,128)S(1)}, f32[3,2,256]{2,1,0:T(2,128)S(1)}, f32[3,2,256]{2,1,0:T(2,128)S...) fusion(bf16[3,1,2,256,128]{4,3,2,1,0:T(8,128)(2,1)S(1)} %copy-d, ...), kind=kLoop, calls=%fused_computation.60 | loop fusion | flops 3526656 | bytes 2801664 | tf_op jit(solution)/shard_map/reduce_sum | solution.py:80
  17.3 5.8 %collective-permute-start = (f32[4,3,256]{2,0,1:T(4,128)S(1)}, f32[4,3,256]{2,0,1:T(4,128)S(1)}, u32[]{:S(2)}, u32[]{:S(2)}) collective-permute-start(f32[4,3,256]{2,0,1:T(4,128)S(1)} %slice_bitcast_fusion.15), channel_id=1, source_target_pairs={{0,32},{32,64},{64,96},{96,128},{128,160},{160,192},{192,224},{224... | collective-permute-start | bytes 36872 | tf_op jit(solution)/shard_map/ppermute | solution.py:21
  23.2 0.9 convert_bitcast_fusion.6
  24.1 1.7 %fusion.14 = (f32[2,256]{1,0:T(2,128)S(1)}, f32[2,256]{1,0:T(2,128)S(1)}, f32[2,256]{1,0:T(2,128)S(1)}, f32[2,256]{1,0:T(2,128)S(1)}, f32[2,256]{1,0:T(2,128)S(1...) fusion(pred[1,2,256,128]{3,2,1,0:T(8,128)(4,1)S(1)} %get-tuple-, ...), kind=kLoop, calls=%fused_computation.141 | loop fusion | flops 3595264 | bytes 5937152 | tf_op jit(solution)/shard_map/reduce_sum | solution.py:80
  25.7 4.7 %collective-permute-done = f32[4,3,256]{2,0,1:T(4,128)S(1)} collective-permute-done((f32[4,3,256]{2,0,1:T(4,128)S(1)}, f32[4,3,256]{2,0,1:T(4,128)S(1)}, u32[]{:S(2)}, u32[]{:S(2)}) %collective-permute-start) | collective-permute-done | bytes 12320 | tf_op jit(solution)/shard_map/ppermute | solution.py:21
  30.5 5.7 %collective-permute-start.1 = (f32[4,1,256]{2,0,1:T(4,128)S(1)}, f32[4,1,256]{2,0,1:T(4,128)S(1)}, u32[]{:S(2)}, u32[]{:S(2)}) collective-permute-start(f32[4,1,256]{2,0,1:T(4,128)S(1)} %slice_bitcast_fusion.19), channel_id=1, source_target_pairs={{0,1},{1,2},{2,3},{3,4},{4,5},{5,6},{6,7},{7,8},{8,9},{9,10},{10,1... | collective-permute-start | bytes 12296 | tf_op jit(solution)/shard_map/ppermute | solution.py:21
  36.4 0.5 collective-permute-done.1
  37.1 1.9 %collective-permute-start.2 = (f32[6,1,256]{2,0,1:T(8,128)S(1)}, f32[6,1,256]{2,0,1:T(8,128)S(1)}, u32[]{:S(2)}, u32[]{:S(2)}) collective-permute-start(f32[6,1,256]{2,0,1:T(8,128)S(1)} %fusion.216), channel_id=1, source_target_pairs={{0,31},{1,0},{2,1},{3,2},{4,3},{5,4},{6,5},{7,6},{8,7},{9,8},{10,9... | collective-permute-start | bytes 18440 | tf_op jit(solution)/shard_map/ppermute | solution.py:21
  39.1 5.6 %collective-permute-done.2 = f32[6,1,256]{2,0,1:T(8,128)S(1)} collective-permute-done((f32[6,1,256]{2,0,1:T(8,128)S(1)}, f32[6,1,256]{2,0,1:T(8,128)S(1)}, u32[]{:S(2)}, u32[]{:S(2)}) %collective-permute-start.2) | collective-permute-done | bytes 6176 | tf_op jit(solution)/shard_map/ppermute | solution.py:21
  44.8 4.5 %collective-permute-start.3 = (f32[6,3,256]{2,0,1:T(8,128)S(1)}, f32[6,3,256]{2,0,1:T(8,128)S(1)}, u32[]{:S(2)}, u32[]{:S(2)}) collective-permute-start(f32[6,3,256]{2,0,1:T(8,128)S(1)} %get-tuple-element.371), channel_id=1, source_target_pairs={{0,480},{32,0},{64,32},{96,64},{128,96},{160,128},{192,160},{224,1... | collective-permute-start | bytes 55304 | tf_op jit(solution)/shard_map/ppermute | solution.py:21
  49.4 0.8 collective-permute-done.3
  50.5 3.4 %multiply_add_fusion.3 = f32[6,1,2,256,128]{4,3,2,1,0:T(8,128)S(1)} fusion(f32[6,2,256]{2,1,0:T(2,128)S(1)} %copy.55, f32[2,256,128]{2,1,0:T(8,128)S(1)} %get-tuple-element.420, f32[6,2,256]{2,1,0:T(2,128)S(1)} %copy.54, f32[2,256,128]{2,1,0:T(8,128)S(1)} %get-tuple-element.418, f32[6,2,256]{2,1,0:T(2,128)S(1)} %copy.53, ...), kind=kLoop, calls=%fused_computation.3 | loop fusion | flops 5898240 | bytes 3768320 | tf_op jit(solution)/shard_map/add | solution.py:106
  54.3 1.8 %multiply_reduce_fusion.26 = (f32[3,2,256]{2,1,0:T(2,128)S(1)}, f32[3,2,256]{2,1,0:T(2,128)S(1)}, f32[3,2,256]{2,1,0:T(2,128)S(1)}, f32[3,2,256]{2,1,0:T(2,128)S...) fusion(f32[2,256,128]{2,1,0:T(8,128)S(1)} %get-tuple-element.33, ...), kind=kLoop, calls=%fused_computation.51 | loop fusion | flops 4902912 | bytes 6602752 | tf_op jit(solution)/shard_map/reduce_sum | solution.py:80
  56.6 2.2 %collective-permute-start.4 = (f32[4,3,256]{2,0,1:T(4,128)S(1)}, f32[4,3,256]{2,0,1:T(4,128)S(1)}, u32[]{:S(2)}, u32[]{:S(2)}) collective-permute-start(f32[4,3,256]{2,0,1:T(4,128)S(1)} %slice_bitcast_fusion.14), channel_id=1, source_target_pairs={{0,32},{32,64},{64,96},{96,128},{128,160},{160,192},{192,224},{224... | collective-permute-start | bytes 36872 | tf_op jit(solution)/shard_map/ppermute | solution.py:21
  58.8 6.8 %collective-permute-done.4 = f32[4,3,256]{2,0,1:T(4,128)S(1)} collective-permute-done((f32[4,3,256]{2,0,1:T(4,128)S(1)}, f32[4,3,256]{2,0,1:T(4,128)S(1)}, u32[]{:S(2)}, u32[]{:S(2)}) %collective-permute-start.4) | collective-permute-done | bytes 12320 | tf_op jit(solution)/shard_map/ppermute | solution.py:21
  65.6 4.3 %collective-permute-start.5 = (f32[4,1,256]{2,0,1:T(4,128)S(1)}, f32[4,1,256]{2,0,1:T(4,128)S(1)}, u32[]{:S(2)}, u32[]{:S(2)}) collective-permute-start(f32[4,1,256]{2,0,1:T(4,128)S(1)} %slice_bitcast_fusion.18), channel_id=1, source_target_pairs={{0,1},{1,2},{2,3},{3,4},{4,5},{5,6},{6,7},{7,8},{8,9},{9,10},{10,1... | collective-permute-start | bytes 12296 | tf_op jit(solution)/shard_map/ppermute | solution.py:21
  70.5 1.9 %collective-permute-start.6 = (f32[6,1,256]{2,0,1:T(8,128)S(1)}, f32[6,1,256]{2,0,1:T(8,128)S(1)}, u32[]{:S(2)}, u32[]{:S(2)}) collective-permute-start(f32[6,1,256]{2,0,1:T(8,128)S(1)} %fusion.213), channel_id=1, source_target_pairs={{0,31},{1,0},{2,1},{3,2},{4,3},{5,4},{6,5},{7,6},{8,7},{9,8},{10,9... | collective-permute-start | bytes 18440 | tf_op jit(solution)/shard_map/ppermute | solution.py:21
  72.6 5.6 %collective-permute-done.6 = f32[6,1,256]{2,0,1:T(8,128)S(1)} collective-permute-done((f32[6,1,256]{2,0,1:T(8,128)S(1)}, f32[6,1,256]{2,0,1:T(8,128)S(1)}, u32[]{:S(2)}, u32[]{:S(2)}) %collective-permute-start.6) | collective-permute-done | bytes 6176 | tf_op jit(solution)/shard_map/ppermute | solution.py:21
  78.3 4.4 %collective-permute-start.7 = (f32[6,3,256]{2,0,1:T(8,128)S(1)}, f32[6,3,256]{2,0,1:T(8,128)S(1)}, u32[]{:S(2)}, u32[]{:S(2)}) collective-permute-start(f32[6,3,256]{2,0,1:T(8,128)S(1)} %get-tuple-element.363), channel_id=1, source_target_pairs={{0,480},{32,0},{64,32},{96,64},{128,96},{160,128},{192,160},{224,1... | collective-permute-start | bytes 55304 | tf_op jit(solution)/shard_map/ppermute | solution.py:21
  82.8 1.0 collective-permute-done.7
  84.0 3.4 %multiply_add_fusion.2 = f32[6,1,2,256,128]{4,3,2,1,0:T(8,128)S(1)} fusion(f32[6,2,256]{2,1,0:T(2,128)S(1)} %copy.71, f32[2,256,128]{2,1,0:T(8,128)S(1)} %get-tuple-element.288, f32[6,2,256]{2,1,0:T(2,128)S(1)} %copy.70, f32[2,256,128]{2,1,0:T(8,128)S(1)} %get-tuple-element.278, f32[6,2,256]{2,1,0:T(2,128)S(1)} %copy.69, ...), kind=kLoop, calls=%fused_computation.2 | loop fusion | flops 5898240 | bytes 3768320 | tf_op jit(solution)/shard_map/add | solution.py:106
  87.7 1.8 %multiply_reduce_fusion.17 = (f32[3,2,256]{2,1,0:T(2,128)S(1)}, f32[3,2,256]{2,1,0:T(2,128)S(1)}, f32[3,2,256]{2,1,0:T(2,128)S(1)}, f32[3,2,256]{2,1,0:T(2,128)S...) fusion(f32[2,256,128]{2,1,0:T(8,128)S(1)} %get-tuple-element.34, ...), kind=kLoop, calls=%fused_computation.42 | loop fusion | flops 4902912 | bytes 6602752 | tf_op jit(solution)/shard_map/reduce_sum | solution.py:80
  90.0 1.9 %collective-permute-start.8 = (f32[4,3,256]{2,0,1:T(4,128)S(1)}, f32[4,3,256]{2,0,1:T(4,128)S(1)}, u32[]{:S(2)}, u32[]{:S(2)}) collective-permute-start(f32[4,3,256]{2,0,1:T(4,128)S(1)} %slice_bitcast_fusion.13), channel_id=1, source_target_pairs={{0,32},{32,64},{64,96},{96,128},{128,160},{160,192},{192,224},{224... | collective-permute-start | bytes 36872 | tf_op jit(solution)/shard_map/ppermute | solution.py:21
  92.0 6.9 %collective-permute-done.8 = f32[4,3,256]{2,0,1:T(4,128)S(1)} collective-permute-done((f32[4,3,256]{2,0,1:T(4,128)S(1)}, f32[4,3,256]{2,0,1:T(4,128)S(1)}, u32[]{:S(2)}, u32[]{:S(2)}) %collective-permute-start.8) | collective-permute-done | bytes 12320 | tf_op jit(solution)/shard_map/ppermute | solution.py:21
  98.8 4.1 %collective-permute-start.9 = (f32[4,1,256]{2,0,1:T(4,128)S(1)}, f32[4,1,256]{2,0,1:T(4,128)S(1)}, u32[]{:S(2)}, u32[]{:S(2)}) collective-permute-start(f32[4,1,256]{2,0,1:T(4,128)S(1)} %slice_bitcast_fusion.17), channel_id=1, source_target_pairs={{0,1},{1,2},{2,3},{3,4},{4,5},{5,6},{6,7},{7,8},{8,9},{9,10},{10,1... | collective-permute-start | bytes 12296 | tf_op jit(solution)/shard_map/ppermute | solution.py:21
  103.2 0.5 collective-permute-done.9
  103.8 1.9 %collective-permute-start.10 = (f32[6,1,256]{2,0,1:T(8,128)S(1)}, f32[6,1,256]{2,0,1:T(8,128)S(1)}, u32[]{:S(2)}, u32[]{:S(2)}) collective-permute-start(f32[6,1,256]{2,0,1:T(8,128)S(1)} %fusion.210), channel_id=1, source_target_pairs={{0,31},{1,0},{2,1},{3,2},{4,3},{5,4},{6,5},{7,6},{8,7},{9,8},{10,9... | collective-permute-start | bytes 18440 | tf_op jit(solution)/shard_map/ppermute | solution.py:21
  105.9 5.6 %collective-permute-done.10 = f32[6,1,256]{2,0,1:T(8,128)S(1)} collective-permute-done((f32[6,1,256]{2,0,1:T(8,128)S(1)}, f32[6,1,256]{2,0,1:T(8,128)S(1)}, u32[]{:S(2)}, u32[]{:S(2)}) %collective-permute-start.10) | collective-permute-done | bytes 6176 | tf_op jit(solution)/shard_map/ppermute | solution.py:21
  111.6 4.4 %collective-permute-start.11 = (f32[6,3,256]{2,0,1:T(8,128)S(1)}, f32[6,3,256]{2,0,1:T(8,128)S(1)}, u32[]{:S(2)}, u32[]{:S(2)}) collective-permute-start(f32[6,3,256]{2,0,1:T(8,128)S(1)} %get-tuple-element.355), channel_id=1, source_target_pairs={{0,480},{32,0},{64,32},{96,64},{128,96},{160,128},{192,160},{224,1... | collective-permute-start | bytes 55304 | tf_op jit(solution)/shard_map/ppermute | solution.py:21
  116.1 1.0 collective-permute-done.11
  117.3 3.4 %multiply_add_fusion.1 = f32[6,1,2,256,128]{4,3,2,1,0:T(8,128)S(1)} fusion(f32[6,2,256]{2,1,0:T(2,128)S(1)} %copy.87, f32[2,256,128]{2,1,0:T(8,128)S(1)} %get-tuple-element.394, f32[6,2,256]{2,1,0:T(2,128)S(1)} %copy.86, f32[2,256,128]{2,1,0:T(8,128)S(1)} %get-tuple-element.404, f32[6,2,256]{2,1,0:T(2,128)S(1)} %copy.85, ...), kind=kLoop, calls=%fused_computation.1 | loop fusion | flops 5898240 | bytes 3768320 | tf_op jit(solution)/shard_map/add | solution.py:106
  121.0 1.8 %multiply_reduce_fusion.8 = (f32[3,2,256]{2,1,0:T(2,128)S(1)}, f32[3,2,256]{2,1,0:T(2,128)S(1)}, f32[3,2,256]{2,1,0:T(2,128)S(1)}, f32[3,2,256]{2,1,0:T(2,128)S(...) fusion(f32[2,256,128]{2,1,0:T(8,128)S(1)} %get-tuple-element.33, ...), kind=kLoop, calls=%fused_computation.33 | loop fusion | flops 4902912 | bytes 6602752 | tf_op jit(solution)/shard_map/reduce_sum | solution.py:80
  123.3 1.9 %collective-permute-start.12 = (f32[4,3,256]{2,0,1:T(4,128)S(1)}, f32[4,3,256]{2,0,1:T(4,128)S(1)}, u32[]{:S(2)}, u32[]{:S(2)}) collective-permute-start(f32[4,3,256]{2,0,1:T(4,128)S(1)} %slice_bitcast_fusion.12), channel_id=1, source_target_pairs={{0,32},{32,64},{64,96},{96,128},{128,160},{160,192},{192,224},{224... | collective-permute-start | bytes 36872 | tf_op jit(solution)/shard_map/ppermute | solution.py:21
  125.2 6.9 %collective-permute-done.12 = f32[4,3,256]{2,0,1:T(4,128)S(1)} collective-permute-done((f32[4,3,256]{2,0,1:T(4,128)S(1)}, f32[4,3,256]{2,0,1:T(4,128)S(1)}, u32[]{:S(2)}, u32[]{:S(2)}) %collective-permute-start.12) | collective-permute-done | bytes 12320 | tf_op jit(solution)/shard_map/ppermute | solution.py:21
  132.1 4.1 %collective-permute-start.13 = (f32[4,1,256]{2,0,1:T(4,128)S(1)}, f32[4,1,256]{2,0,1:T(4,128)S(1)}, u32[]{:S(2)}, u32[]{:S(2)}) collective-permute-start(f32[4,1,256]{2,0,1:T(4,128)S(1)} %slice_bitcast_fusion.16), channel_id=1, source_target_pairs={{0,1},{1,2},{2,3},{3,4},{4,5},{5,6},{6,7},{7,8},{8,9},{9,10},{10,1... | collective-permute-start | bytes 12296 | tf_op jit(solution)/shard_map/ppermute | solution.py:21
  136.4 0.6 collective-permute-done.13
  137.1 1.9 %collective-permute-start.14 = (f32[6,1,256]{2,0,1:T(8,128)S(1)}, f32[6,1,256]{2,0,1:T(8,128)S(1)}, u32[]{:S(2)}, u32[]{:S(2)}) collective-permute-start(f32[6,1,256]{2,0,1:T(8,128)S(1)} %fusion.207), channel_id=1, source_target_pairs={{0,31},{1,0},{2,1},{3,2},{4,3},{5,4},{6,5},{7,6},{8,7},{9,8},{10,9... | collective-permute-start | bytes 18440 | tf_op jit(solution)/shard_map/ppermute | solution.py:21
  139.1 0.6 copy.104
  139.7 5.0 %collective-permute-done.14 = f32[6,1,256]{2,0,1:T(8,128)S(1)} collective-permute-done((f32[6,1,256]{2,0,1:T(8,128)S(1)}, f32[6,1,256]{2,0,1:T(8,128)S(1)}, u32[]{:S(2)}, u32[]{:S(2)}) %collective-permute-start.14) | collective-permute-done | bytes 6176 | tf_op jit(solution)/shard_map/ppermute | solution.py:21
  144.8 4.4 %collective-permute-start.15 = (f32[6,3,256]{2,0,1:T(8,128)S(1)}, f32[6,3,256]{2,0,1:T(8,128)S(1)}, u32[]{:S(2)}, u32[]{:S(2)}) collective-permute-start(f32[6,3,256]{2,0,1:T(8,128)S(1)} %get-tuple-element.347), channel_id=1, source_target_pairs={{0,480},{32,0},{64,32},{96,64},{128,96},{160,128},{192,160},{224,1... | collective-permute-start | bytes 55304 | tf_op jit(solution)/shard_map/ppermute | solution.py:21
  149.3 1.0 collective-permute-done.15
  150.6 3.4 %multiply_add_fusion = f32[6,1,2,256,128]{4,3,2,1,0:T(8,128)S(1)} fusion(f32[6,2,256]{2,1,0:T(2,128)S(1)} %copy.103, f32[2,256,128]{2,1,0:T(8,128)S(1)} %get-tuple-element.312, f32[6,2,256]{2,1,0:T(2,128)S(1)} %copy.102, f32[2,256,128]{2,1,0:T(8,128)S(1)} %get-tuple-element.302, f32[6,2,256]{2,1,0:T(2,128)S(1)} %copy.101, ...), kind=kLoop, calls=%fused_computation | loop fusion | flops 5898240 | bytes 3768320 | tf_op jit(solution)/shard_map/add | solution.py:106
  154.3 1.0 fusion.12
  (234 shorter events, 6.5 us)
Async XLA Ops:
  12.7 0.8 copy-start.1
  13.5 1.4 copy-start
  14.8 8.3 %copy-start.2 = (s32[4,1,2,256]{3,2,1,0:T(2,128)S(1)}, s32[4,1,2,256]{3,2,1,0:T(2,128)}, u32[]{:S(2)}) copy-start(s32[4,1,2,256]{3,2,1,0:T(2,128)} %param.25) | copy-start | bytes 24580
  17.3 13.2 %collective-permute-start = (f32[4,3,256]{2,0,1:T(4,128)S(1)}, f32[4,3,256]{2,0,1:T(4,128)S(1)}, u32[]{:S(2)}, u32[]{:S(2)}) collective-permute-start(f32[4,3,256]{2,0,1:T(4,128)S(1)} %slice_bitcast_fusion.15), channel_id=1, source_target_pairs={{0,32},{32,64},{64,96},{96,128},{128,160},{160,192},{192,224},{224... | collective-permute-start | bytes 36872 | tf_op jit(solution)/shard_map/ppermute | solution.py:21
  30.5 6.4 %collective-permute-start.1 = (f32[4,1,256]{2,0,1:T(4,128)S(1)}, f32[4,1,256]{2,0,1:T(4,128)S(1)}, u32[]{:S(2)}, u32[]{:S(2)}) collective-permute-start(f32[4,1,256]{2,0,1:T(4,128)S(1)} %slice_bitcast_fusion.19), channel_id=1, source_target_pairs={{0,1},{1,2},{2,3},{3,4},{4,5},{5,6},{6,7},{7,8},{8,9},{9,10},{10,1... | collective-permute-start | bytes 12296 | tf_op jit(solution)/shard_map/ppermute | solution.py:21
  37.1 7.6 %collective-permute-start.2 = (f32[6,1,256]{2,0,1:T(8,128)S(1)}, f32[6,1,256]{2,0,1:T(8,128)S(1)}, u32[]{:S(2)}, u32[]{:S(2)}) collective-permute-start(f32[6,1,256]{2,0,1:T(8,128)S(1)} %fusion.216), channel_id=1, source_target_pairs={{0,31},{1,0},{2,1},{3,2},{4,3},{5,4},{6,5},{7,6},{8,7},{9,8},{10,9... | collective-permute-start | bytes 18440 | tf_op jit(solution)/shard_map/ppermute | solution.py:21
  44.8 5.5 %collective-permute-start.3 = (f32[6,3,256]{2,0,1:T(8,128)S(1)}, f32[6,3,256]{2,0,1:T(8,128)S(1)}, u32[]{:S(2)}, u32[]{:S(2)}) collective-permute-start(f32[6,3,256]{2,0,1:T(8,128)S(1)} %get-tuple-element.371), channel_id=1, source_target_pairs={{0,480},{32,0},{64,32},{96,64},{128,96},{160,128},{192,160},{224,1... | collective-permute-start | bytes 55304 | tf_op jit(solution)/shard_map/ppermute | solution.py:21
  56.6 8.9 %collective-permute-start.4 = (f32[4,3,256]{2,0,1:T(4,128)S(1)}, f32[4,3,256]{2,0,1:T(4,128)S(1)}, u32[]{:S(2)}, u32[]{:S(2)}) collective-permute-start(f32[4,3,256]{2,0,1:T(4,128)S(1)} %slice_bitcast_fusion.14), channel_id=1, source_target_pairs={{0,32},{32,64},{64,96},{96,128},{128,160},{160,192},{192,224},{224... | collective-permute-start | bytes 36872 | tf_op jit(solution)/shard_map/ppermute | solution.py:21
  65.6 4.8 %collective-permute-start.5 = (f32[4,1,256]{2,0,1:T(4,128)S(1)}, f32[4,1,256]{2,0,1:T(4,128)S(1)}, u32[]{:S(2)}, u32[]{:S(2)}) collective-permute-start(f32[4,1,256]{2,0,1:T(4,128)S(1)} %slice_bitcast_fusion.18), channel_id=1, source_target_pairs={{0,1},{1,2},{2,3},{3,4},{4,5},{5,6},{6,7},{7,8},{8,9},{9,10},{10,1... | collective-permute-start | bytes 12296 | tf_op jit(solution)/shard_map/ppermute | solution.py:21
  70.5 7.6 %collective-permute-start.6 = (f32[6,1,256]{2,0,1:T(8,128)S(1)}, f32[6,1,256]{2,0,1:T(8,128)S(1)}, u32[]{:S(2)}, u32[]{:S(2)}) collective-permute-start(f32[6,1,256]{2,0,1:T(8,128)S(1)} %fusion.213), channel_id=1, source_target_pairs={{0,31},{1,0},{2,1},{3,2},{4,3},{5,4},{6,5},{7,6},{8,7},{9,8},{10,9... | collective-permute-start | bytes 18440 | tf_op jit(solution)/shard_map/ppermute | solution.py:21
  78.3 5.5 %collective-permute-start.7 = (f32[6,3,256]{2,0,1:T(8,128)S(1)}, f32[6,3,256]{2,0,1:T(8,128)S(1)}, u32[]{:S(2)}, u32[]{:S(2)}) collective-permute-start(f32[6,3,256]{2,0,1:T(8,128)S(1)} %get-tuple-element.363), channel_id=1, source_target_pairs={{0,480},{32,0},{64,32},{96,64},{128,96},{160,128},{192,160},{224,1... | collective-permute-start | bytes 55304 | tf_op jit(solution)/shard_map/ppermute | solution.py:21
  90.0 8.8 %collective-permute-start.8 = (f32[4,3,256]{2,0,1:T(4,128)S(1)}, f32[4,3,256]{2,0,1:T(4,128)S(1)}, u32[]{:S(2)}, u32[]{:S(2)}) collective-permute-start(f32[4,3,256]{2,0,1:T(4,128)S(1)} %slice_bitcast_fusion.13), channel_id=1, source_target_pairs={{0,32},{32,64},{64,96},{96,128},{128,160},{160,192},{192,224},{224... | collective-permute-start | bytes 36872 | tf_op jit(solution)/shard_map/ppermute | solution.py:21
  98.8 4.8 %collective-permute-start.9 = (f32[4,1,256]{2,0,1:T(4,128)S(1)}, f32[4,1,256]{2,0,1:T(4,128)S(1)}, u32[]{:S(2)}, u32[]{:S(2)}) collective-permute-start(f32[4,1,256]{2,0,1:T(4,128)S(1)} %slice_bitcast_fusion.17), channel_id=1, source_target_pairs={{0,1},{1,2},{2,3},{3,4},{4,5},{5,6},{6,7},{7,8},{8,9},{9,10},{10,1... | collective-permute-start | bytes 12296 | tf_op jit(solution)/shard_map/ppermute | solution.py:21
  103.8 7.6 %collective-permute-start.10 = (f32[6,1,256]{2,0,1:T(8,128)S(1)}, f32[6,1,256]{2,0,1:T(8,128)S(1)}, u32[]{:S(2)}, u32[]{:S(2)}) collective-permute-start(f32[6,1,256]{2,0,1:T(8,128)S(1)} %fusion.210), channel_id=1, source_target_pairs={{0,31},{1,0},{2,1},{3,2},{4,3},{5,4},{6,5},{7,6},{8,7},{9,8},{10,9... | collective-permute-start | bytes 18440 | tf_op jit(solution)/shard_map/ppermute | solution.py:21
  111.6 5.5 %collective-permute-start.11 = (f32[6,3,256]{2,0,1:T(8,128)S(1)}, f32[6,3,256]{2,0,1:T(8,128)S(1)}, u32[]{:S(2)}, u32[]{:S(2)}) collective-permute-start(f32[6,3,256]{2,0,1:T(8,128)S(1)} %get-tuple-element.355), channel_id=1, source_target_pairs={{0,480},{32,0},{64,32},{96,64},{128,96},{160,128},{192,160},{224,1... | collective-permute-start | bytes 55304 | tf_op jit(solution)/shard_map/ppermute | solution.py:21
  123.3 8.8 %collective-permute-start.12 = (f32[4,3,256]{2,0,1:T(4,128)S(1)}, f32[4,3,256]{2,0,1:T(4,128)S(1)}, u32[]{:S(2)}, u32[]{:S(2)}) collective-permute-start(f32[4,3,256]{2,0,1:T(4,128)S(1)} %slice_bitcast_fusion.12), channel_id=1, source_target_pairs={{0,32},{32,64},{64,96},{96,128},{128,160},{160,192},{192,224},{224... | collective-permute-start | bytes 36872 | tf_op jit(solution)/shard_map/ppermute | solution.py:21
  132.1 4.8 %collective-permute-start.13 = (f32[4,1,256]{2,0,1:T(4,128)S(1)}, f32[4,1,256]{2,0,1:T(4,128)S(1)}, u32[]{:S(2)}, u32[]{:S(2)}) collective-permute-start(f32[4,1,256]{2,0,1:T(4,128)S(1)} %slice_bitcast_fusion.16), channel_id=1, source_target_pairs={{0,1},{1,2},{2,3},{3,4},{4,5},{5,6},{6,7},{7,8},{8,9},{9,10},{10,1... | collective-permute-start | bytes 12296 | tf_op jit(solution)/shard_map/ppermute | solution.py:21
  137.1 7.6 %collective-permute-start.14 = (f32[6,1,256]{2,0,1:T(8,128)S(1)}, f32[6,1,256]{2,0,1:T(8,128)S(1)}, u32[]{:S(2)}, u32[]{:S(2)}) collective-permute-start(f32[6,1,256]{2,0,1:T(8,128)S(1)} %fusion.207), channel_id=1, source_target_pairs={{0,31},{1,0},{2,1},{3,2},{4,3},{5,4},{6,5},{7,6},{8,7},{9,8},{10,9... | collective-permute-start | bytes 18440 | tf_op jit(solution)/shard_map/ppermute | solution.py:21
  144.8 5.5 %collective-permute-start.15 = (f32[6,3,256]{2,0,1:T(8,128)S(1)}, f32[6,3,256]{2,0,1:T(8,128)S(1)}, u32[]{:S(2)}, u32[]{:S(2)}) collective-permute-start(f32[6,3,256]{2,0,1:T(8,128)S(1)} %get-tuple-element.347), channel_id=1, source_target_pairs={{0,480},{32,0},{64,32},{96,64},{128,96},{160,128},{192,160},{224,1... | collective-permute-start | bytes 55304 | tf_op jit(solution)/shard_map/ppermute | solution.py:21
where the time goes:
time: 156 us; the launch traced here: 155 us
  starting transfers between devices  55.4 us (36%)
  waiting for transfers between devices  52.6 us (34%)
  other arithmetic  41.3 us (26%)
  local copies, waits for them, and re-layouts  3.58 us (2%)
  between operations  1.86 us (1%)
    ppermute x16, starting transfers between devices, shifted(): return lax.ppermute(value, axis, pairs)  55.4 us
    ppermute x16, waiting for transfers between devices, shifted(): return lax.ppermute(value, axis, pairs)  52.6 us
    add x4, other arithmetic, on_device(): gathered = gathered + chosen_all[corner][None] * window[..., None]  13.7 us
    mul x23, other arithmetic, on_device(): gathered = gathered + chosen_all[corner][None] * window[..., None]  12.3 us
    reduce_sum x4, other arithmetic, on_device(): jnp.sum(velocities * chosen[None], axis=-1)  7.21 us
  transfers between devices with their start and end apart: 16, of which 16 were waited for; matrix products, arithmetic and copies ran while one was open for 3% of the time, Pallas kernels for 0%

commit v1 on v0

v1 whole, which is shorter than its diff:
```python
import functools
import math

import jax
import jax.numpy as jnp
import numpy as np
from jax import lax
from jax.experimental import pallas as pl
from jax.experimental.pallas import tpu as pltpu
from jax.sharding import PartitionSpec as P

SUBDIV = 8
NAXES = 32
ITERS = 4
GOLDEN = 2.399963229728653
TURN_COS = math.cos(130.0 * math.pi / 180.0)
TURN_SIN = math.sin(130.0 * math.pi / 180.0)
ALONG = (1.0 - TURN_COS) / (TURN_SIN * TURN_SIN)

F32 = jnp.float32
CHUNK = 32


def axis_table():
    ordinal = np.arange(NAXES, dtype=np.float64)
    height = 1.0 - (2.0 * ordinal + 1.0) / NAXES
    radius = np.sqrt(1.0 - height * height)
    phases = ordinal * GOLDEN
    return TURN_SIN * np.stack([radius * np.cos(phases), radius * np.sin(phases), height])


AXES = axis_table()


def is_odd(axis):
    return lax.rem(lax.axis_index(axis), 2) == 1


def hop_masks(code, shifts_ref, step):
    hop_x = code >= (SUBDIV - shifts_ref[step, 0]) * (SUBDIV * SUBDIV)
    hop_y = (code & (SUBDIV * SUBDIV - 1)) >= (SUBDIV - shifts_ref[step, 1]) * SUBDIV
    hop_z = (code & (SUBDIV - 1)) >= SUBDIV - shifts_ref[step, 2]
    return hop_x, hop_y, hop_z


def deposit(vel_ref, code_ref, shifts_ref, step, mom_ref, sums_ref):
    for col in range(2):
        for half in range(2):
            lanes = slice(half * 128, half * 128 + 128)

            def body(i, acc):
                rows = pl.ds(pl.multiple_of(i * 8, 8), 8)
                code = code_ref[col, rows, lanes]
                hop_x, hop_y, hop_z = hop_masks(code, shifts_ref, step)
                parts = [vel_ref[comp * 2 + col, rows, lanes] for comp in range(3)]
                parts.append(jnp.where(code >= 0, 1.0, 0.0))
                out = list(acc)
                for comp, value in enumerate(parts):
                    with_x = jnp.where(hop_x, value, 0.0)
                    with_y = jnp.where(hop_y, value, 0.0)
                    with_xy = jnp.where(hop_y, with_x, 0.0)
                    for pair, base in ((0, value), (2, with_y), (4, with_x), (6, with_xy)):
                        at = comp * 8 + pair
                        out[at] = out[at] + base
                        out[at + 1] = out[at + 1] + jnp.where(hop_z, base, 0.0)
                return tuple(out)

            zero = jnp.zeros((8, 128), F32)
            acc = lax.fori_loop(0, 16, body, (zero,) * 32, unroll=2)
            for comp in range(4):
                for moment in range(8):
                    row = (col * 8 + moment) * 8 + comp
                    mom_ref[row : row + 1, lanes] = jnp.sum(acc[comp * 8 + moment], axis=0, keepdims=True)
    pieces = {}
    for col in range(2):
        def moment_of(moment):
            row = (col * 8 + moment) * 8
            return mom_ref[row : row + 8, :]

        quads = {}
        for moment in (0, 2, 4, 6):
            up = moment_of(moment + 1)
            quads[moment] = moment_of(moment) - up + pltpu.roll(up, 1, 1)
        pieces[col, 1, 1] = quads[6]
        pieces[col, 1, 0] = quads[4] - quads[6]
        pieces[col, 0, 1] = quads[2] - quads[6]
        pieces[col, 0, 0] = quads[0] - quads[2] - quads[4] + quads[6]
    for hop in range(2):
        columns = (pieces[0, hop, 0], pieces[0, hop, 1] + pieces[1, hop, 0], pieces[1, hop, 1])
        for at, piece in enumerate(columns):
            row = (hop * 3 + at) * 4
            sums_ref[row : row + 4, :] = piece[0:4, :]


def fill_messages_y(sums_ref, odd_ref, even_ref):
    odd = is_odd("gy")
    for hop in range(2):
        left = sums_ref[hop * 12 : hop * 12 + 4, :]
        right = sums_ref[hop * 12 + 8 : hop * 12 + 12, :]
        odd_ref[hop * 4 : hop * 4 + 4, :] = jnp.where(odd, right, left)
        even_ref[hop * 4 : hop * 4 + 4, :] = jnp.where(odd, left, right)


def start_kernel(shifts_ref, vel_in_ref, code_in_ref, occ_ref, ids_ref, vel_ref, code_ref, sums_ref, odd_ref, even_ref, mom_ref):
    slot = lax.broadcasted_iota(jnp.int32, (128, 256), 0)
    for col in range(2):
        filled = slot < occ_ref[col : col + 1, :]
        code_ref[col] = jnp.where(filled, code_in_ref[col].T, -1)
        for comp in range(3):
            vel_ref[comp * 2 + col] = jnp.where(filled, vel_in_ref[comp * 2 + col].astype(F32).T, 0.0)
    mom_ref[...] = jnp.zeros_like(mom_ref)
    deposit(vel_ref, code_ref, shifts_ref, 0, mom_ref, sums_ref)
    fill_messages_y(sums_ref, odd_ref, even_ref)
    for step in range(ITERS):
        ids = ids_ref[step * 2 : step * 2 + 1, :].astype(F32)
        odd_ref[8 + step : 9 + step, :] = ids
        even_ref[8 + step : 9 + step, :] = ids


def middle_kernel(first, *refs):
    if first:
        sums_ref, from_odd_ref, from_even_ref, ids_ref, out_ref, odd_ref, even_ref = refs
    else:
        sums_ref, from_odd_ref, from_even_ref, out_ref, odd_ref, even_ref = refs
    odd_y, odd_x = is_odd("gy"), is_odd("gx")
    out_ref[0:24, :] = sums_ref[...]
    for hop in range(2):
        rows = slice(hop * 4, hop * 4 + 4)
        by_odd, by_even = from_odd_ref[rows, :], from_even_ref[rows, :]
        left = slice(hop * 12, hop * 12 + 4)
        right = slice(hop * 12 + 8, hop * 12 + 12)
        out_ref[left, :] = out_ref[left, :] + jnp.where(odd_y, by_even, by_odd)
        out_ref[right, :] = out_ref[right, :] + jnp.where(odd_y, by_odd, by_even)
    low, high = out_ref[0:12, :], out_ref[12:24, :]
    odd_ref[0:12, :] = jnp.where(odd_x, high, low)
    even_ref[0:12, :] = jnp.where(odd_x, low, high)
    if first:
        for step in range(ITERS):
            row = 24 + step * 3
            out_ref[row : row + 2, :] = ids_ref[step * 2 : step * 2 + 2, :].astype(F32)
            by_odd, by_even = from_odd_ref[8 + step : 9 + step, :], from_even_ref[8 + step : 9 + step, :]
            out_ref[row + 2 : row + 3, :] = jnp.where(odd_y, by_odd, by_even)
        own = out_ref[24:36, :]
        odd_ref[12:24, :] = own
        even_ref[12:24, :] = own


def totals_and_axes(step, sums_ref, from_odd_ref, from_even_ref, ids, mean_ref, axis_ref):
    odd_x = is_odd("gx")
    by_odd, by_even = from_odd_ref[0:12, :], from_even_ref[0:12, :]
    mean_ref[0, 0:12, :] = sums_ref[0:12, :] + jnp.where(odd_x, by_even, by_odd)
    mean_ref[0, 12:24, :] = sums_ref[12:24, :] + jnp.where(odd_x, by_odd, by_even)
    for cell in range(6):
        count = jnp.maximum(mean_ref[0, cell * 4 + 3 : cell * 4 + 4, :], 1.0)
        mean_ref[0, cell * 4 : cell * 4 + 3, :] = mean_ref[0, cell * 4 : cell * 4 + 3, :] / count
    mean_ref[1] = pltpu.roll(mean_ref[0], 255, 1)
    axes = [jnp.zeros((8, 256), F32) for _ in range(3)]
    for k in range(NAXES):
        match = ids == float(k)
        axes = [jnp.where(match, float(AXES[comp, k]), axes[comp]) for comp in range(3)]
    for comp in range(3):
        axis_ref[0, comp] = axes[comp]
        axis_ref[1, comp] = pltpu.roll(axes[comp], 255, 1)


def rotate(step, vel_ref, code_ref, shifts_ref, mean_ref, axis_ref, out_ref):
    for col in range(2):
        for half in range(2):
            lanes = slice(half * 128, half * 128 + 128)

            def body(i, carry):
                rows = pl.ds(pl.multiple_of(i * CHUNK, CHUNK), CHUNK)
                code = code_ref[col, rows, lanes]
                hop_x, hop_y, hop_z = hop_masks(code, shifts_ref, step)

                def pick(row_of):
                    by_x = []
                    for step_x in range(2):
                        by_y = []
                        for step_y in range(2):
                            cell = step_x * 3 + col + step_y
                            by_y.append(jnp.where(hop_z, row_of(1, cell), row_of(0, cell)))
                        by_x.append(jnp.where(hop_y, by_y[1], by_y[0]))
                    return jnp.where(hop_x, by_x[1], by_x[0])

                mean, rel, axis = [], [], []
                for comp in range(3):
                    mean.append(pick(lambda z, cell: mean_ref[z, cell * 4 + comp : cell * 4 + comp + 1, lanes]))
                    axis.append(pick(lambda z, cell: axis_ref[z, comp, cell : cell + 1, lanes]))
                    rel.append(vel_ref[comp * 2 + col, rows, lanes] - mean[comp])
                along = (axis[0] * rel[0] + axis[1] * rel[1] + axis[2] * rel[2]) * ALONG
                filled = code >= 0
                for comp in range(3):
                    b, c = (comp + 1) % 3, (comp + 2) % 3
                    value = mean[comp] + TURN_COS * rel[comp] + (axis[b] * rel[c] - axis[c] * rel[b]) + along * axis[comp]
                    out_ref[comp * 2 + col, rows, lanes] = jnp.where(filled, value, 0.0)
                return carry

            lax.fori_loop(0, 128 // CHUNK, body, 0)


def step_kernel(step, *refs):
    if step == 0:
        shifts_ref, vel_ref, code_ref, sums_ref, from_odd_ref, from_even_ref, *refs = refs
        out_ref, ids_ref, new_ref, odd_ref, even_ref, mom_ref, mean_ref, axis_ref = refs
        odd_x = is_odd("gx")
        ids_ref[...] = jnp.zeros_like(ids_ref)
        for t in range(ITERS):
            ids_ref[t * 8 : t * 8 + 3, :] = sums_ref[24 + t * 3 : 27 + t * 3, :]
            rows = slice(12 + t * 3, 15 + t * 3)
            ids_ref[t * 8 + 3 : t * 8 + 6, :] = jnp.where(odd_x, from_odd_ref[rows, :], from_even_ref[rows, :])
    else:
        shifts_ref, vel_ref, code_ref, sums_ref, from_odd_ref, from_even_ref, ids_ref, *refs = refs
        if step < ITERS - 1:
            out_ref, new_ref, odd_ref, even_ref, mom_ref, mean_ref, axis_ref = refs
        else:
            final_ref, final_means_ref, out_ref, mean_ref, axis_ref = refs
    ids = ids_ref[step * 8 : step * 8 + 8, :]
    totals_and_axes(step, sums_ref, from_odd_ref, from_even_ref, ids, mean_ref, axis_ref)
    rotate(step, vel_ref, code_ref, shifts_ref, mean_ref, axis_ref, out_ref)
    if step < ITERS - 1:
        mom_ref[...] = jnp.zeros_like(mom_ref)
        deposit(out_ref, code_ref, shifts_ref, step + 1, mom_ref, new_ref)
        fill_messages_y(new_ref, odd_ref, even_ref)
    else:
        for at in range(6):
            final_ref[at] = out_ref[at].T.astype(jnp.bfloat16)
        for comp in range(3):
            for col in range(2):
                final_means_ref[comp * 2 + col : comp * 2 + col + 1, :] = mean_ref[0, col * 4 + comp : col * 4 + comp + 1, :]


VMEM = pl.BlockSpec(memory_space=pltpu.VMEM)
SMEM = pl.BlockSpec(memory_space=pltpu.SMEM)


def call(kernel, name, n_in, shapes, scratch, smem=True):
    return pl.pallas_call(
        kernel,
        out_shape=[jax.ShapeDtypeStruct(s, d) for s, d in shapes],
        in_specs=([SMEM] if smem else []) + [VMEM] * n_in,
        out_specs=[VMEM] * len(shapes),
        scratch_shapes=scratch,
        compiler_params=pltpu.CompilerParams(vmem_limit_bytes=16 * 1024 * 1024),
        name=name,
    )


def swap(odd, even, axis):
    count = lax.axis_size(axis)
    evens = [(s, s ^ 1) for s in range(count)]
    odds = [(s, (((s - 1) % count ^ 1) + 1) % count) for s in range(count)]
    from_even = lax.ppermute(even, axis, evens)
    from_odd = lax.ppermute(odd, axis, odds)
    return from_odd, from_even


def on_device(velocity, position_code, occupancy, shifts, axis_ids):
    vel_in = velocity.reshape(6, 256, 128)
    code_in = position_code.reshape(2, 256, 128)
    occ = occupancy.reshape(2, 256)
    ids_in = axis_ids.reshape(8, 256)
    vel_shape, code_shape = ((6, 128, 256), F32), ((2, 128, 256), jnp.int32)
    moments = pltpu.VMEM((128, 256), F32)
    means = pltpu.VMEM((2, 24, 256), F32)
    axes = pltpu.VMEM((2, 3, 8, 256), F32)

    vel, code, sums, odd, even = call(
        start_kernel, "start", 4,
        [vel_shape, code_shape, ((24, 256), F32), ((12, 256), F32), ((12, 256), F32)], [moments],
    )(shifts, vel_in, code_in, occ, ids_in)
    ids = None
    for step in range(ITERS):
        first = step == 0
        from_odd, from_even = swap(odd, even, "gy")
        rows = 24 if first else 12
        middle = call(
            functools.partial(middle_kernel, first), f"middle{step}", 4 if first else 3,
            [((40 if first else 24, 256), F32), ((rows, 256), F32), ((rows, 256), F32)], [], smem=False,
        )
        sums, odd, even = middle(sums, from_odd, from_even, *((ids_in,) if first else ()))
        from_odd, from_even = swap(odd, even, "gx")
        body = functools.partial(step_kernel, step)
        args = [shifts, vel, code, sums, from_odd, from_even] + ([] if first else [ids])
        message = ((8, 256), F32)
        if step < ITERS - 1:
            shapes = [vel_shape] + ([((32, 256), F32)] if first else []) + [((24, 256), F32), message, message]
            vel, *rest = call(body, f"step{step}", len(args) - 1, shapes, [moments, means, axes])(*args)
            if first:
                ids, *rest = rest
            sums, odd, even = rest
        else:
            shapes = [((6, 256, 128), jnp.bfloat16), ((6, 256), F32)]
            scratch = [pltpu.VMEM((6, 128, 256), F32), means, axes]
            out, out_means = call(body, f"step{step}", len(args) - 1, shapes, scratch)(*args)
    return out.reshape(velocity.shape), out_means.reshape(3, *occupancy.shape)


def solution(mesh):
    in_specs = (
        P(None, "gx", "gy", None, None),
        P("gx", "gy", None, None),
        P("gx", "gy", None),
        P(),
        P(None, "gx", "gy", None),
    )
    out_specs = (P(None, "gx", "gy", None, None), P(None, "gx", "gy", None))
    return jax.shard_map(
        on_device, mesh=mesh, in_specs=in_specs, out_specs=out_specs, check_vma=False
    )
```

time: 156 us -> 99.4 us (0.64)
  the two profiles are of different devices: /device:TPU:89 before, /device:TPU:1 now
where the time goes in v1:
time: 99.4 us; the launch traced here: 98.7 us
  starting transfers between devices  64 us (64%)
  waiting for transfers between devices  17.1 us (17%)
  Pallas kernels  12.8 us (13%)
  local copies, waits for them, and re-layouts  3.95 us (4%)
    ppermute x8, starting transfers between devices, swap(): from_odd = lax.ppermute(odd, axis, odds)  37.3 us
    ppermute x8, starting transfers between devices, swap(): from_even = lax.ppermute(even, axis, evens)  26.7 us
    ppermute x8, waiting for transfers between devices, swap(): from_even = lax.ppermute(even, axis, evens)  9.78 us
    pallas_call x3, Pallas kernels, on_device(): call(body, f'step{step}', len(args) - 1, shapes, [moments, means, axes])  8.3 us
    ppermute x8, waiting for transfers between devices, swap(): from_odd = lax.ppermute(odd, axis, odds)  7.33 us
    unnamed x8, local copies, waits for them, and re-layouts  2.64 us
    pallas_call x1, Pallas kernels, on_device(): call(body, f'step{step}', len(args) - 1, shapes, scratch)(*args)  2.49 us
  transfers between devices with their start and end apart: 16, of which 10 were waited for; matrix products, arithmetic and copies ran while one was open for 0% of the time, Pallas kernels for 0%

profile of v1, /device:TPU:1, one launch (start us, length us, event | category | flops | bytes accessed | tf_op | source)
XLA Modules:
  0.0 98.7 jit_solution(3246921452136952298)
XLA Ops:
  0.6 0.7 reshape.25.ids_ref.refs_3_
  1.3 0.0 copy-start.3
  1.3 0.0 copy-start.2
  1.3 0.7 copy-done.3
  2.0 0.0 copy-done.2
  2.0 0.0 copy-start
  2.0 1.0 %copy-done = bf16[3,1,2,256,128]{4,3,2,1,0:T(8,128)(2,1)S(1)} copy-done((bf16[3,1,2,256,128]{4,3,2,1,0:T(8,128)(2,1)S(1)}, bf16[3,1,2,256,128]{4,3,2,1,0:T(8,128)(2,1)}, u32[]{:S(2)}) %copy-start) | copy-done | bytes 393240
  3.0 0.0 copy-start.1
  3.0 0.9 copy-done.1
  4.0 2.0 %start.1 = (f32[6,128,256]{2,1,0:T(8,128)S(1)}, s32[2,128,256]{2,1,0:T(8,128)S(1)}, f32[24,256]{1,0:T(8,128)S(1)}, f32[12,256]{1,0:T(8,128)S(1)}, f32[12,256]{1,0:T(8,128)S(1)}) custom-call(s32[4,3]{1,0:T(4,128)S(1)} %copy-done.2, bf16[6,256,128]{2,1,0:T(8,128)(2,1)S(1)} %bitcast.7, s32[2,256,128]{2,1,0:T(8,128)S(1)} %bitcast.8, s32[2,256]{1,0:T(2,128)S(1)} %bitcast.9, ...), custom_call_target="tpu_custom_call" | custom-call | tf_op jit(solution)/shard_map/start/pallas_call | solution.py:268
  5.9 5.4 %collective-permute-start = (f32[12,256]{1,0:T(8,128)S(1)}, f32[12,256]{1,0:T(8,128)S(1)}, u32[]{:S(2)}, u32[]{:S(2)}) collective-permute-start(f32[12,256]{1,0:T(8,128)S(1)} %get-tuple-element.37), channel_id=1, source_target_pairs={{0,31},{1,2},{2,1},{3,4},{4,3},{5,6},{6,5},{7,8},{8,7},{9,10},{10,... | collective-permute-start | bytes 36872 | tf_op jit(solution)/shard_map/ppermute | solution.py:254
  11.3 5.3 %collective-permute-start.1 = (f32[12,256]{1,0:T(8,128)S(1)}, f32[12,256]{1,0:T(8,128)S(1)}, u32[]{:S(2)}, u32[]{:S(2)}) collective-permute-start(f32[12,256]{1,0:T(8,128)S(1)} %get-tuple-element.38), channel_id=1, source_target_pairs={{0,1},{1,0},{2,3},{3,2},{4,5},{5,4},{6,7},{7,6},{8,9},{9,8},{10,11... | collective-permute-start | bytes 36872 | tf_op jit(solution)/shard_map/ppermute | solution.py:253
  16.7 0.0 collective-permute-done.refs_1_
  16.7 0.8 collective-permute-done.1.refs_2_
  17.5 11.3 %collective-permute-start.2 = (f32[24,256]{1,0:T(8,128)S(1)}, f32[24,256]{1,0:T(8,128)S(1)}, u32[]{:S(2)}, u32[]{:S(2)}) collective-permute-start(f32[24,256]{1,0:T(8,128)S(1)} %get-tuple-element.40), channel_id=1, source_target_pairs={{0,480},{32,64},{64,32},{96,128},{128,96},{160,192},{192,160},{224... | collective-permute-start | bytes 73736 | tf_op jit(solution)/shard_map/ppermute | solution.py:254
  28.8 1.9 %collective-permute-start.3 = (f32[24,256]{1,0:T(8,128)S(1)}, f32[24,256]{1,0:T(8,128)S(1)}, u32[]{:S(2)}, u32[]{:S(2)}) collective-permute-start(f32[24,256]{1,0:T(8,128)S(1)} %get-tuple-element.41), channel_id=1, source_target_pairs={{0,32},{32,0},{64,96},{96,64},{128,160},{160,128},{192,224},{224,1... | collective-permute-start | bytes 73736 | tf_op jit(solution)/shard_map/ppermute | solution.py:253
  30.7 0.0 collective-permute-done.2.refs_4_
  30.7 3.5 %collective-permute-done.3.refs_5_ = f32[24,256]{1,0:T(8,128)S(1)} collective-permute-done((f32[24,256]{1,0:T(8,128)S(1)}, f32[24,256]{1,0:T(8,128)S(1)}, u32[]{:S(2)}, u32[]{:S(2)}) %collective-permute-start.3) | collective-permute-done | bytes 24608 | tf_op jit(solution)/shard_map/ppermute | solution.py:253
  34.3 2.8 %step0.1 = (f32[6,128,256]{2,1,0:T(8,128)S(1)}, f32[32,256]{1,0:T(8,128)S(1)}, f32[24,256]{1,0:T(8,128)S(1)}, f32[8,256]{1,0:T(8,128)S(1)}, f32[8,256]{1,0:T(8,128)S(1)}) custom-call(s32[4,3]{1,0:T(4,128)S(1)} %copy-done.2, f32[6,128,256]{2,1,0:T(8,128)S(1)} %get-tuple-element.34.refs_1_, s32[2,128,256]{2,1,0:T(8,128)S(1)} %get-tuple-element.35.refs_2_, ...), custom_call_target="tpu_custom_call" | custom-call | tf_op jit(solution)/shard_map/step0/pallas_call | solution.py:288
  37.1 2.3 %collective-permute-start.4 = (f32[8,256]{1,0:T(8,128)S(1)}, f32[8,256]{1,0:T(8,128)S(1)}, u32[]{:S(2)}, u32[]{:S(2)}) collective-permute-start(f32[8,256]{1,0:T(8,128)S(1)} %get-tuple-element.44), channel_id=1, source_target_pairs={{0,31},{1,2},{2,1},{3,4},{4,3},{5,6},{6,5},{7,8},{8,7},{9,10},{10,... | collective-permute-start | bytes 24584 | tf_op jit(solution)/shard_map/ppermute | solution.py:254
  39.3 4.1 %collective-permute-start.5 = (f32[8,256]{1,0:T(8,128)S(1)}, f32[8,256]{1,0:T(8,128)S(1)}, u32[]{:S(2)}, u32[]{:S(2)}) collective-permute-start(f32[8,256]{1,0:T(8,128)S(1)} %get-tuple-element.45), channel_id=1, source_target_pairs={{0,1},{1,0},{2,3},{3,2},{4,5},{5,4},{6,7},{7,6},{8,9},{9,8},{10,11... | collective-permute-start | bytes 24584 | tf_op jit(solution)/shard_map/ppermute | solution.py:253
  43.4 0.0 collective-permute-done.4.refs_1_
  43.4 0.8 collective-permute-done.5.refs_2_
  44.3 3.3 %collective-permute-start.6 = (f32[12,256]{1,0:T(8,128)S(1)}, f32[12,256]{1,0:T(8,128)S(1)}, u32[]{:S(2)}, u32[]{:S(2)}) collective-permute-start(f32[12,256]{1,0:T(8,128)S(1)} %get-tuple-element.47), channel_id=1, source_target_pairs={{0,480},{32,64},{64,32},{96,128},{128,96},{160,192},{192,160},{224... | collective-permute-start | bytes 36872 | tf_op jit(solution)/shard_map/ppermute | solution.py:254
  47.6 1.9 %collective-permute-start.7 = (f32[12,256]{1,0:T(8,128)S(1)}, f32[12,256]{1,0:T(8,128)S(1)}, u32[]{:S(2)}, u32[]{:S(2)}) collective-permute-start(f32[12,256]{1,0:T(8,128)S(1)} %get-tuple-element.48), channel_id=1, source_target_pairs={{0,32},{32,0},{64,96},{96,64},{128,160},{160,128},{192,224},{224,1... | collective-permute-start | bytes 36872 | tf_op jit(solution)/shard_map/ppermute | solution.py:253
  49.5 3.5 %collective-permute-done.6.refs_4_ = f32[12,256]{1,0:T(8,128)S(1)} collective-permute-done((f32[12,256]{1,0:T(8,128)S(1)}, f32[12,256]{1,0:T(8,128)S(1)}, u32[]{:S(2)}, u32[]{:S(2)}) %collective-permute-start.6) | collective-permute-done | bytes 12320 | tf_op jit(solution)/shard_map/ppermute | solution.py:254
  53.0 0.0 collective-permute-done.7.refs_5_
  53.0 2.8 %step1.1 = (f32[6,128,256]{2,1,0:T(8,128)S(1)}, f32[24,256]{1,0:T(8,128)S(1)}, f32[8,256]{1,0:T(8,128)S(1)}, f32[8,256]{1,0:T(8,128)S(1)}) custom-call(s32[4,3]{1,0:T(4,128)S(1)} %copy-done.2, f32[6,128,256]{2,1,0:T(8,128)S(1)} %get-tuple-element.42.refs_1_, s32[2,128,256]{2,1,0:T(8,128)S(1)} %get-tuple-element.35.refs_2_, ...), custom_call_target="tpu_custom_call" | custom-call | tf_op jit(solution)/shard_map/step1/pallas_call | solution.py:288
  55.7 2.9 %collective-permute-start.8 = (f32[8,256]{1,0:T(8,128)S(1)}, f32[8,256]{1,0:T(8,128)S(1)}, u32[]{:S(2)}, u32[]{:S(2)}) collective-permute-start(f32[8,256]{1,0:T(8,128)S(1)} %get-tuple-element.52), channel_id=1, source_target_pairs={{0,31},{1,2},{2,1},{3,4},{4,3},{5,6},{6,5},{7,8},{8,7},{9,10},{10,... | collective-permute-start | bytes 24584 | tf_op jit(solution)/shard_map/ppermute | solution.py:254
  58.7 4.3 %collective-permute-start.9 = (f32[8,256]{1,0:T(8,128)S(1)}, f32[8,256]{1,0:T(8,128)S(1)}, u32[]{:S(2)}, u32[]{:S(2)}) collective-permute-start(f32[8,256]{1,0:T(8,128)S(1)} %get-tuple-element.53), channel_id=1, source_target_pairs={{0,1},{1,0},{2,3},{3,2},{4,5},{5,4},{6,7},{7,6},{8,9},{9,8},{10,11... | collective-permute-start | bytes 24584 | tf_op jit(solution)/shard_map/ppermute | solution.py:253
  63.0 0.0 collective-permute-done.8.refs_1_
  63.0 0.8 collective-permute-done.9.refs_2_
  63.8 6.2 %collective-permute-start.10 = (f32[12,256]{1,0:T(8,128)S(1)}, f32[12,256]{1,0:T(8,128)S(1)}, u32[]{:S(2)}, u32[]{:S(2)}) collective-permute-start(f32[12,256]{1,0:T(8,128)S(1)} %get-tuple-element.55), channel_id=1, source_target_pairs={{0,480},{32,64},{64,32},{96,128},{128,96},{160,192},{192,160},{224... | collective-permute-start | bytes 36872 | tf_op jit(solution)/shard_map/ppermute | solution.py:254
  70.0 1.9 %collective-permute-start.11 = (f32[12,256]{1,0:T(8,128)S(1)}, f32[12,256]{1,0:T(8,128)S(1)}, u32[]{:S(2)}, u32[]{:S(2)}) collective-permute-start(f32[12,256]{1,0:T(8,128)S(1)} %get-tuple-element.56), channel_id=1, source_target_pairs={{0,32},{32,0},{64,96},{96,64},{128,160},{160,128},{192,224},{224,1... | collective-permute-start | bytes 36872 | tf_op jit(solution)/shard_map/ppermute | solution.py:253
  71.9 0.6 collective-permute-done.10.refs_4_
  72.5 2.9 %collective-permute-done.11.refs_5_ = f32[12,256]{1,0:T(8,128)S(1)} collective-permute-done((f32[12,256]{1,0:T(8,128)S(1)}, f32[12,256]{1,0:T(8,128)S(1)}, u32[]{:S(2)}, u32[]{:S(2)}) %collective-permute-start.11) | collective-permute-done | bytes 12320 | tf_op jit(solution)/shard_map/ppermute | solution.py:253
  75.4 2.8 %step2.1 = (f32[6,128,256]{2,1,0:T(8,128)S(1)}, f32[24,256]{1,0:T(8,128)S(1)}, f32[8,256]{1,0:T(8,128)S(1)}, f32[8,256]{1,0:T(8,128)S(1)}) custom-call(s32[4,3]{1,0:T(4,128)S(1)} %copy-done.2, f32[6,128,256]{2,1,0:T(8,128)S(1)} %get-tuple-element.50.refs_1_, s32[2,128,256]{2,1,0:T(8,128)S(1)} %get-tuple-element.35.refs_2_, ...), custom_call_target="tpu_custom_call" | custom-call | tf_op jit(solution)/shard_map/step2/pallas_call | solution.py:288
  78.2 2.4 %collective-permute-start.12 = (f32[8,256]{1,0:T(8,128)S(1)}, f32[8,256]{1,0:T(8,128)S(1)}, u32[]{:S(2)}, u32[]{:S(2)}) collective-permute-start(f32[8,256]{1,0:T(8,128)S(1)} %get-tuple-element.59), channel_id=1, source_target_pairs={{0,31},{1,2},{2,1},{3,4},{4,3},{5,6},{6,5},{7,8},{8,7},{9,10},{10,... | collective-permute-start | bytes 24584 | tf_op jit(solution)/shard_map/ppermute | solution.py:254
  80.6 5.3 %collective-permute-start.13 = (f32[8,256]{1,0:T(8,128)S(1)}, f32[8,256]{1,0:T(8,128)S(1)}, u32[]{:S(2)}, u32[]{:S(2)}) collective-permute-start(f32[8,256]{1,0:T(8,128)S(1)} %get-tuple-element.60), channel_id=1, source_target_pairs={{0,1},{1,0},{2,3},{3,2},{4,5},{5,4},{6,7},{7,6},{8,9},{9,8},{10,11... | collective-permute-start | bytes 24584 | tf_op jit(solution)/shard_map/ppermute | solution.py:253
  85.9 0.0 collective-permute-done.12.refs_1_
  85.9 0.8 collective-permute-done.13.refs_2_
  86.7 3.5 %collective-permute-start.14 = (f32[12,256]{1,0:T(8,128)S(1)}, f32[12,256]{1,0:T(8,128)S(1)}, u32[]{:S(2)}, u32[]{:S(2)}) collective-permute-start(f32[12,256]{1,0:T(8,128)S(1)} %get-tuple-element.62), channel_id=1, source_target_pairs={{0,480},{32,64},{64,32},{96,128},{128,96},{160,192},{192,160},{224... | collective-permute-start | bytes 36872 | tf_op jit(solution)/shard_map/ppermute | solution.py:254
  90.2 1.9 %collective-permute-start.15 = (f32[12,256]{1,0:T(8,128)S(1)}, f32[12,256]{1,0:T(8,128)S(1)}, u32[]{:S(2)}, u32[]{:S(2)}) collective-permute-start(f32[12,256]{1,0:T(8,128)S(1)} %get-tuple-element.63), channel_id=1, source_target_pairs={{0,32},{32,0},{64,96},{96,64},{128,160},{160,128},{192,224},{224,1... | collective-permute-start | bytes 36872 | tf_op jit(solution)/shard_map/ppermute | solution.py:253
  92.1 3.3 %collective-permute-done.14.refs_4_ = f32[12,256]{1,0:T(8,128)S(1)} collective-permute-done((f32[12,256]{1,0:T(8,128)S(1)}, f32[12,256]{1,0:T(8,128)S(1)}, u32[]{:S(2)}, u32[]{:S(2)}) %collective-permute-start.14) | collective-permute-done | bytes 12320 | tf_op jit(solution)/shard_map/ppermute | solution.py:254
  95.4 0.2 collective-permute-done.15.refs_5_
  95.6 2.5 %step3.1 = (bf16[6,256,128]{2,1,0:T(8,128)(2,1)}, f32[6,256]{1,0:T(8,128)S(1)}) custom-call(s32[4,3]{1,0:T(4,128)S(1)} %copy-done.2, f32[6,128,256]{2,1,0:T(8,128)S(1)} %get-tuple-element.57.refs_1_, s32[2,128,256]{2,1,0:T(8,128)S(1)} %get-tuple-element.35.refs_2_, f32[24,256]{1,0:T(8,128)S(1)} %get-tuple-element.61.refs_3_, ...), custom_call_target="tpu_custom_call" | custom-call | tf_op jit(solution)/shard_map/step3/pallas_call | solution.py:295
  98.1 0.6 reshape.27
  (4 shorter events, 0.1 us)
Async XLA Ops:
  1.3 0.7 copy-start.3
  1.3 0.7 copy-start.2
  2.0 1.0 %copy-start = (bf16[3,1,2,256,128]{4,3,2,1,0:T(8,128)(2,1)S(1)}, bf16[3,1,2,256,128]{4,3,2,1,0:T(8,128)(2,1)}, u32[]{:S(2)}) copy-start(bf16[3,1,2,256,128]{4,3,2,1,0:T(8,128)(2,1)} %param.5) | copy-start | bytes 1179652
  3.0 0.9 copy-start.1
  5.9 10.7 %collective-permute-start = (f32[12,256]{1,0:T(8,128)S(1)}, f32[12,256]{1,0:T(8,128)S(1)}, u32[]{:S(2)}, u32[]{:S(2)}) collective-permute-start(f32[12,256]{1,0:T(8,128)S(1)} %get-tuple-element.37), channel_id=1, source_target_pairs={{0,31},{1,2},{2,1},{3,4},{4,3},{5,6},{6,5},{7,8},{8,7},{9,10},{10,... | collective-permute-start | bytes 36872 | tf_op jit(solution)/shard_map/ppermute | solution.py:254
  11.3 6.1 %collective-permute-start.1 = (f32[12,256]{1,0:T(8,128)S(1)}, f32[12,256]{1,0:T(8,128)S(1)}, u32[]{:S(2)}, u32[]{:S(2)}) collective-permute-start(f32[12,256]{1,0:T(8,128)S(1)} %get-tuple-element.38), channel_id=1, source_target_pairs={{0,1},{1,0},{2,3},{3,2},{4,5},{5,4},{6,7},{7,6},{8,9},{9,8},{10,11... | collective-permute-start | bytes 36872 | tf_op jit(solution)/shard_map/ppermute | solution.py:253
  17.5 13.2 %collective-permute-start.2 = (f32[24,256]{1,0:T(8,128)S(1)}, f32[24,256]{1,0:T(8,128)S(1)}, u32[]{:S(2)}, u32[]{:S(2)}) collective-permute-start(f32[24,256]{1,0:T(8,128)S(1)} %get-tuple-element.40), channel_id=1, source_target_pairs={{0,480},{32,64},{64,32},{96,128},{128,96},{160,192},{192,160},{224... | collective-permute-start | bytes 73736 | tf_op jit(solution)/shard_map/ppermute | solution.py:254
  28.8 5.5 %collective-permute-start.3 = (f32[24,256]{1,0:T(8,128)S(1)}, f32[24,256]{1,0:T(8,128)S(1)}, u32[]{:S(2)}, u32[]{:S(2)}) collective-permute-start(f32[24,256]{1,0:T(8,128)S(1)} %get-tuple-element.41), channel_id=1, source_target_pairs={{0,32},{32,0},{64,96},{96,64},{128,160},{160,128},{192,224},{224,1... | collective-permute-start | bytes 73736 | tf_op jit(solution)/shard_map/ppermute | solution.py:253
  37.1 6.4 %collective-permute-start.4 = (f32[8,256]{1,0:T(8,128)S(1)}, f32[8,256]{1,0:T(8,128)S(1)}, u32[]{:S(2)}, u32[]{:S(2)}) collective-permute-start(f32[8,256]{1,0:T(8,128)S(1)} %get-tuple-element.44), channel_id=1, source_target_pairs={{0,31},{1,2},{2,1},{3,4},{4,3},{5,6},{6,5},{7,8},{8,7},{9,10},{10,... | collective-permute-start | bytes 24584 | tf_op jit(solution)/shard_map/ppermute | solution.py:254
  39.3 4.9 %collective-permute-start.5 = (f32[8,256]{1,0:T(8,128)S(1)}, f32[8,256]{1,0:T(8,128)S(1)}, u32[]{:S(2)}, u32[]{:S(2)}) collective-permute-start(f32[8,256]{1,0:T(8,128)S(1)} %get-tuple-element.45), channel_id=1, source_target_pairs={{0,1},{1,0},{2,3},{3,2},{4,5},{5,4},{6,7},{7,6},{8,9},{9,8},{10,11... | collective-permute-start | bytes 24584 | tf_op jit(solution)/shard_map/ppermute | solution.py:253
  44.3 8.7 %collective-permute-start.6 = (f32[12,256]{1,0:T(8,128)S(1)}, f32[12,256]{1,0:T(8,128)S(1)}, u32[]{:S(2)}, u32[]{:S(2)}) collective-permute-start(f32[12,256]{1,0:T(8,128)S(1)} %get-tuple-element.47), channel_id=1, source_target_pairs={{0,480},{32,64},{64,32},{96,128},{128,96},{160,192},{192,160},{224... | collective-permute-start | bytes 36872 | tf_op jit(solution)/shard_map/ppermute | solution.py:254
  47.6 5.4 %collective-permute-start.7 = (f32[12,256]{1,0:T(8,128)S(1)}, f32[12,256]{1,0:T(8,128)S(1)}, u32[]{:S(2)}, u32[]{:S(2)}) collective-permute-start(f32[12,256]{1,0:T(8,128)S(1)} %get-tuple-element.48), channel_id=1, source_target_pairs={{0,32},{32,0},{64,96},{96,64},{128,160},{160,128},{192,224},{224,1... | collective-permute-start | bytes 36872 | tf_op jit(solution)/shard_map/ppermute | solution.py:253
  55.7 7.3 %collective-permute-start.8 = (f32[8,256]{1,0:T(8,128)S(1)}, f32[8,256]{1,0:T(8,128)S(1)}, u32[]{:S(2)}, u32[]{:S(2)}) collective-permute-start(f32[8,256]{1,0:T(8,128)S(1)} %get-tuple-element.52), channel_id=1, source_target_pairs={{0,31},{1,2},{2,1},{3,4},{4,3},{5,6},{6,5},{7,8},{8,7},{9,10},{10,... | collective-permute-start | bytes 24584 | tf_op jit(solution)/shard_map/ppermute | solution.py:254
  58.7 5.2 %collective-permute-start.9 = (f32[8,256]{1,0:T(8,128)S(1)}, f32[8,256]{1,0:T(8,128)S(1)}, u32[]{:S(2)}, u32[]{:S(2)}) collective-permute-start(f32[8,256]{1,0:T(8,128)S(1)} %get-tuple-element.53), channel_id=1, source_target_pairs={{0,1},{1,0},{2,3},{3,2},{4,5},{5,4},{6,7},{7,6},{8,9},{9,8},{10,11... | collective-permute-start | bytes 24584 | tf_op jit(solution)/shard_map/ppermute | solution.py:253
  63.8 8.7 %collective-permute-start.10 = (f32[12,256]{1,0:T(8,128)S(1)}, f32[12,256]{1,0:T(8,128)S(1)}, u32[]{:S(2)}, u32[]{:S(2)}) collective-permute-start(f32[12,256]{1,0:T(8,128)S(1)} %get-tuple-element.55), channel_id=1, source_target_pairs={{0,480},{32,64},{64,32},{96,128},{128,96},{160,192},{192,160},{224... | collective-permute-start | bytes 36872 | tf_op jit(solution)/shard_map/ppermute | solution.py:254
  70.0 5.4 %collective-permute-start.11 = (f32[12,256]{1,0:T(8,128)S(1)}, f32[12,256]{1,0:T(8,128)S(1)}, u32[]{:S(2)}, u32[]{:S(2)}) collective-permute-start(f32[12,256]{1,0:T(8,128)S(1)} %get-tuple-element.56), channel_id=1, source_target_pairs={{0,32},{32,0},{64,96},{96,64},{128,160},{160,128},{192,224},{224,1... | collective-permute-start | bytes 36872 | tf_op jit(solution)/shard_map/ppermute | solution.py:253
  78.2 7.7 %collective-permute-start.12 = (f32[8,256]{1,0:T(8,128)S(1)}, f32[8,256]{1,0:T(8,128)S(1)}, u32[]{:S(2)}, u32[]{:S(2)}) collective-permute-start(f32[8,256]{1,0:T(8,128)S(1)} %get-tuple-element.59), channel_id=1, source_target_pairs={{0,31},{1,2},{2,1},{3,4},{4,3},{5,6},{6,5},{7,8},{8,7},{9,10},{10,... | collective-permute-start | bytes 24584 | tf_op jit(solution)/shard_map/ppermute | solution.py:254
  80.6 6.1 %collective-permute-start.13 = (f32[8,256]{1,0:T(8,128)S(1)}, f32[8,256]{1,0:T(8,128)S(1)}, u32[]{:S(2)}, u32[]{:S(2)}) collective-permute-start(f32[8,256]{1,0:T(8,128)S(1)} %get-tuple-element.60), channel_id=1, source_target_pairs={{0,1},{1,0},{2,3},{3,2},{4,5},{5,4},{6,7},{7,6},{8,9},{9,8},{10,11... | collective-permute-start | bytes 24584 | tf_op jit(solution)/shard_map/ppermute | solution.py:253
  86.7 8.7 %collective-permute-start.14 = (f32[12,256]{1,0:T(8,128)S(1)}, f32[12,256]{1,0:T(8,128)S(1)}, u32[]{:S(2)}, u32[]{:S(2)}) collective-permute-start(f32[12,256]{1,0:T(8,128)S(1)} %get-tuple-element.62), channel_id=1, source_target_pairs={{0,480},{32,64},{64,32},{96,128},{128,96},{160,192},{192,160},{224... | collective-permute-start | bytes 36872 | tf_op jit(solution)/shard_map/ppermute | solution.py:254
  90.2 5.4 %collective-permute-start.15 = (f32[12,256]{1,0:T(8,128)S(1)}, f32[12,256]{1,0:T(8,128)S(1)}, u32[]{:S(2)}, u32[]{:S(2)}) collective-permute-start(f32[12,256]{1,0:T(8,128)S(1)} %get-tuple-element.63), channel_id=1, source_target_pairs={{0,32},{32,0},{64,96},{96,64},{128,160},{160,128},{192,224},{224,1... | collective-permute-start | bytes 36872 | tf_op jit(solution)/shard_map/ppermute | solution.py:253

commit v2 on v1

v2 whole, which is shorter than its diff:
```python
import functools
import math

import jax
import jax.numpy as jnp
import numpy as np
from jax import lax
from jax.experimental import pallas as pl
from jax.experimental.pallas import tpu as pltpu
from jax.sharding import PartitionSpec as P

SUBDIV = 8
NAXES = 32
ITERS = 4
GOLDEN = 2.399963229728653
TURN_COS = math.cos(130.0 * math.pi / 180.0)
TURN_SIN = math.sin(130.0 * math.pi / 180.0)
ALONG = (1.0 - TURN_COS) / (TURN_SIN * TURN_SIN)

F32 = jnp.float32
CHUNK = 32
WIDE = 48


def axis_table():
    ordinal = np.arange(NAXES, dtype=np.float64)
    height = 1.0 - (2.0 * ordinal + 1.0) / NAXES
    radius = np.sqrt(1.0 - height * height)
    phases = ordinal * GOLDEN
    return TURN_SIN * np.stack([radius * np.cos(phases), radius * np.sin(phases), height])


AXES = axis_table()


def is_odd(axis):
    return lax.rem(lax.axis_index(axis), 2) == 1


def hop_masks(code, shifts_ref, step):
    hop_x = code >= (SUBDIV - shifts_ref[step, 0]) * (SUBDIV * SUBDIV)
    hop_y = (code & (SUBDIV * SUBDIV - 1)) >= (SUBDIV - shifts_ref[step, 1]) * SUBDIV
    hop_z = (code & (SUBDIV - 1)) >= SUBDIV - shifts_ref[step, 2]
    return hop_x, hop_y, hop_z


def slot_sums(values, count, col, lanes, code_ref, shifts_ref, step, mom_ref):
    def body(i, acc):
        rows = pl.ds(pl.multiple_of(i * 8, 8), 8)
        code = code_ref[col, rows, lanes]
        hop_x, hop_y, hop_z = hop_masks(code, shifts_ref, step)
        out = list(acc)
        for comp, value in enumerate(values(rows, code)):
            with_x = jnp.where(hop_x, value, 0.0)
            with_y = jnp.where(hop_y, value, 0.0)
            with_xy = jnp.where(hop_y, with_x, 0.0)
            for pair, base in ((0, value), (2, with_y), (4, with_x), (6, with_xy)):
                at = comp * 8 + pair
                out[at] = out[at] + base
                out[at + 1] = out[at + 1] + jnp.where(hop_z, base, 0.0)
        return tuple(out)

    zero = jnp.zeros((8, 128), F32)
    acc = lax.fori_loop(0, 16, body, (zero,) * (8 * count), unroll=2)
    for comp in range(count):
        for moment in range(8):
            row = (col * 8 + moment) * 8 + comp
            mom_ref[row : row + 1, lanes] = jnp.sum(acc[comp * 8 + moment], axis=0, keepdims=True)


def blocks():
    for col in range(2):
        for half in range(2):
            yield col, slice(half * 128, half * 128 + 128)


def deposit(vel_ref, code_ref, shifts_ref, step, mom_ref, counted):
    for col, lanes in blocks():

        def values(rows, code):
            parts = [vel_ref[comp * 2 + col, rows, lanes] for comp in range(3)]
            return parts + ([jnp.where(code >= 0, 1.0, 0.0)] if counted else [])

        slot_sums(values, 4 if counted else 3, col, lanes, code_ref, shifts_ref, step, mom_ref)


def cell_sums(moment_of, sums_ref):
    pieces = {}
    for col in range(2):
        quads = {}
        for moment in (0, 2, 4, 6):
            up = moment_of(col, moment + 1)
            quads[moment] = moment_of(col, moment) - up + pltpu.roll(up, 1, 1)
        pieces[col, 1, 1] = quads[6]
        pieces[col, 1, 0] = quads[4] - quads[6]
        pieces[col, 0, 1] = quads[2] - quads[6]
        pieces[col, 0, 0] = quads[0] - quads[2] - quads[4] + quads[6]
    for hop in range(2):
        columns = (pieces[0, hop, 0], pieces[0, hop, 1] + pieces[1, hop, 0], pieces[1, hop, 1])
        for at, piece in enumerate(columns):
            row = (hop * 3 + at) * 4
            sums_ref[row : row + 4, :] = piece[0:4, :]


def stored_moment(mom_ref):
    def moment_of(col, moment):
        row = (col * 8 + moment) * 8
        return mom_ref[row : row + 8, :]

    return moment_of


def fill_messages_y(sums_ref, odd_ref, even_ref):
    odd = is_odd("gy")
    for hop in range(2):
        left = sums_ref[hop * 12 : hop * 12 + 4, :]
        right = sums_ref[hop * 12 + 8 : hop * 12 + 12, :]
        odd_ref[hop * 4 : hop * 4 + 4, :] = jnp.where(odd, right, left)
        even_ref[hop * 4 : hop * 4 + 4, :] = jnp.where(odd, left, right)


def start_kernel(shifts_hbm, vel_hbm, code_hbm, occ_hbm, ids_hbm, vel_ref, code_ref, sums_ref, odd_ref, even_ref, mom_ref, vel_in_ref, code_in_ref, occ_ref, ids_ref, shifts_ref, sems):
    fetch_shifts = pltpu.make_async_copy(shifts_hbm, shifts_ref, sems.at[10])
    fetch_occ = pltpu.make_async_copy(occ_hbm, occ_ref, sems.at[8])
    fetch_ids = pltpu.make_async_copy(ids_hbm, ids_ref, sems.at[9])
    copies = []
    for col in range(2):
        copies.append(pltpu.make_async_copy(code_hbm.at[col], code_in_ref.at[col], sems.at[col]))
    for at in range(6):
        copies.append(pltpu.make_async_copy(vel_hbm.at[at], vel_in_ref.at[at], sems.at[2 + at]))
    fetch_occ.start()
    for copy in copies:
        copy.start()
    fetch_ids.start()
    fetch_shifts.start()
    mom_ref[...] = jnp.zeros_like(mom_ref)
    slot = lax.broadcasted_iota(jnp.int32, (128, 256), 0)
    fetch_occ.wait()
    for col in range(2):
        filled = slot < occ_ref[col : col + 1, :]
        copies[col].wait()
        code_ref[col] = jnp.where(filled, code_in_ref[col].T, -1)
    for comp in range(3):
        for col in range(2):
            at = comp * 2 + col
            copies[2 + at].wait()
            filled = code_ref[col] >= 0
            vel_ref[at] = jnp.where(filled, vel_in_ref[at].astype(F32).T, 0.0)
    fetch_ids.wait()
    fetch_shifts.wait()
    for step in range(ITERS):
        ids = ids_ref[step, 0:1, :].astype(F32)
        odd_ref[8 + step : 9 + step, :] = ids
        even_ref[8 + step : 9 + step, :] = ids
    deposit(vel_ref, code_ref, shifts_ref, 0, mom_ref, True)
    cell_sums(stored_moment(mom_ref), sums_ref)
    fill_messages_y(sums_ref, odd_ref, even_ref)


def middle_kernel(first, *refs):
    if first:
        sums_ref, from_odd_ref, from_even_ref, ids_ref, out_ref, odd_ref, even_ref = refs
    else:
        sums_ref, from_odd_ref, from_even_ref, out_ref, odd_ref, even_ref = refs
    odd_y, odd_x = is_odd("gy"), is_odd("gx")
    out_ref[0:24, :] = sums_ref[...]
    for hop in range(2):
        rows = slice(hop * 4, hop * 4 + 4)
        by_odd, by_even = from_odd_ref[rows, :], from_even_ref[rows, :]
        left = slice(hop * 12, hop * 12 + 4)
        right = slice(hop * 12 + 8, hop * 12 + 12)
        out_ref[left, :] = out_ref[left, :] + jnp.where(odd_y, by_even, by_odd)
        out_ref[right, :] = out_ref[right, :] + jnp.where(odd_y, by_odd, by_even)
    low, high = out_ref[0:12, :], out_ref[12:24, :]
    odd_ref[0:12, :] = jnp.where(odd_x, high, low)
    even_ref[0:12, :] = jnp.where(odd_x, low, high)
    if first:
        for step in range(ITERS):
            row = 24 + step * 3
            out_ref[row : row + 2, :] = ids_ref[step].astype(F32)
            by_odd, by_even = from_odd_ref[8 + step : 9 + step, :], from_even_ref[8 + step : 9 + step, :]
            out_ref[row + 2 : row + 3, :] = jnp.where(odd_y, by_odd, by_even)
        own = out_ref[24:36, :]
        odd_ref[12:24, :] = own
        even_ref[12:24, :] = own


def cell_means(sums_ref, from_odd_ref, from_even_ref, work_ref, tot_ref):
    odd_x = is_odd("gx")
    by_odd, by_even = from_odd_ref[0:12, :], from_even_ref[0:12, :]
    work_ref[0:12, :] = sums_ref[0:12, :] + jnp.where(odd_x, by_even, by_odd)
    work_ref[12:24, :] = sums_ref[12:24, :] + jnp.where(odd_x, by_odd, by_even)
    tot_ref[...] = jnp.zeros_like(tot_ref)
    for cell in range(6):
        for comp in range(4):
            tot_ref[comp, cell : cell + 1, :] = work_ref[cell * 4 + comp : cell * 4 + comp + 1, :]
    count = jnp.maximum(tot_ref[3], 1.0)
    return [tot_ref[comp] / count for comp in range(3)]


def cell_axes(ids):
    axes = [jnp.zeros((8, 256), F32) for _ in range(3)]
    for k in range(NAXES):
        match = ids == float(k)
        axes = [jnp.where(match, float(AXES[comp, k]), axes[comp]) for comp in range(3)]
    return axes


def turned(axis, vec):
    along = (axis[0] * vec[0] + axis[1] * vec[1] + axis[2] * vec[2]) * ALONG
    out = []
    for comp in range(3):
        b, c = (comp + 1) % 3, (comp + 2) % 3
        out.append(TURN_COS * vec[comp] + (axis[b] * vec[c] - axis[c] * vec[b]) + along * axis[comp])
    return out


def next_z(value):
    return pltpu.roll(value, 255, 1)


def store_cells(table_ref, parts):
    for cell in range(6):
        for comp, part in enumerate(parts):
            table_ref[0, cell * 8 + comp : cell * 8 + comp + 1, :] = part[cell : cell + 1, :]
    table_ref[1] = next_z(table_ref[0])


def pick(table_ref, comp, col, lanes, masks):
    hop_x, hop_y, hop_z = masks
    by_x = []
    for step_x in range(2):
        by_y = []
        for step_y in range(2):
            row = (step_x * 3 + col + step_y) * 8 + comp
            by_y.append(jnp.where(hop_z, table_ref[1, row : row + 1, lanes], table_ref[0, row : row + 1, lanes]))
        by_x.append(jnp.where(hop_y, by_y[1], by_y[0]))
    return jnp.where(hop_x, by_x[1], by_x[0])


def over_slots(body):
    def run(i, carry):
        body(pl.ds(pl.multiple_of(i * CHUNK, CHUNK), CHUNK))
        return carry

    lax.fori_loop(0, 128 // CHUNK, run, 0)


def first_kernel(shifts_ref, vel_ref, code_ref, sums_ref, from_odd_ref, from_even_ref, joint_ref, out_ref, ids_ref, new_ref, odd_ref, even_ref, mom_ref, work_ref, tot_ref, table_ref):
    odd_x = is_odd("gx")
    ids_ref[...] = jnp.zeros_like(ids_ref)
    for t in range(ITERS):
        ids_ref[t * 8 : t * 8 + 3, :] = sums_ref[24 + t * 3 : 27 + t * 3, :]
        rows = slice(12 + t * 3, 15 + t * 3)
        ids_ref[t * 8 + 3 : t * 8 + 6, :] = jnp.where(odd_x, from_odd_ref[rows, :], from_even_ref[rows, :])
    means = cell_means(sums_ref, from_odd_ref, from_even_ref, work_ref, tot_ref)
    axes = cell_axes(ids_ref[0:8, :])
    turn = turned(axes, means)
    table_ref[...] = jnp.zeros_like(table_ref)
    store_cells(table_ref, axes + [means[comp] - turn[comp] for comp in range(3)])
    for col, lanes in blocks():

        def body(rows):
            code = code_ref[col, rows, lanes]
            masks = hop_masks(code, shifts_ref, 0)
            vel = [vel_ref[comp * 2 + col, rows, lanes] for comp in range(3)]
            turn = turned([pick(table_ref, comp, col, lanes, masks) for comp in range(3)], vel)
            filled = code >= 0
            for comp in range(3):
                value = turn[comp] + pick(table_ref, 3 + comp, col, lanes, masks)
                out_ref[comp * 2 + col, rows, lanes] = jnp.where(filled, value, 0.0)

        over_slots(body)
    mom_ref[...] = jnp.zeros_like(mom_ref)
    deposit(out_ref, code_ref, shifts_ref, 1, mom_ref, True)
    cell_sums(stored_moment(mom_ref), new_ref)
    fill_messages_y(new_ref, odd_ref, even_ref)


def joint_kernel(shifts_ref, code_ref, *out_refs):
    for t, out_ref in zip((1, 2), out_refs):
        out_ref[...] = jnp.zeros_like(out_ref)
        for col, lanes in blocks():

            def body(i, acc):
                rows = pl.ds(pl.multiple_of(i * 8, 8), 8)
                code = code_ref[col, rows, lanes]
                now, later = hop_masks(code, shifts_ref, t), hop_masks(code, shifts_ref, t + 1)
                out, at = list(acc), 0
                one = jnp.where(code >= 0, 1.0, 0.0)
                for by_x in (one, jnp.where(now[0], one, 0.0), jnp.where(later[0], one, 0.0)):
                    for by_y in (by_x, jnp.where(now[1], by_x, 0.0), jnp.where(later[1], by_x, 0.0)):
                        for by_z in (by_y, jnp.where(now[2], by_y, 0.0), jnp.where(later[2], by_y, 0.0)):
                            out[at] = out[at] + by_z
                            at += 1
                return tuple(out)

            acc = lax.fori_loop(0, 16, body, (jnp.zeros((8, 128), F32),) * 27, unroll=2)
            for at in range(27):
                out_ref[col * 27 + at : col * 27 + at + 1, lanes] = jnp.sum(acc[at], axis=0, keepdims=True)


def turn_kernel(step, *refs):
    sums = step < ITERS - 1
    if step == 1:
        shifts_ref, code_ref, ids_ref, vel_ref, *refs = refs
    else:
        shifts_ref, code_ref, ids_ref, vel_ref, last_ref, *refs = refs
    if sums:
        out_ref, axes_ref, mom_ref, table_ref = refs
    else:
        out_ref, axes_ref, table_ref = refs
    axes = cell_axes(ids_ref[step * 8 : step * 8 + 8, :])
    for comp in range(3):
        axes_ref[comp] = axes[comp]
    table_ref[...] = jnp.zeros_like(table_ref)
    store_cells(table_ref, axes)
    for col, lanes in blocks():

        def body(rows):
            code = code_ref[col, rows, lanes]
            vel = [vel_ref[comp * 2 + col, rows, lanes] for comp in range(3)]
            if step > 1:
                masks = hop_masks(code, shifts_ref, step - 1)
                filled = code >= 0
                vel = [jnp.where(filled, vel[comp] + pick(last_ref, comp, col, lanes, masks), 0.0) for comp in range(3)]
            masks = hop_masks(code, shifts_ref, step)
            turn = turned([pick(table_ref, comp, col, lanes, masks) for comp in range(3)], vel)
            for comp in range(3):
                out_ref[comp * 2 + col, rows, lanes] = turn[comp]

        over_slots(body)
    if sums:
        mom_ref[...] = jnp.zeros_like(mom_ref)
        deposit(out_ref, code_ref, shifts_ref, step + 1, mom_ref, False)


def shift_kernel(step, shifts_ref, sums_ref, from_odd_ref, from_even_ref, axes_ref, mom_ref, joint_ref, shift_ref, new_ref, odd_ref, even_ref, work_ref, tot_ref, next_ref):
    means = cell_means(sums_ref, from_odd_ref, from_even_ref, work_ref, tot_ref)
    turn = turned([axes_ref[comp] for comp in range(3)], means)
    shift_ref[...] = jnp.zeros_like(shift_ref)
    ones = jnp.ones((8, 256), F32)
    store_cells(shift_ref, [means[comp] - turn[comp] for comp in range(3)] + [ones])
    nested = []
    for dim in range(3):
        nested.append(jnp.where(shifts_ref[step, dim] <= shifts_ref[step + 1, dim], 1, 2))
    for col in range(2):
        parts = {}
        for corner in range(8):
            cell = (corner >> 2) * 3 + col + (corner >> 1 & 1)
            parts[corner] = shift_ref[corner & 1, cell * 8 : cell * 8 + 8, :]
        for bit in (1, 2, 4):
            for corner in range(8):
                if corner & bit:
                    parts[corner] = parts[corner] - parts[corner ^ bit]
        for later in range(8):
            row = (col * 8 + later) * 8
            total = mom_ref[row : row + 8, :]
            for now in range(8):
                at = col * 27
                for dim, (bit, weight) in enumerate(((4, 9), (2, 3), (1, 1))):
                    if now & bit and later & bit:
                        at = at + nested[dim] * weight
                    elif now & bit:
                        at = at + weight
                    elif later & bit:
                        at = at + 2 * weight
                total = total + joint_ref[pl.ds(at, 1), :] * parts[now]
            next_ref[row : row + 8, :] = total
    cell_sums(stored_moment(next_ref), new_ref)
    fill_messages_y(new_ref, odd_ref, even_ref)


def last_kernel(shifts_ref, code_ref, vel_ref, sums_ref, from_odd_ref, from_even_ref, axes_ref, out_ref, means_ref, work_ref, tot_ref, table_ref, end_ref):
    means = cell_means(sums_ref, from_odd_ref, from_even_ref, work_ref, tot_ref)
    turn = turned([axes_ref[comp] for comp in range(3)], means)
    table_ref[...] = jnp.zeros_like(table_ref)
    store_cells(table_ref, [means[comp] - turn[comp] for comp in range(3)])
    for comp in range(3):
        means_ref[comp] = means[comp][0:2, :]
    for col, lanes in blocks():

        def body(rows):
            code = code_ref[col, rows, lanes]
            masks = hop_masks(code, shifts_ref, ITERS - 1)
            filled = code >= 0
            for comp in range(3):
                value = vel_ref[comp * 2 + col, rows, lanes] + pick(table_ref, comp, col, lanes, masks)
                end_ref[comp * 2 + col, rows, lanes] = jnp.where(filled, value, 0.0)

        over_slots(body)
    for at in range(6):
        out_ref[at] = end_ref[at].T.astype(jnp.bfloat16)


VMEM = pl.BlockSpec(memory_space=pltpu.VMEM)
SMEM = pl.BlockSpec(memory_space=pltpu.SMEM)
HBM = pl.BlockSpec(memory_space=pltpu.HBM)
BYTES = 8_000_000


def call(kernel, name, in_specs, shapes, scratch, cost=0):
    return pl.pallas_call(
        kernel,
        out_shape=[jax.ShapeDtypeStruct(s, d) for s, d in shapes],
        in_specs=in_specs,
        out_specs=[VMEM] * len(shapes),
        scratch_shapes=scratch,
        compiler_params=pltpu.CompilerParams(vmem_limit_bytes=16 * 1024 * 1024),
        cost_estimate=pl.CostEstimate(flops=0, bytes_accessed=cost, transcendentals=0) if cost else None,
        name=name,
    )


def swap(odd, even, axis):
    count = lax.axis_size(axis)
    evens = [(s, s ^ 1) for s in range(count)]
    odds = [(s, (((s - 1) % count ^ 1) + 1) % count) for s in range(count)]
    from_even = lax.ppermute(even, axis, evens)
    from_odd = lax.ppermute(odd, axis, odds)
    return from_odd, from_even


def on_device(velocity, position_code, occupancy, shifts, axis_ids):
    vel_in = velocity.reshape(6, 256, 128)
    code_in = position_code.reshape(2, 256, 128)
    occ = occupancy.reshape(2, 256)
    ids_in = axis_ids.reshape(ITERS, 2, 256)

    def rows(count):
        return ((count, 256), F32)

    def room(*shape):
        return pltpu.VMEM(shape, F32)

    vel_shape, code_shape = ((6, 128, 256), F32), ((2, 128, 256), jnp.int32)
    table_shape, axes_shape = ((2, WIDE, 256), F32), ((3, 8, 256), F32)
    moments, table = room(128, 256), room(2, WIDE, 256)
    small = [room(24, 256), room(4, 8, 256)]

    vel, code, sums, odd, even = call(
        start_kernel, "start", [HBM] * 5, [vel_shape, code_shape, rows(24), rows(12), rows(12)],
        [moments, pltpu.VMEM((6, 256, 128), jnp.bfloat16), pltpu.VMEM((2, 256, 128), jnp.int32), pltpu.VMEM((2, 256), jnp.int32), pltpu.VMEM((ITERS, 2, 256), jnp.int32), pltpu.SMEM((ITERS, 3), jnp.int32), pltpu.SemaphoreType.DMA((11,))],
    )(*(pltpu.with_memory_space_constraint(x, pltpu.HBM) for x in (shifts, vel_in, code_in, occ, ids_in)))

    from_odd, from_even = swap(odd, even, "gy")
    sums, odd, even = call(
        functools.partial(middle_kernel, True), "middle0", [VMEM] * 4, [rows(36), rows(24), rows(24)], [],
    )(sums, from_odd, from_even, ids_in)
    from_odd, from_even = swap(odd, even, "gx")
    joints = call(joint_kernel, "joint", [SMEM, VMEM], [rows(56), rows(56)], [], BYTES)(shifts, code)
    vel, ids, sums, odd, even = call(
        first_kernel, "first", [SMEM] + [VMEM] * 6, [vel_shape, rows(32), rows(24), rows(8), rows(8)], [moments, *small, table],
    )(shifts, vel, code, sums, from_odd, from_even, joints[0])

    shift = None
    for step in range(1, ITERS):
        last = step == ITERS - 1
        from_odd, from_even = swap(odd, even, "gy")
        sums, odd, even = call(
            functools.partial(middle_kernel, False), f"middle{step}", [VMEM] * 3, [rows(24), rows(12), rows(12)], [],
        )(sums, from_odd, from_even)
        from_odd, from_even = swap(odd, even, "gx")
        args = [shifts, code, ids, vel] + ([] if step == 1 else [shift])
        vel, axes, *moms = call(
            functools.partial(turn_kernel, step), f"turn{step}", [SMEM] + [VMEM] * (len(args) - 1),
            [vel_shape, axes_shape] + ([] if last else [rows(128)]), [table], BYTES,
        )(*args)
        if last:
            out, out_means = call(
                last_kernel, "last", [SMEM] + [VMEM] * 6, [((6, 256, 128), jnp.bfloat16), ((3, 2, 256), F32)],
                [*small, table, room(6, 128, 256)],
            )(shifts, code, vel, sums, from_odd, from_even, axes)
        else:
            shift, sums, odd, even = call(
                functools.partial(shift_kernel, step), f"shift{step}", [SMEM] + [VMEM] * 6,
                [table_shape, rows(24), rows(8), rows(8)], [*small, moments],
            )(shifts, sums, from_odd, from_even, axes, moms[0], joints[step - 1])
    return out.reshape(velocity.shape), out_means.reshape(3, *occupancy.shape)


def solution(mesh):
    in_specs = (
        P(None, "gx", "gy", None, None),
        P("gx", "gy", None, None),
        P("gx", "gy", None),
        P(),
        P(None, "gx", "gy", None),
    )
    out_specs = (P(None, "gx", "gy", None, None), P(None, "gx", "gy", None))
    return jax.shard_map(
        on_device, mesh=mesh, in_specs=in_specs, out_specs=out_specs, check_vma=False
    )
```

time: 99.4 us -> 92 us (0.926)
  waiting for transfers between devices: 17.1 us -> 8.28 us
  Pallas kernels: 12.8 us -> 18.2 us
  local copies, waits for them, and re-layouts: 3.95 us -> 0.01 us
    pallas_call x9 -> x13, Pallas kernels: 12.8 us -> 18.2 us  [the longest x3 6.16 us: on_device(): call(functools.partial(turn_kernel, step), f'turn{step}', [SMEM] + [VMEM]...]
    ppermute x8, waiting for transfers between devices: 9.78 us -> 5.31 us  [swap(): from_even = lax.ppermute(even, axis, evens)]
    ppermute x8, waiting for transfers between devices: 7.33 us -> 2.97 us  [swap(): from_odd = lax.ppermute(odd, axis, odds)]
    unnamed x8 -> x4, local copies, waits for them, and re-layouts: 2.64 us -> 0.01 us
    reshape x2 -> x0, local copies, waits for them, and re-layouts: 1.31 us -> none  [the longest x1 0.71 us: on_device(): ids_in = axis_ids.reshape(8, 256)]
  transfers between devices with their start and end apart: 16 -> 16, of which waited for: 10 -> 9; matrix products, arithmetic and copies ran while one was open for 0% -> 0% of each run, Pallas kernels for 0% -> 10%
where the time goes in v2:
time: 92 us; the launch traced here: 91.4 us
  starting transfers between devices  64 us (70%)
  Pallas kernels  18.2 us (20%)
  waiting for transfers between devices  8.28 us (9%)
    ppermute x8, starting transfers between devices, swap(): from_odd = lax.ppermute(odd, axis, odds)  37.3 us
    ppermute x8, starting transfers between devices, swap(): from_even = lax.ppermute(even, axis, evens)  26.7 us
    pallas_call x3, Pallas kernels, on_device(): call(functools.partial(turn_kernel, step), f'turn{step}', [SMEM] + [VMEM]...  6.16 us
    ppermute x8, waiting for transfers between devices, swap(): from_even = lax.ppermute(even, axis, evens)  5.31 us
    pallas_call x1, Pallas kernels, on_device(): call(start_kernel, 'start', [HBM] * 5, [vel_shape, code_shape, rows(24),...  3.02 us
    ppermute x8, waiting for transfers between devices, swap(): from_odd = lax.ppermute(odd, axis, odds)  2.97 us
    pallas_call x1, Pallas kernels, on_device(): call(first_kernel, 'first', [SMEM] + [VMEM] * 6, [vel_shape, rows(32), ro...  2.71 us
    pallas_call x1, Pallas kernels, on_device(): call(joint_kernel, 'joint', [SMEM, VMEM], [rows(56), rows(56)], [], BYTES)  2.59 us
  transfers between devices with their start and end apart: 16, of which 9 were waited for; matrix products, arithmetic and copies ran while one was open for 0% of the time, Pallas kernels for 10%

profile of v2, /device:TPU:1, one launch (start us, length us, event | category | flops | bytes accessed | tf_op | source)
XLA Modules:
  0.0 91.4 jit_solution(11998668689308978473)
XLA Ops:
  0.6 0.0 copy-start.1
  0.6 3.0 %start.1 = (f32[6,128,256]{2,1,0:T(8,128)S(1)}, s32[2,128,256]{2,1,0:T(8,128)S(1)}, f32[24,256]{1,0:T(8,128)S(1)}, f32[12,256]{1,0:T(8,128)S(1)}, f32[12,256]{1,0:T(8,128)S(1)}) custom-call(s32[4,3]{1,0:T(4,128)} %shifts_ref.9, bf16[6,256,128]{2,1,0:T(8,128)(2,1)} %bitcast.12, s32[2,256,128]{2,1,0:T(8,128)} %bitcast.13, s32[2,256]{1,0:T(2,128)} %bitcast.14, ...), custom_call_target="tpu_custom_call" | custom-call | tf_op jit(solution)/shard_map/start/pallas_call | solution.py:441
  3.7 5.4 %collective-permute-start = (f32[12,256]{1,0:T(8,128)S(1)}, f32[12,256]{1,0:T(8,128)S(1)}, u32[]{:S(2)}, u32[]{:S(2)}) collective-permute-start(f32[12,256]{1,0:T(8,128)S(1)} %get-tuple-element.47), channel_id=1, source_target_pairs={{0,31},{1,2},{2,1},{3,4},{4,3},{5,6},{6,5},{7,8},{8,7},{9,10},{10,... | collective-permute-start | bytes 36872 | tf_op jit(solution)/shard_map/ppermute | solution.py:420
  9.1 5.3 %collective-permute-start.1 = (f32[12,256]{1,0:T(8,128)S(1)}, f32[12,256]{1,0:T(8,128)S(1)}, u32[]{:S(2)}, u32[]{:S(2)}) collective-permute-start(f32[12,256]{1,0:T(8,128)S(1)} %get-tuple-element.48), channel_id=1, source_target_pairs={{0,1},{1,0},{2,3},{3,2},{4,5},{5,4},{6,7},{7,6},{8,9},{9,8},{10,11... | collective-permute-start | bytes 36872 | tf_op jit(solution)/shard_map/ppermute | solution.py:419
  14.4 0.0 collective-permute-done.refs_1_
  14.4 0.8 collective-permute-done.1.refs_2_
  15.2 0.0 copy-done.1
  15.2 0.0 copy-start
  15.3 11.3 %collective-permute-start.2 = (f32[24,256]{1,0:T(8,128)S(1)}, f32[24,256]{1,0:T(8,128)S(1)}, u32[]{:S(2)}, u32[]{:S(2)}) collective-permute-start(f32[24,256]{1,0:T(8,128)S(1)} %get-tuple-element.50), channel_id=1, source_target_pairs={{0,480},{32,64},{64,32},{96,128},{128,96},{160,192},{192,160},{224... | collective-permute-start | bytes 73736 | tf_op jit(solution)/shard_map/ppermute | solution.py:420
  26.5 1.9 %collective-permute-start.3 = (f32[24,256]{1,0:T(8,128)S(1)}, f32[24,256]{1,0:T(8,128)S(1)}, u32[]{:S(2)}, u32[]{:S(2)}) collective-permute-start(f32[24,256]{1,0:T(8,128)S(1)} %get-tuple-element.51), channel_id=1, source_target_pairs={{0,32},{32,0},{64,96},{96,64},{128,160},{160,128},{192,224},{224,1... | collective-permute-start | bytes 73736 | tf_op jit(solution)/shard_map/ppermute | solution.py:419
  28.5 0.0 copy-done
  28.5 2.6 %joint.1 = (f32[56,256]{1,0:T(8,128)S(1)}, f32[56,256]{1,0:T(8,128)S(1)}) custom-call(s32[4,3]{1,0:T(4,128)S(1)} %copy-done, s32[2,128,256]{2,1,0:T(8,128)S(1)} %get-tuple-element.44.code_ref.refs_1_), custom_call_target="tpu_custom_call" | custom-call | bytes 8000000 | tf_op jit(solution)/shard_map/joint/pallas_call | solution.py:451
  31.1 0.0 collective-permute-done.2.from_odd_ref
  31.1 0.9 %collective-permute-done.3.from_even_ref = f32[24,256]{1,0:T(8,128)S(1)} collective-permute-done((f32[24,256]{1,0:T(8,128)S(1)}, f32[24,256]{1,0:T(8,128)S(1)}, u32[]{:S(2)}, u32[]{:S(2)}) %collective-permute-start.3) | collective-permute-done | bytes 24608 | tf_op jit(solution)/shard_map/ppermute | solution.py:419
  32.0 2.7 %first.1 = (f32[6,128,256]{2,1,0:T(8,128)S(1)}, f32[32,256]{1,0:T(8,128)S(1)}, f32[24,256]{1,0:T(8,128)S(1)}, f32[8,256]{1,0:T(8,128)S(1)}, f32[8,256]{1,0:T(8,128)S(1)}) custom-call(s32[4,3]{1,0:T(4,128)S(1)} %copy-done, f32[6,128,256]{2,1,0:T(8,128)S(1)} %get-tuple-element.45.vel_ref, s32[2,128,256]{2,1,0:T(8,128)S(1)} %get-tuple-element.44.code_ref.refs_1_, ...), custom_call_target="tpu_custom_call" | custom-call | tf_op jit(solution)/shard_map/first/pallas_call | solution.py:452
  34.7 2.3 %collective-permute-start.4 = (f32[8,256]{1,0:T(8,128)S(1)}, f32[8,256]{1,0:T(8,128)S(1)}, u32[]{:S(2)}, u32[]{:S(2)}) collective-permute-start(f32[8,256]{1,0:T(8,128)S(1)} %get-tuple-element.57), channel_id=1, source_target_pairs={{0,31},{1,2},{2,1},{3,4},{4,3},{5,6},{6,5},{7,8},{8,7},{9,10},{10,... | collective-permute-start | bytes 24584 | tf_op jit(solution)/shard_map/ppermute | solution.py:420
  37.0 4.1 %collective-permute-start.5 = (f32[8,256]{1,0:T(8,128)S(1)}, f32[8,256]{1,0:T(8,128)S(1)}, u32[]{:S(2)}, u32[]{:S(2)}) collective-permute-start(f32[8,256]{1,0:T(8,128)S(1)} %get-tuple-element.58), channel_id=1, source_target_pairs={{0,1},{1,0},{2,3},{3,2},{4,5},{5,4},{6,7},{7,6},{8,9},{9,8},{10,11... | collective-permute-start | bytes 24584 | tf_op jit(solution)/shard_map/ppermute | solution.py:419
  41.1 0.0 collective-permute-done.4.refs_1_
  41.1 0.8 collective-permute-done.5.refs_2_
  41.9 3.3 %collective-permute-start.6 = (f32[12,256]{1,0:T(8,128)S(1)}, f32[12,256]{1,0:T(8,128)S(1)}, u32[]{:S(2)}, u32[]{:S(2)}) collective-permute-start(f32[12,256]{1,0:T(8,128)S(1)} %get-tuple-element.60), channel_id=1, source_target_pairs={{0,480},{32,64},{64,32},{96,128},{128,96},{160,192},{192,160},{224... | collective-permute-start | bytes 36872 | tf_op jit(solution)/shard_map/ppermute | solution.py:420
  45.2 2.0 %collective-permute-start.7 = (f32[12,256]{1,0:T(8,128)S(1)}, f32[12,256]{1,0:T(8,128)S(1)}, u32[]{:S(2)}, u32[]{:S(2)}) collective-permute-start(f32[12,256]{1,0:T(8,128)S(1)} %get-tuple-element.61), channel_id=1, source_target_pairs={{0,32},{32,0},{64,96},{96,64},{128,160},{160,128},{192,224},{224,1... | collective-permute-start | bytes 36872 | tf_op jit(solution)/shard_map/ppermute | solution.py:419
  47.2 2.1 %turn1.1 = (f32[6,128,256]{2,1,0:T(8,128)S(1)}, f32[3,8,256]{2,1,0:T(8,128)S(1)}, f32[128,256]{1,0:T(8,128)S(1)}) custom-call(s32[4,3]{1,0:T(4,128)S(1)} %copy-done, s32[2,128,256]{2,1,0:T(8,128)S(1)} %get-tuple-element.44.code_ref.refs_1_, f32[32,256]{1,0:T(8,128)S(1)} %get-tuple-element.53.refs_2_, f32[6,128,256]{2,1,0:T(8,128)S(1)} %get-tuple-element.54.refs_3_), custom_call_target="tpu_custom_call" | custom-call | bytes 8000000 | tf_op jit(solution)/shard_map/turn1/pallas_call | solution.py:465
  49.3 1.3 %collective-permute-done.6.from_odd_ref = f32[12,256]{1,0:T(8,128)S(1)} collective-permute-done((f32[12,256]{1,0:T(8,128)S(1)}, f32[12,256]{1,0:T(8,128)S(1)}, u32[]{:S(2)}, u32[]{:S(2)}) %collective-permute-start.6) | collective-permute-done | bytes 12320 | tf_op jit(solution)/shard_map/ppermute | solution.py:420
  50.6 0.0 collective-permute-done.7.from_even_ref
  50.6 0.8 shift1.1
  51.5 2.9 %collective-permute-start.8 = (f32[8,256]{1,0:T(8,128)S(1)}, f32[8,256]{1,0:T(8,128)S(1)}, u32[]{:S(2)}, u32[]{:S(2)}) collective-permute-start(f32[8,256]{1,0:T(8,128)S(1)} %get-tuple-element.67), channel_id=1, source_target_pairs={{0,31},{1,2},{2,1},{3,4},{4,3},{5,6},{6,5},{7,8},{8,7},{9,10},{10,... | collective-permute-start | bytes 24584 | tf_op jit(solution)/shard_map/ppermute | solution.py:420
  54.4 4.3 %collective-permute-start.9 = (f32[8,256]{1,0:T(8,128)S(1)}, f32[8,256]{1,0:T(8,128)S(1)}, u32[]{:S(2)}, u32[]{:S(2)}) collective-permute-start(f32[8,256]{1,0:T(8,128)S(1)} %get-tuple-element.68), channel_id=1, source_target_pairs={{0,1},{1,0},{2,3},{3,2},{4,5},{5,4},{6,7},{7,6},{8,9},{9,8},{10,11... | collective-permute-start | bytes 24584 | tf_op jit(solution)/shard_map/ppermute | solution.py:419
  58.7 0.0 collective-permute-done.8.refs_1_
  58.8 0.8 collective-permute-done.9.refs_2_
  59.6 6.2 %collective-permute-start.10 = (f32[12,256]{1,0:T(8,128)S(1)}, f32[12,256]{1,0:T(8,128)S(1)}, u32[]{:S(2)}, u32[]{:S(2)}) collective-permute-start(f32[12,256]{1,0:T(8,128)S(1)} %get-tuple-element.70), channel_id=1, source_target_pairs={{0,480},{32,64},{64,32},{96,128},{128,96},{160,192},{192,160},{224... | collective-permute-start | bytes 36872 | tf_op jit(solution)/shard_map/ppermute | solution.py:420
  65.8 1.9 %collective-permute-start.11 = (f32[12,256]{1,0:T(8,128)S(1)}, f32[12,256]{1,0:T(8,128)S(1)}, u32[]{:S(2)}, u32[]{:S(2)}) collective-permute-start(f32[12,256]{1,0:T(8,128)S(1)} %get-tuple-element.71), channel_id=1, source_target_pairs={{0,32},{32,0},{64,96},{96,64},{128,160},{160,128},{192,224},{224,1... | collective-permute-start | bytes 36872 | tf_op jit(solution)/shard_map/ppermute | solution.py:419
  67.7 2.4 %turn2.1 = (f32[6,128,256]{2,1,0:T(8,128)S(1)}, f32[3,8,256]{2,1,0:T(8,128)S(1)}, f32[128,256]{1,0:T(8,128)S(1)}) custom-call(s32[4,3]{1,0:T(4,128)S(1)} %copy-done, s32[2,128,256]{2,1,0:T(8,128)S(1)} %get-tuple-element.44.code_ref.refs_1_, f32[32,256]{1,0:T(8,128)S(1)} %get-tuple-element.53.refs_2_, f32[6,128,256]{2,1,0:T(8,128)S(1)} %get-tuple-element.55.refs_3_, ...), custom_call_target="tpu_custom_call" | custom-call | bytes 8000000 | tf_op jit(solution)/shard_map/turn2/pallas_call | solution.py:465
  70.1 0.0 collective-permute-done.10.from_odd_ref
  70.1 1.0 %collective-permute-done.11.from_even_ref = f32[12,256]{1,0:T(8,128)S(1)} collective-permute-done((f32[12,256]{1,0:T(8,128)S(1)}, f32[12,256]{1,0:T(8,128)S(1)}, u32[]{:S(2)}, u32[]{:S(2)}) %collective-permute-start.11) | collective-permute-done | bytes 12320 | tf_op jit(solution)/shard_map/ppermute | solution.py:419
  71.1 0.8 shift2.1
  72.0 2.4 %collective-permute-start.12 = (f32[8,256]{1,0:T(8,128)S(1)}, f32[8,256]{1,0:T(8,128)S(1)}, u32[]{:S(2)}, u32[]{:S(2)}) collective-permute-start(f32[8,256]{1,0:T(8,128)S(1)} %get-tuple-element.78), channel_id=1, source_target_pairs={{0,31},{1,2},{2,1},{3,4},{4,3},{5,6},{6,5},{7,8},{8,7},{9,10},{10,... | collective-permute-start | bytes 24584 | tf_op jit(solution)/shard_map/ppermute | solution.py:420
  74.4 5.3 %collective-permute-start.13 = (f32[8,256]{1,0:T(8,128)S(1)}, f32[8,256]{1,0:T(8,128)S(1)}, u32[]{:S(2)}, u32[]{:S(2)}) collective-permute-start(f32[8,256]{1,0:T(8,128)S(1)} %get-tuple-element.79), channel_id=1, source_target_pairs={{0,1},{1,0},{2,3},{3,2},{4,5},{5,4},{6,7},{7,6},{8,9},{9,8},{10,11... | collective-permute-start | bytes 24584 | tf_op jit(solution)/shard_map/ppermute | solution.py:419
  79.7 0.0 collective-permute-done.12.refs_1_
  79.7 0.8 collective-permute-done.13.refs_2_
  80.5 3.5 %collective-permute-start.14 = (f32[12,256]{1,0:T(8,128)S(1)}, f32[12,256]{1,0:T(8,128)S(1)}, u32[]{:S(2)}, u32[]{:S(2)}) collective-permute-start(f32[12,256]{1,0:T(8,128)S(1)} %get-tuple-element.81), channel_id=1, source_target_pairs={{0,480},{32,64},{64,32},{96,128},{128,96},{160,192},{192,160},{224... | collective-permute-start | bytes 36872 | tf_op jit(solution)/shard_map/ppermute | solution.py:420
  84.0 1.9 %collective-permute-start.15 = (f32[12,256]{1,0:T(8,128)S(1)}, f32[12,256]{1,0:T(8,128)S(1)}, u32[]{:S(2)}, u32[]{:S(2)}) collective-permute-start(f32[12,256]{1,0:T(8,128)S(1)} %get-tuple-element.82), channel_id=1, source_target_pairs={{0,32},{32,0},{64,96},{96,64},{128,160},{160,128},{192,224},{224,1... | collective-permute-start | bytes 36872 | tf_op jit(solution)/shard_map/ppermute | solution.py:419
  85.9 1.6 %turn3.1 = (f32[6,128,256]{2,1,0:T(8,128)S(1)}, f32[3,8,256]{2,1,0:T(8,128)S(1)}) custom-call(s32[4,3]{1,0:T(4,128)S(1)} %copy-done, s32[2,128,256]{2,1,0:T(8,128)S(1)} %get-tuple-element.44.code_ref.refs_1_, f32[32,256]{1,0:T(8,128)S(1)} %get-tuple-element.53.refs_2_, f32[6,128,256]{2,1,0:T(8,128)S(1)} %get-tuple-element.65.refs_3_, ...), custom_call_target="tpu_custom_call" | custom-call | bytes 8000000 | tf_op jit(solution)/shard_map/turn3/pallas_call | solution.py:465
  87.5 1.7 %collective-permute-done.14.from_odd_ref = f32[12,256]{1,0:T(8,128)S(1)} collective-permute-done((f32[12,256]{1,0:T(8,128)S(1)}, f32[12,256]{1,0:T(8,128)S(1)}, u32[]{:S(2)}, u32[]{:S(2)}) %collective-permute-start.14) | collective-permute-done | bytes 12320 | tf_op jit(solution)/shard_map/ppermute | solution.py:420
  89.2 0.2 collective-permute-done.15.from_even_ref
  89.4 2.0 %last.1 = (bf16[6,256,128]{2,1,0:T(8,128)(2,1)}, f32[3,2,256]{2,1,0:T(2,128)}) custom-call(s32[4,3]{1,0:T(4,128)S(1)} %copy-done, s32[2,128,256]{2,1,0:T(8,128)S(1)} %get-tuple-element.44.code_ref.refs_1_, f32[6,128,256]{2,1,0:T(8,128)S(1)} %get-tuple-element.76.vel_ref, f32[24,256]{1,0:T(8,128)S(1)} %get-tuple-element.80.sums_ref, ...), custom_call_target="tpu_custom_call" | custom-call | tf_op jit(solution)/shard_map/last/pallas_call | solution.py:470
  (4 shorter events, 0.1 us)
Async XLA Ops:
  0.6 14.6 %copy-start.1 = (s32[4,1,2,256]{3,2,1,0:T(2,128)S(1)}, s32[4,1,2,256]{3,2,1,0:T(2,128)}, u32[]{:S(2)}) copy-start(s32[4,1,2,256]{3,2,1,0:T(2,128)} %param.9) | copy-start | bytes 24580
  3.7 10.7 %collective-permute-start = (f32[12,256]{1,0:T(8,128)S(1)}, f32[12,256]{1,0:T(8,128)S(1)}, u32[]{:S(2)}, u32[]{:S(2)}) collective-permute-start(f32[12,256]{1,0:T(8,128)S(1)} %get-tuple-element.47), channel_id=1, source_target_pairs={{0,31},{1,2},{2,1},{3,4},{4,3},{5,6},{6,5},{7,8},{8,7},{9,10},{10,... | collective-permute-start | bytes 36872 | tf_op jit(solution)/shard_map/ppermute | solution.py:420
  9.1 6.1 %collective-permute-start.1 = (f32[12,256]{1,0:T(8,128)S(1)}, f32[12,256]{1,0:T(8,128)S(1)}, u32[]{:S(2)}, u32[]{:S(2)}) collective-permute-start(f32[12,256]{1,0:T(8,128)S(1)} %get-tuple-element.48), channel_id=1, source_target_pairs={{0,1},{1,0},{2,3},{3,2},{4,5},{5,4},{6,7},{7,6},{8,9},{9,8},{10,11... | collective-permute-start | bytes 36872 | tf_op jit(solution)/shard_map/ppermute | solution.py:419
  15.2 13.2 %copy-start = (s32[4,3]{1,0:T(4,128)S(1)}, s32[4,3]{1,0:T(4,128)}, u32[]{:S(2)}) copy-start(s32[4,3]{1,0:T(4,128)} %shifts_ref.9) | copy-start | bytes 148
  15.3 15.8 %collective-permute-start.2 = (f32[24,256]{1,0:T(8,128)S(1)}, f32[24,256]{1,0:T(8,128)S(1)}, u32[]{:S(2)}, u32[]{:S(2)}) collective-permute-start(f32[24,256]{1,0:T(8,128)S(1)} %get-tuple-element.50), channel_id=1, source_target_pairs={{0,480},{32,64},{64,32},{96,128},{128,96},{160,192},{192,160},{224... | collective-permute-start | bytes 73736 | tf_op jit(solution)/shard_map/ppermute | solution.py:420
  26.5 5.5 %collective-permute-start.3 = (f32[24,256]{1,0:T(8,128)S(1)}, f32[24,256]{1,0:T(8,128)S(1)}, u32[]{:S(2)}, u32[]{:S(2)}) collective-permute-start(f32[24,256]{1,0:T(8,128)S(1)} %get-tuple-element.51), channel_id=1, source_target_pairs={{0,32},{32,0},{64,96},{96,64},{128,160},{160,128},{192,224},{224,1... | collective-permute-start | bytes 73736 | tf_op jit(solution)/shard_map/ppermute | solution.py:419
  34.7 6.4 %collective-permute-start.4 = (f32[8,256]{1,0:T(8,128)S(1)}, f32[8,256]{1,0:T(8,128)S(1)}, u32[]{:S(2)}, u32[]{:S(2)}) collective-permute-start(f32[8,256]{1,0:T(8,128)S(1)} %get-tuple-element.57), channel_id=1, source_target_pairs={{0,31},{1,2},{2,1},{3,4},{4,3},{5,6},{6,5},{7,8},{8,7},{9,10},{10,... | collective-permute-start | bytes 24584 | tf_op jit(solution)/shard_map/ppermute | solution.py:420
  37.0 4.9 %collective-permute-start.5 = (f32[8,256]{1,0:T(8,128)S(1)}, f32[8,256]{1,0:T(8,128)S(1)}, u32[]{:S(2)}, u32[]{:S(2)}) collective-permute-start(f32[8,256]{1,0:T(8,128)S(1)} %get-tuple-element.58), channel_id=1, source_target_pairs={{0,1},{1,0},{2,3},{3,2},{4,5},{5,4},{6,7},{7,6},{8,9},{9,8},{10,11... | collective-permute-start | bytes 24584 | tf_op jit(solution)/shard_map/ppermute | solution.py:419
  41.9 8.7 %collective-permute-start.6 = (f32[12,256]{1,0:T(8,128)S(1)}, f32[12,256]{1,0:T(8,128)S(1)}, u32[]{:S(2)}, u32[]{:S(2)}) collective-permute-start(f32[12,256]{1,0:T(8,128)S(1)} %get-tuple-element.60), channel_id=1, source_target_pairs={{0,480},{32,64},{64,32},{96,128},{128,96},{160,192},{192,160},{224... | collective-permute-start | bytes 36872 | tf_op jit(solution)/shard_map/ppermute | solution.py:420
  45.2 5.4 %collective-permute-start.7 = (f32[12,256]{1,0:T(8,128)S(1)}, f32[12,256]{1,0:T(8,128)S(1)}, u32[]{:S(2)}, u32[]{:S(2)}) collective-permute-start(f32[12,256]{1,0:T(8,128)S(1)} %get-tuple-element.61), channel_id=1, source_target_pairs={{0,32},{32,0},{64,96},{96,64},{128,160},{160,128},{192,224},{224,1... | collective-permute-start | bytes 36872 | tf_op jit(solution)/shard_map/ppermute | solution.py:419
  51.5 7.3 %collective-permute-start.8 = (f32[8,256]{1,0:T(8,128)S(1)}, f32[8,256]{1,0:T(8,128)S(1)}, u32[]{:S(2)}, u32[]{:S(2)}) collective-permute-start(f32[8,256]{1,0:T(8,128)S(1)} %get-tuple-element.67), channel_id=1, source_target_pairs={{0,31},{1,2},{2,1},{3,4},{4,3},{5,6},{6,5},{7,8},{8,7},{9,10},{10,... | collective-permute-start | bytes 24584 | tf_op jit(solution)/shard_map/ppermute | solution.py:420
  54.4 5.2 %collective-permute-start.9 = (f32[8,256]{1,0:T(8,128)S(1)}, f32[8,256]{1,0:T(8,128)S(1)}, u32[]{:S(2)}, u32[]{:S(2)}) collective-permute-start(f32[8,256]{1,0:T(8,128)S(1)} %get-tuple-element.68), channel_id=1, source_target_pairs={{0,1},{1,0},{2,3},{3,2},{4,5},{5,4},{6,7},{7,6},{8,9},{9,8},{10,11... | collective-permute-start | bytes 24584 | tf_op jit(solution)/shard_map/ppermute | solution.py:419
  59.6 10.6 %collective-permute-start.10 = (f32[12,256]{1,0:T(8,128)S(1)}, f32[12,256]{1,0:T(8,128)S(1)}, u32[]{:S(2)}, u32[]{:S(2)}) collective-permute-start(f32[12,256]{1,0:T(8,128)S(1)} %get-tuple-element.70), channel_id=1, source_target_pairs={{0,480},{32,64},{64,32},{96,128},{128,96},{160,192},{192,160},{224... | collective-permute-start | bytes 36872 | tf_op jit(solution)/shard_map/ppermute | solution.py:420
  65.8 5.4 %collective-permute-start.11 = (f32[12,256]{1,0:T(8,128)S(1)}, f32[12,256]{1,0:T(8,128)S(1)}, u32[]{:S(2)}, u32[]{:S(2)}) collective-permute-start(f32[12,256]{1,0:T(8,128)S(1)} %get-tuple-element.71), channel_id=1, source_target_pairs={{0,32},{32,0},{64,96},{96,64},{128,160},{160,128},{192,224},{224,1... | collective-permute-start | bytes 36872 | tf_op jit(solution)/shard_map/ppermute | solution.py:419
  72.0 7.7 %collective-permute-start.12 = (f32[8,256]{1,0:T(8,128)S(1)}, f32[8,256]{1,0:T(8,128)S(1)}, u32[]{:S(2)}, u32[]{:S(2)}) collective-permute-start(f32[8,256]{1,0:T(8,128)S(1)} %get-tuple-element.78), channel_id=1, source_target_pairs={{0,31},{1,2},{2,1},{3,4},{4,3},{5,6},{6,5},{7,8},{8,7},{9,10},{10,... | collective-permute-start | bytes 24584 | tf_op jit(solution)/shard_map/ppermute | solution.py:420
  74.4 6.1 %collective-permute-start.13 = (f32[8,256]{1,0:T(8,128)S(1)}, f32[8,256]{1,0:T(8,128)S(1)}, u32[]{:S(2)}, u32[]{:S(2)}) collective-permute-start(f32[8,256]{1,0:T(8,128)S(1)} %get-tuple-element.79), channel_id=1, source_target_pairs={{0,1},{1,0},{2,3},{3,2},{4,5},{5,4},{6,7},{7,6},{8,9},{9,8},{10,11... | collective-permute-start | bytes 24584 | tf_op jit(solution)/shard_map/ppermute | solution.py:419
  80.5 8.7 %collective-permute-start.14 = (f32[12,256]{1,0:T(8,128)S(1)}, f32[12,256]{1,0:T(8,128)S(1)}, u32[]{:S(2)}, u32[]{:S(2)}) collective-permute-start(f32[12,256]{1,0:T(8,128)S(1)} %get-tuple-element.81), channel_id=1, source_target_pairs={{0,480},{32,64},{64,32},{96,128},{128,96},{160,192},{192,160},{224... | collective-permute-start | bytes 36872 | tf_op jit(solution)/shard_map/ppermute | solution.py:420
  84.0 5.4 %collective-permute-start.15 = (f32[12,256]{1,0:T(8,128)S(1)}, f32[12,256]{1,0:T(8,128)S(1)}, u32[]{:S(2)}, u32[]{:S(2)}) collective-permute-start(f32[12,256]{1,0:T(8,128)S(1)} %get-tuple-element.82), channel_id=1, source_target_pairs={{0,32},{32,0},{64,96},{96,64},{128,160},{160,128},{192,224},{224,1... | collective-permute-start | bytes 36872 | tf_op jit(solution)/shard_map/ppermute | solution.py:419

commit v3 on v2

--- a/solution.py
+++ b/solution.py
@@ -20,6 +20,7 @@
 F32 = jnp.float32
 CHUNK = 32
 WIDE = 48
+WIDE_STEP = 2
 
 
 def axis_table():
@@ -61,7 +62,7 @@
         return tuple(out)
 
     zero = jnp.zeros((8, 128), F32)
-    acc = lax.fori_loop(0, 16, body, (zero,) * (8 * count), unroll=2)
+    acc = lax.fori_loop(0, 16, body, (zero,) * (8 * count), unroll=16)
     for comp in range(count):
         for moment in range(8):
             row = (col * 8 + moment) * 8 + comp
@@ -110,13 +111,27 @@
     return moment_of
 
 
-def fill_messages_y(sums_ref, odd_ref, even_ref):
+def fill_messages_y(sums_ref, odd_ref, even_ref, columns=1, first=0):
     odd = is_odd("gy")
+    size = columns * 4
     for hop in range(2):
-        left = sums_ref[hop * 12 : hop * 12 + 4, :]
-        right = sums_ref[hop * 12 + 8 : hop * 12 + 12, :]
-        odd_ref[hop * 4 : hop * 4 + 4, :] = jnp.where(odd, right, left)
-        even_ref[hop * 4 : hop * 4 + 4, :] = jnp.where(odd, left, right)
+        left = sums_ref[hop * 12 : hop * 12 + size, :]
+        right = sums_ref[hop * 12 + 12 - size : hop * 12 + 12, :]
+        rows = slice(first + hop * size, first + hop * size + size)
+        odd_ref[rows, :] = jnp.where(odd, right, left)
+        even_ref[rows, :] = jnp.where(odd, left, right)
+
+
+def fill_messages_x(out_ref, size, odd_ref, even_ref):
+    odd = is_odd("gx")
+    low, high = out_ref[0:size, :], out_ref[size : 2 * size, :]
+    odd_ref[0:size, :] = jnp.where(odd, high, low)
+    even_ref[0:size, :] = jnp.where(odd, low, high)
+
+
+def from_sides(axis, from_odd, from_even):
+    odd = is_odd(axis)
+    return jnp.where(odd, from_even, from_odd), jnp.where(odd, from_odd, from_even)
 
 
 def start_kernel(shifts_hbm, vel_hbm, code_hbm, occ_hbm, ids_hbm, vel_ref, code_ref, sums_ref, odd_ref, even_ref, mom_ref, vel_in_ref, code_in_ref, occ_ref, ids_ref, shifts_ref, sems):
@@ -152,6 +167,9 @@
         ids = ids_ref[step, 0:1, :].astype(F32)
         odd_ref[8 + step : 9 + step, :] = ids
         even_ref[8 + step : 9 + step, :] = ids
+    far = ids_ref[WIDE_STEP, 1:2, :].astype(F32)
+    odd_ref[12:13, :] = far
+    even_ref[12:13, :] = far
     deposit(vel_ref, code_ref, shifts_ref, 0, mom_ref, True)
     cell_sums(stored_moment(mom_ref), sums_ref)
     fill_messages_y(sums_ref, odd_ref, even_ref)
@@ -162,36 +180,49 @@
         sums_ref, from_odd_ref, from_even_ref, ids_ref, out_ref, odd_ref, even_ref = refs
     else:
         sums_ref, from_odd_ref, from_even_ref, out_ref, odd_ref, even_ref = refs
-    odd_y, odd_x = is_odd("gy"), is_odd("gx")
     out_ref[0:24, :] = sums_ref[...]
     for hop in range(2):
         rows = slice(hop * 4, hop * 4 + 4)
-        by_odd, by_even = from_odd_ref[rows, :], from_even_ref[rows, :]
+        by_left, by_right = from_sides("gy", from_odd_ref[rows, :], from_even_ref[rows, :])
         left = slice(hop * 12, hop * 12 + 4)
         right = slice(hop * 12 + 8, hop * 12 + 12)
-        out_ref[left, :] = out_ref[left, :] + jnp.where(odd_y, by_even, by_odd)
-        out_ref[right, :] = out_ref[right, :] + jnp.where(odd_y, by_odd, by_even)
-    low, high = out_ref[0:12, :], out_ref[12:24, :]
-    odd_ref[0:12, :] = jnp.where(odd_x, high, low)
-    even_ref[0:12, :] = jnp.where(odd_x, low, high)
+        out_ref[left, :] = out_ref[left, :] + by_left
+        out_ref[right, :] = out_ref[right, :] + by_right
+    fill_messages_x(out_ref, 12, odd_ref, even_ref)
     if first:
         for step in range(ITERS):
             row = 24 + step * 3
             out_ref[row : row + 2, :] = ids_ref[step].astype(F32)
-            by_odd, by_even = from_odd_ref[8 + step : 9 + step, :], from_even_ref[8 + step : 9 + step, :]
-            out_ref[row + 2 : row + 3, :] = jnp.where(odd_y, by_odd, by_even)
-        own = out_ref[24:36, :]
-        odd_ref[12:24, :] = own
-        even_ref[12:24, :] = own
-
-
-def cell_means(sums_ref, from_odd_ref, from_even_ref, work_ref, tot_ref):
-    odd_x = is_odd("gx")
-    by_odd, by_even = from_odd_ref[0:12, :], from_even_ref[0:12, :]
-    work_ref[0:12, :] = sums_ref[0:12, :] + jnp.where(odd_x, by_even, by_odd)
-    work_ref[12:24, :] = sums_ref[12:24, :] + jnp.where(odd_x, by_odd, by_even)
+            _, by_right = from_sides("gy", from_odd_ref[8 + step : 9 + step, :], from_even_ref[8 + step : 9 + step, :])
+            out_ref[row + 2 : row + 3, :] = by_right
+        by_left, by_right = from_sides("gy", from_odd_ref[12:13, :], from_even_ref[12:13, :])
+        out_ref[36:37, :] = by_left
+        out_ref[37:38, :] = by_right
+        own = out_ref[24:38, :]
+        odd_ref[12:26, :] = own
+        even_ref[12:26, :] = own
+
+
+def wide_middle_kernel(sums_ref, from_odd_ref, from_even_ref, out_ref, odd_ref, even_ref):
+    for hop in range(2):
+        at, own = hop * 20, hop * 12
+        rows = slice(hop * 8, hop * 8 + 8)
+        by_left, by_right = from_sides("gy", from_odd_ref[rows, :], from_even_ref[rows, :])
+        out_ref[at : at + 8, :] = by_left
+        out_ref[at + 12 : at + 20, :] = by_right
+        out_ref[at + 8 : at + 12, :] = sums_ref[own + 4 : own + 8, :]
+        out_ref[at + 4 : at + 8, :] = out_ref[at + 4 : at + 8, :] + sums_ref[own : own + 4, :]
+        out_ref[at + 12 : at + 16, :] = out_ref[at + 12 : at + 16, :] + sums_ref[own + 8 : own + 12, :]
+    fill_messages_x(out_ref, 20, odd_ref, even_ref)
+
+
+def cell_means(sums_ref, from_odd_ref, from_even_ref, work_ref, tot_ref, width=3):
+    size = width * 4
+    by_low, by_high = from_sides("gx", from_odd_ref[0:size, :], from_even_ref[0:size, :])
+    work_ref[0:size, :] = sums_ref[0:size, :] + by_low
+    work_ref[size : 2 * size, :] = sums_ref[size : 2 * size, :] + by_high
     tot_ref[...] = jnp.zeros_like(tot_ref)
-    for cell in range(6):
+    for cell in range(2 * width):
         for comp in range(4):
             tot_ref[comp, cell : cell + 1, :] = work_ref[cell * 4 + comp : cell * 4 + comp + 1, :]
     count = jnp.maximum(tot_ref[3], 1.0)
@@ -199,7 +230,7 @@
 
 
 def cell_axes(ids):
-    axes = [jnp.zeros((8, 256), F32) for _ in range(3)]
+    axes = [jnp.zeros(ids.shape, F32) for _ in range(3)]
     for k in range(NAXES):
         match = ids == float(k)
         axes = [jnp.where(match, float(AXES[comp, k]), axes[comp]) for comp in range(3)]
@@ -219,8 +250,8 @@
     return pltpu.roll(value, 255, 1)
 
 
-def store_cells(table_ref, parts):
-    for cell in range(6):
+def store_cells(table_ref, parts, cells=6):
+    for cell in range(cells):
         for comp, part in enumerate(parts):
             table_ref[0, cell * 8 + comp : cell * 8 + comp + 1, :] = part[cell : cell + 1, :]
     table_ref[1] = next_z(table_ref[0])
@@ -243,16 +274,23 @@
         body(pl.ds(pl.multiple_of(i * CHUNK, CHUNK), CHUNK))
         return carry
 
-    lax.fori_loop(0, 128 // CHUNK, run, 0)
-
-
-def first_kernel(shifts_ref, vel_ref, code_ref, sums_ref, from_odd_ref, from_even_ref, joint_ref, out_ref, ids_ref, new_ref, odd_ref, even_ref, mom_ref, work_ref, tot_ref, table_ref):
-    odd_x = is_odd("gx")
+    lax.fori_loop(0, 128 // CHUNK, run, 0, unroll=128 // CHUNK)
+
+
+def first_kernel(shifts_ref, vel_ref, code_ref, sums_ref, from_odd_ref, from_even_ref, joint_ref, out_ref, ids_ref, far_ids_ref, new_ref, odd_ref, even_ref, mom_ref, work_ref, tot_ref, table_ref):
     ids_ref[...] = jnp.zeros_like(ids_ref)
+    far_ids_ref[...] = jnp.zeros_like(far_ids_ref)
+    _, by_high = from_sides("gx", from_odd_ref[12:26, :], from_even_ref[12:26, :])
+    work_ref[0:14, :] = by_high
     for t in range(ITERS):
         ids_ref[t * 8 : t * 8 + 3, :] = sums_ref[24 + t * 3 : 27 + t * 3, :]
-        rows = slice(12 + t * 3, 15 + t * 3)
-        ids_ref[t * 8 + 3 : t * 8 + 6, :] = jnp.where(odd_x, from_odd_ref[rows, :], from_even_ref[rows, :])
+        ids_ref[t * 8 + 3 : t * 8 + 6, :] = work_ref[t * 3 : t * 3 + 3, :]
+    far_ids_ref[0:1, :] = sums_ref[36:37, :]
+    far_ids_ref[1:4, :] = sums_ref[24 + WIDE_STEP * 3 : 27 + WIDE_STEP * 3, :]
+    far_ids_ref[4:5, :] = sums_ref[37:38, :]
+    far_ids_ref[5:6, :] = work_ref[12:13, :]
+    far_ids_ref[6:9, :] = work_ref[WIDE_STEP * 3 : WIDE_STEP * 3 + 3, :]
+    far_ids_ref[9:10, :] = work_ref[13:14, :]
     means = cell_means(sums_ref, from_odd_ref, from_even_ref, work_ref, tot_ref)
     axes = cell_axes(ids_ref[0:8, :])
     turn = turned(axes, means)
@@ -277,8 +315,8 @@
     fill_messages_y(new_ref, odd_ref, even_ref)
 
 
-def joint_kernel(shifts_ref, code_ref, *out_refs):
-    for t, out_ref in zip((1, 2), out_refs):
+def joint_kernel(shifts_ref, code_ref, first_ref, second_ref, odd_ref, even_ref):
+    for t, out_ref in ((1, first_ref), (2, second_ref)):
         out_ref[...] = jnp.zeros_like(out_ref)
         for col, lanes in blocks():
 
@@ -298,21 +336,36 @@
             acc = lax.fori_loop(0, 16, body, (jnp.zeros((8, 128), F32),) * 27, unroll=2)
             for at in range(27):
                 out_ref[col * 27 + at : col * 27 + at + 1, lanes] = jnp.sum(acc[at], axis=0, keepdims=True)
+    odd = is_odd("gy")
+    nested = nested_hops(WIDE_STEP, shifts_ref)
+    for x in range(3):
+        for y in range(2):
+            for z in range(3):
+                hopped = nested[1] if y else 2
+                left = second_ref[x * 9 + y * 3 + z : x * 9 + y * 3 + z + 1, :] - second_ref[pl.ds(x * 9 + hopped * 3 + z, 1), :]
+                right = second_ref[pl.ds(27 + x * 9 + hopped * 3 + z, 1), :]
+                row = x * 6 + y * 3 + z
+                odd_ref[row : row + 1, :] = jnp.where(odd, right, left)
+                even_ref[row : row + 1, :] = jnp.where(odd, left, right)
 
 
 def turn_kernel(step, *refs):
-    sums = step < ITERS - 1
     if step == 1:
         shifts_ref, code_ref, ids_ref, vel_ref, *refs = refs
     else:
         shifts_ref, code_ref, ids_ref, vel_ref, last_ref, *refs = refs
-    if sums:
+    if step == WIDE_STEP:
+        far_ids_ref, joint_odd_ref, joint_even_ref, now_ref, out_ref, axes_ref, sums_ref, odd_ref, even_ref, table_ref, mom_ref = refs
+        for comp, axis in enumerate(cell_axes(far_ids_ref[...])):
+            axes_ref[comp] = axis
+    elif step < ITERS - 1:
         out_ref, axes_ref, mom_ref, table_ref = refs
     else:
         out_ref, axes_ref, table_ref = refs
     axes = cell_axes(ids_ref[step * 8 : step * 8 + 8, :])
-    for comp in range(3):
-        axes_ref[comp] = axes[comp]
+    if step != WIDE_STEP:
+        for comp in range(3):
+            axes_ref[comp] = axes[comp]
     table_ref[...] = jnp.zeros_like(table_ref)
     store_cells(table_ref, axes)
     for col, lanes in blocks():
@@ -330,45 +383,97 @@
                 out_ref[comp * 2 + col, rows, lanes] = turn[comp]
 
         over_slots(body)
-    if sums:
+    if step < ITERS - 1:
         mom_ref[...] = jnp.zeros_like(mom_ref)
         deposit(out_ref, code_ref, shifts_ref, step + 1, mom_ref, False)
-
-
-def shift_kernel(step, shifts_ref, sums_ref, from_odd_ref, from_even_ref, axes_ref, mom_ref, joint_ref, shift_ref, new_ref, odd_ref, even_ref, work_ref, tot_ref, next_ref):
+    if step == WIDE_STEP:
+        cell_sums(stored_moment(mom_ref), sums_ref)
+        fill_messages_y(now_ref, odd_ref, even_ref, 2)
+        fill_messages_y(sums_ref, odd_ref, even_ref, 1, 16)
+        odd_ref[24:42, :] = joint_odd_ref[...]
+        even_ref[24:42, :] = joint_even_ref[...]
+
+
+def nested_hops(step, shifts_ref):
+    return [jnp.where(shifts_ref[step, dim] <= shifts_ref[step + 1, dim], 1, 2) for dim in range(3)]
+
+
+def corner_differences(shift_ref, cells):
+    parts = {}
+    for corner in range(8):
+        cell = cells[corner >> 2][corner >> 1 & 1]
+        parts[corner] = shift_ref[corner & 1, cell * 8 : cell * 8 + 8, :]
+    for bit in (1, 2, 4):
+        for corner in range(8):
+            if corner & bit:
+                parts[corner] = parts[corner] - parts[corner ^ bit]
+    return parts
+
+
+def shift_moment(joint_ref, first, parts, later, nested, weights=(9, 3, 1)):
+    total = None
+    for now in range(8):
+        at = first
+        for dim, (bit, weight) in enumerate(zip((4, 2, 1), weights)):
+            if now & bit and later & bit:
+                at = at + nested[dim] * weight
+            elif now & bit:
+                at = at + weight
+            elif later & bit:
+                at = at + 2 * weight
+        term = joint_ref[pl.ds(at, 1), :] * parts[now]
+        total = term if total is None else total + term
+    return total
+
+
+def shifts_of(means, axes):
+    turn = turned(axes, means)
+    return [means[comp] - turn[comp] for comp in range(3)] + [jnp.ones_like(means[0])]
+
+
+def shift_kernel(step, shifts_ref, sums_ref, from_odd_ref, from_even_ref, axes_ref, mom_ref, joint_ref, shift_ref, new_ref, *refs):
+    *messages, work_ref, tot_ref, next_ref = refs
     means = cell_means(sums_ref, from_odd_ref, from_even_ref, work_ref, tot_ref)
-    turn = turned([axes_ref[comp] for comp in range(3)], means)
     shift_ref[...] = jnp.zeros_like(shift_ref)
-    ones = jnp.ones((8, 256), F32)
-    store_cells(shift_ref, [means[comp] - turn[comp] for comp in range(3)] + [ones])
-    nested = []
-    for dim in range(3):
-        nested.append(jnp.where(shifts_ref[step, dim] <= shifts_ref[step + 1, dim], 1, 2))
+    store_cells(shift_ref, shifts_of(means, [axes_ref[comp] for comp in range(3)]))
+    nested = nested_hops(step, shifts_ref)
     for col in range(2):
-        parts = {}
-        for corner in range(8):
-            cell = (corner >> 2) * 3 + col + (corner >> 1 & 1)
-            parts[corner] = shift_ref[corner & 1, cell * 8 : cell * 8 + 8, :]
-        for bit in (1, 2, 4):
-            for corner in range(8):
-                if corner & bit:
-                    parts[corner] = parts[corner] - parts[corner ^ bit]
+        parts = corner_differences(shift_ref, ((col, col + 1), (3 + col, 4 + col)))
         for later in range(8):
             row = (col * 8 + later) * 8
-            total = mom_ref[row : row + 8, :]
-            for now in range(8):
-                at = col * 27
-                for dim, (bit, weight) in enumerate(((4, 9), (2, 3), (1, 1))):
-                    if now & bit and later & bit:
-                        at = at + nested[dim] * weight
-                    elif now & bit:
-                        at = at + weight
-                    elif later & bit:
-                        at = at + 2 * weight
-                total = total + joint_ref[pl.ds(at, 1), :] * parts[now]
-            next_ref[row : row + 8, :] = total
+            next_ref[row : row + 8, :] = mom_ref[row : row + 8, :] + shift_moment(joint_ref, col * 27, parts, later, nested)
     cell_sums(stored_moment(next_ref), new_ref)
-    fill_messages_y(new_ref, odd_ref, even_ref)
+    if messages:
+        fill_messages_y(new_ref, *messages)
+
+
+def wide_shift_kernel(step, shifts_ref, sums_ref, from_odd_ref, from_even_ref, axes_ref, turned_ref, joint_ref, y_odd_ref, y_even_ref, shift_ref, new_ref, odd_ref, even_ref, work_ref, tot_ref, next_ref, far_ref, side_ref):
+    means = cell_means(sums_ref, from_odd_ref, from_even_ref, work_ref, tot_ref, 5)
+    far_ref[...] = jnp.zeros_like(far_ref)
+    store_cells(far_ref, shifts_of(means, [axes_ref[comp] for comp in range(3)]), 10)
+    for hop in range(2):
+        for side in range(2):
+            shift_ref[side, hop * 24 : hop * 24 + 24, :] = far_ref[side, hop * 40 + 8 : hop * 40 + 32, :]
+    nested = nested_hops(step, shifts_ref)
+    for col in range(2):
+        parts = corner_differences(far_ref, ((col + 1, col + 2), (col + 6, col + 7)))
+        for later in range(8):
+            row = (col * 8 + later) * 8
+            next_ref[row : row + 8, :] = shift_moment(joint_ref, col * 27, parts, later, nested)
+    cell_sums(stored_moment(next_ref), new_ref)
+    new_ref[...] = new_ref[...] + turned_ref[...]
+    for side, came in enumerate(from_sides("gy", y_odd_ref[16:42, :], y_even_ref[16:42, :])):
+        side_ref[...] = came
+        first = side * 3
+        parts = corner_differences(far_ref, ((first, first + 1), (first + 5, first + 6)))
+        quads = []
+        for moment in (0, 4):
+            up = shift_moment(side_ref, 8, parts, moment + 1, nested, (6, 3, 1))
+            quads.append(shift_moment(side_ref, 8, parts, moment, nested, (6, 3, 1)) - up + pltpu.roll(up, 1, 1))
+        for hop, piece in enumerate((quads[0] - quads[1], quads[1])):
+            rows = slice(hop * 12 + side * 8, hop * 12 + side * 8 + 4)
+            new_ref[rows, :] = new_ref[rows, :] + piece[0:4, :] + side_ref[hop * 4 : hop * 4 + 4, :]
+    fill_messages_x(new_ref, 12, odd_ref, even_ref)
 
 
 def last_kernel(shifts_ref, code_ref, vel_ref, sums_ref, from_odd_ref, from_even_ref, axes_ref, out_ref, means_ref, work_ref, tot_ref, table_ref, end_ref):
@@ -439,43 +544,64 @@
     small = [room(24, 256), room(4, 8, 256)]
 
     vel, code, sums, odd, even = call(
-        start_kernel, "start", [HBM] * 5, [vel_shape, code_shape, rows(24), rows(12), rows(12)],
+        start_kernel, "start", [HBM] * 5, [vel_shape, code_shape, rows(24), rows(13), rows(13)],
         [moments, pltpu.VMEM((6, 256, 128), jnp.bfloat16), pltpu.VMEM((2, 256, 128), jnp.int32), pltpu.VMEM((2, 256), jnp.int32), pltpu.VMEM((ITERS, 2, 256), jnp.int32), pltpu.SMEM((ITERS, 3), jnp.int32), pltpu.SemaphoreType.DMA((11,))],
     )(*(pltpu.with_memory_space_constraint(x, pltpu.HBM) for x in (shifts, vel_in, code_in, occ, ids_in)))
 
     from_odd, from_even = swap(odd, even, "gy")
     sums, odd, even = call(
-        functools.partial(middle_kernel, True), "middle0", [VMEM] * 4, [rows(36), rows(24), rows(24)], [],
+        functools.partial(middle_kernel, True), "middle0", [VMEM] * 4, [rows(38), rows(26), rows(26)], [],
     )(sums, from_odd, from_even, ids_in)
     from_odd, from_even = swap(odd, even, "gx")
-    joints = call(joint_kernel, "joint", [SMEM, VMEM], [rows(56), rows(56)], [], BYTES)(shifts, code)
-    vel, ids, sums, odd, even = call(
-        first_kernel, "first", [SMEM] + [VMEM] * 6, [vel_shape, rows(32), rows(24), rows(8), rows(8)], [moments, *small, table],
+    *joints, joint_odd, joint_even = call(
+        joint_kernel, "joint", [SMEM, VMEM], [rows(56), rows(56), rows(18), rows(18)], [], BYTES
+    )(shifts, code)
+    vel, ids, far_ids, sums, odd, even = call(
+        first_kernel, "first", [SMEM] + [VMEM] * 6, [vel_shape, rows(32), rows(16), rows(24), rows(8), rows(8)], [moments, *small, table],
     )(shifts, vel, code, sums, from_odd, from_even, joints[0])
 
     shift = None
     for step in range(1, ITERS):
-        last = step == ITERS - 1
-        from_odd, from_even = swap(odd, even, "gy")
-        sums, odd, even = call(
-            functools.partial(middle_kernel, False), f"middle{step}", [VMEM] * 3, [rows(24), rows(12), rows(12)], [],
-        )(sums, from_odd, from_even)
+        last, wide, after_wide = step == ITERS - 1, step == WIDE_STEP, step == WIDE_STEP + 1
+        args = [shifts, code, ids, vel] + ([] if step == 1 else [shift])
+        shapes, scratch = [vel_shape, axes_shape], [table]
+        if wide:
+            args += [far_ids, joint_odd, joint_even, sums]
+            shapes = [vel_shape, ((3, 16, 256), F32), rows(24), rows(42), rows(42)]
+            scratch = [table, moments]
+        elif not last:
+            shapes.append(rows(128))
+        vel, axes, *more = call(
+            functools.partial(turn_kernel, step), f"turn{step}", [SMEM] + [VMEM] * (len(args) - 1), shapes, scratch, BYTES,
+        )(*args)
+        if wide:
+            own, odd, even = more
+        if not after_wide:
+            y_odd, y_even = swap(odd, even, "gy")
+            sums, odd, even = call(
+                wide_middle_kernel if wide else functools.partial(middle_kernel, False), f"middle{step}", [VMEM] * 3,
+                [rows(40), rows(20), rows(20)] if wide else [rows(24), rows(12), rows(12)], [],
+            )(sums, y_odd, y_even)
         from_odd, from_even = swap(odd, even, "gx")
-        args = [shifts, code, ids, vel] + ([] if step == 1 else [shift])
-        vel, axes, *moms = call(
-            functools.partial(turn_kernel, step), f"turn{step}", [SMEM] + [VMEM] * (len(args) - 1),
-            [vel_shape, axes_shape] + ([] if last else [rows(128)]), [table], BYTES,
-        )(*args)
         if last:
             out, out_means = call(
                 last_kernel, "last", [SMEM] + [VMEM] * 6, [((6, 256, 128), jnp.bfloat16), ((3, 2, 256), F32)],
                 [*small, table, room(6, 128, 256)],
             )(shifts, code, vel, sums, from_odd, from_even, axes)
+        elif wide:
+            shift, sums, odd, even = call(
+                functools.partial(wide_shift_kernel, step), f"shift{step}", [SMEM] + [VMEM] * 8,
+                [table_shape, rows(24), rows(12), rows(12)],
+                [room(40, 256), room(4, 16, 256), moments, room(2, 80, 256), room(26, 256)],
+            )(shifts, sums, from_odd, from_even, axes, own, joints[step - 1], y_odd, y_even)
         else:
-            shift, sums, odd, even = call(
+            messages = [] if step + 1 == WIDE_STEP else [rows(8), rows(8)]
+            shift, sums, *pair = call(
                 functools.partial(shift_kernel, step), f"shift{step}", [SMEM] + [VMEM] * 6,
-                [table_shape, rows(24), rows(8), rows(8)], [*small, moments],
-            )(shifts, sums, from_odd, from_even, axes, moms[0], joints[step - 1])
+                [table_shape, rows(24), *messages], [*small, moments],
+            )(shifts, sums, from_odd, from_even, axes, more[0], joints[step - 1])
+            if pair:
+                odd, even = pair
     return out.reshape(velocity.shape), out_means.reshape(3, *occupancy.shape)
 
 

time: 92 us -> 87.1 us (0.947)
  the two profiles are of different devices: /device:TPU:1 before, /device:TPU:32 now
where the time goes in v3:
time: 87.1 us; the launch traced here: 86.6 us
  starting transfers between devices  49 us (56%)
  waiting for transfers between devices  19.9 us (23%)
  Pallas kernels  16.9 us (19%)
    ppermute x7, starting transfers between devices, swap(): from_odd = lax.ppermute(odd, axis, odds)  34.8 us
    ppermute x7, waiting for transfers between devices, swap(): from_odd = lax.ppermute(odd, axis, odds)  14.3 us
    ppermute x7, starting transfers between devices, swap(): from_even = lax.ppermute(even, axis, evens)  14.2 us
    ppermute x7, waiting for transfers between devices, swap(): from_even = lax.ppermute(even, axis, evens)  5.57 us
    pallas_call x3, Pallas kernels, on_device(): call(functools.partial(turn_kernel, step), f'turn{step}', [SMEM] + [VMEM]...  5.2 us
    pallas_call x1, Pallas kernels, on_device(): call(start_kernel, 'start', [HBM] * 5, [vel_shape, code_shape, rows(24),...  2.86 us
    pallas_call x1, Pallas kernels, on_device(): call(joint_kernel, 'joint', [SMEM, VMEM], [rows(56), rows(56), rows(18),...  2.62 us
    pallas_call x1, Pallas kernels, on_device(): call(first_kernel, 'first', [SMEM] + [VMEM] * 6, [vel_shape, rows(32), ro...  2.35 us
  transfers between devices with their start and end apart: 14, of which 8 were waited for; matrix products, arithmetic and copies ran while one was open for 0% of the time, Pallas kernels for 7%

profile of v3, /device:TPU:32, one launch (start us, length us, event | category | flops | bytes accessed | tf_op | source)
XLA Modules:
  0.0 86.6 jit_solution(4635795637945676921)
XLA Ops:
  0.6 0.0 copy-start.1
  0.6 2.9 %start.1 = (f32[6,128,256]{2,1,0:T(8,128)S(1)}, s32[2,128,256]{2,1,0:T(8,128)S(1)}, f32[24,256]{1,0:T(8,128)S(1)}, f32[13,256]{1,0:T(8,128)S(1)}, f32[13,256]{1,0:T(8,128)S(1)}) custom-call(s32[4,3]{1,0:T(4,128)} %shifts_ref.9, bf16[6,256,128]{2,1,0:T(8,128)(2,1)} %bitcast.12, s32[2,256,128]{2,1,0:T(8,128)} %bitcast.13, s32[2,256]{1,0:T(2,128)} %bitcast.14, ...), custom_call_target="tpu_custom_call" | custom-call | tf_op jit(solution)/shard_map/start/pallas_call | solution.py:546
  3.5 3.6 %collective-permute-start = (f32[13,256]{1,0:T(8,128)S(1)}, f32[13,256]{1,0:T(8,128)S(1)}, u32[]{:S(2)}, u32[]{:S(2)}) collective-permute-start(f32[13,256]{1,0:T(8,128)S(1)} %get-tuple-element.47), channel_id=1, source_target_pairs={{0,31},{1,2},{2,1},{3,4},{4,3},{5,6},{6,5},{7,8},{8,7},{9,10},{10,... | collective-permute-start | bytes 39944 | tf_op jit(solution)/shard_map/ppermute | solution.py:525
  7.1 2.7 %collective-permute-start.1 = (f32[13,256]{1,0:T(8,128)S(1)}, f32[13,256]{1,0:T(8,128)S(1)}, u32[]{:S(2)}, u32[]{:S(2)}) collective-permute-start(f32[13,256]{1,0:T(8,128)S(1)} %get-tuple-element.48), channel_id=1, source_target_pairs={{0,1},{1,0},{2,3},{3,2},{4,5},{5,4},{6,7},{7,6},{8,9},{9,8},{10,11... | collective-permute-start | bytes 39944 | tf_op jit(solution)/shard_map/ppermute | solution.py:524
  9.8 0.8 collective-permute-done.refs_1_
  10.7 0.0 collective-permute-done.1.refs_2_
  10.7 0.0 copy-done.1
  10.7 0.0 copy-start
  10.7 13.1 %collective-permute-start.2 = (f32[26,256]{1,0:T(8,128)S(1)}, f32[26,256]{1,0:T(8,128)S(1)}, u32[]{:S(2)}, u32[]{:S(2)}) collective-permute-start(f32[26,256]{1,0:T(8,128)S(1)} %get-tuple-element.50), channel_id=1, source_target_pairs={{0,480},{32,64},{64,32},{96,128},{128,96},{160,192},{192,160},{224... | collective-permute-start | bytes 79880 | tf_op jit(solution)/shard_map/ppermute | solution.py:525
  23.9 1.9 %collective-permute-start.3 = (f32[26,256]{1,0:T(8,128)S(1)}, f32[26,256]{1,0:T(8,128)S(1)}, u32[]{:S(2)}, u32[]{:S(2)}) collective-permute-start(f32[26,256]{1,0:T(8,128)S(1)} %get-tuple-element.51), channel_id=1, source_target_pairs={{0,32},{32,0},{64,96},{96,64},{128,160},{160,128},{192,224},{224,1... | collective-permute-start | bytes 79880 | tf_op jit(solution)/shard_map/ppermute | solution.py:524
  25.8 0.0 copy-done
  25.8 2.6 %joint.1 = (f32[56,256]{1,0:T(8,128)S(1)}, f32[56,256]{1,0:T(8,128)S(1)}, f32[18,256]{1,0:T(8,128)S(1)}, f32[18,256]{1,0:T(8,128)S(1)}) custom-call(s32[4,3]{1,0:T(4,128)S(1)} %copy-done, s32[2,128,256]{2,1,0:T(8,128)S(1)} %get-tuple-element.44.code_ref.refs_1_), custom_call_target="tpu_custom_call" | custom-call | bytes 8000000 | tf_op jit(solution)/shard_map/joint/pallas_call | solution.py:556
  28.4 0.0 collective-permute-done.2.from_odd_ref
  28.4 2.1 %collective-permute-done.3.from_even_ref = f32[26,256]{1,0:T(8,128)S(1)} collective-permute-done((f32[26,256]{1,0:T(8,128)S(1)}, f32[26,256]{1,0:T(8,128)S(1)}, u32[]{:S(2)}, u32[]{:S(2)}) %collective-permute-start.3) | collective-permute-done | bytes 26656 | tf_op jit(solution)/shard_map/ppermute | solution.py:524
  30.6 2.3 %first.1 = (f32[6,128,256]{2,1,0:T(8,128)S(1)}, f32[32,256]{1,0:T(8,128)S(1)}, f32[16,256]{1,0:T(8,128)S(1)}, f32[24,256]{1,0:T(8,128)S(1)}, f32[8,256]{1,0:T(8,128)S(1)}, /*index=5*/f32[8,256]{1,0:T(8,128)S(1)}) custom-call(s32[4,3]{1,0:T(4,128)S(1)} %copy-done, f32[6,128,256]{2,1,0:T(8,128)S(1)} %get-tuple-element.45.vel_ref, ...), custom_call_target="tpu_custom_call" | custom-call | tf_op jit(solution)/shard_map/first/pallas_call | solution.py:559
  32.9 2.2 %collective-permute-start.4 = (f32[8,256]{1,0:T(8,128)S(1)}, f32[8,256]{1,0:T(8,128)S(1)}, u32[]{:S(2)}, u32[]{:S(2)}) collective-permute-start(f32[8,256]{1,0:T(8,128)S(1)} %get-tuple-element.57), channel_id=1, source_target_pairs={{0,31},{1,2},{2,1},{3,4},{4,3},{5,6},{6,5},{7,8},{8,7},{9,10},{10,... | collective-permute-start | bytes 24584 | tf_op jit(solution)/shard_map/ppermute | solution.py:525
  35.1 1.9 %collective-permute-start.5 = (f32[8,256]{1,0:T(8,128)S(1)}, f32[8,256]{1,0:T(8,128)S(1)}, u32[]{:S(2)}, u32[]{:S(2)}) collective-permute-start(f32[8,256]{1,0:T(8,128)S(1)} %get-tuple-element.58), channel_id=1, source_target_pairs={{0,1},{1,0},{2,3},{3,2},{4,5},{5,4},{6,7},{7,6},{8,9},{9,8},{10,11... | collective-permute-start | bytes 24584 | tf_op jit(solution)/shard_map/ppermute | solution.py:524
  37.0 3.0 %collective-permute-done.4.refs_1_ = f32[8,256]{1,0:T(8,128)S(1)} collective-permute-done((f32[8,256]{1,0:T(8,128)S(1)}, f32[8,256]{1,0:T(8,128)S(1)}, u32[]{:S(2)}, u32[]{:S(2)}) %collective-permute-start.4) | collective-permute-done | bytes 8224 | tf_op jit(solution)/shard_map/ppermute | solution.py:525
  40.0 0.0 collective-permute-done.5.refs_2_
  40.0 3.3 %collective-permute-start.6 = (f32[12,256]{1,0:T(8,128)S(1)}, f32[12,256]{1,0:T(8,128)S(1)}, u32[]{:S(2)}, u32[]{:S(2)}) collective-permute-start(f32[12,256]{1,0:T(8,128)S(1)} %get-tuple-element.60), channel_id=1, source_target_pairs={{0,480},{32,64},{64,32},{96,128},{128,96},{160,192},{192,160},{224... | collective-permute-start | bytes 36872 | tf_op jit(solution)/shard_map/ppermute | solution.py:525
  43.4 1.9 %collective-permute-start.7 = (f32[12,256]{1,0:T(8,128)S(1)}, f32[12,256]{1,0:T(8,128)S(1)}, u32[]{:S(2)}, u32[]{:S(2)}) collective-permute-start(f32[12,256]{1,0:T(8,128)S(1)} %get-tuple-element.61), channel_id=1, source_target_pairs={{0,32},{32,0},{64,96},{96,64},{128,160},{160,128},{192,224},{224,1... | collective-permute-start | bytes 36872 | tf_op jit(solution)/shard_map/ppermute | solution.py:524
  45.3 1.6 %turn1.1 = (f32[6,128,256]{2,1,0:T(8,128)S(1)}, f32[3,8,256]{2,1,0:T(8,128)S(1)}, f32[128,256]{1,0:T(8,128)S(1)}) custom-call(s32[4,3]{1,0:T(4,128)S(1)} %copy-done, s32[2,128,256]{2,1,0:T(8,128)S(1)} %get-tuple-element.44.code_ref.refs_1_, f32[32,256]{1,0:T(8,128)S(1)} %get-tuple-element.53.refs_2_, f32[6,128,256]{2,1,0:T(8,128)S(1)} %get-tuple-element.54.refs_3_), custom_call_target="tpu_custom_call" | custom-call | bytes 8000000 | tf_op jit(solution)/shard_map/turn1/pallas_call | solution.py:574
  46.9 2.9 %collective-permute-done.6.from_odd_ref = f32[12,256]{1,0:T(8,128)S(1)} collective-permute-done((f32[12,256]{1,0:T(8,128)S(1)}, f32[12,256]{1,0:T(8,128)S(1)}, u32[]{:S(2)}, u32[]{:S(2)}) %collective-permute-start.6) | collective-permute-done | bytes 12320 | tf_op jit(solution)/shard_map/ppermute | solution.py:525
  49.9 0.0 collective-permute-done.7.from_even_ref
  49.9 0.8 shift1.1
  50.7 2.2 %turn2.1 = (f32[6,128,256]{2,1,0:T(8,128)S(1)}, f32[3,16,256]{2,1,0:T(8,128)S(1)}, f32[24,256]{1,0:T(8,128)S(1)}, f32[42,256]{1,0:T(8,128)S(1)}, f32[42,256]{1,0:T(8,128)S(1)}) custom-call(s32[4,3]{1,0:T(4,128)S(1)} %copy-done, s32[2,128,256]{2,1,0:T(8,128)S(1)} %get-tuple-element.44.code_ref.refs_1_, f32[32,256]{1,0:T(8,128)S(1)} %get-tuple-element.53.refs_2_, ...), custom_call_target="tpu_custom_call" | custom-call | bytes 8000000 | tf_op jit(solution)/shard_map/turn2/pallas_call | solution.py:574
  52.9 2.5 %collective-permute-start.8 = (f32[42,256]{1,0:T(8,128)S(1)}, f32[42,256]{1,0:T(8,128)S(1)}, u32[]{:S(2)}, u32[]{:S(2)}) collective-permute-start(f32[42,256]{1,0:T(8,128)S(1)} %get-tuple-element.70), channel_id=1, source_target_pairs={{0,31},{1,2},{2,1},{3,4},{4,3},{5,6},{6,5},{7,8},{8,7},{9,10},{10,... | collective-permute-start | bytes 129032 | tf_op jit(solution)/shard_map/ppermute | solution.py:525
  55.4 1.9 %collective-permute-start.9 = (f32[42,256]{1,0:T(8,128)S(1)}, f32[42,256]{1,0:T(8,128)S(1)}, u32[]{:S(2)}, u32[]{:S(2)}) collective-permute-start(f32[42,256]{1,0:T(8,128)S(1)} %get-tuple-element.71), channel_id=1, source_target_pairs={{0,1},{1,0},{2,3},{3,2},{4,5},{5,4},{6,7},{7,6},{8,9},{9,8},{10,11... | collective-permute-start | bytes 129032 | tf_op jit(solution)/shard_map/ppermute | solution.py:524
  57.4 3.1 %collective-permute-done.8.from_odd_ref.y_odd_ref = f32[42,256]{1,0:T(8,128)S(1)} collective-permute-done((f32[42,256]{1,0:T(8,128)S(1)}, f32[42,256]{1,0:T(8,128)S(1)}, u32[]{:S(2)}, u32[]{:S(2)}) %collective-permute-start.8) | collective-permute-done | bytes 43040 | tf_op jit(solution)/shard_map/ppermute | solution.py:525
  60.4 0.0 collective-permute-done.9.from_even_ref.y_even_ref
  60.5 6.7 %collective-permute-start.10 = (f32[20,256]{1,0:T(8,128)S(1)}, f32[20,256]{1,0:T(8,128)S(1)}, u32[]{:S(2)}, u32[]{:S(2)}) collective-permute-start(f32[20,256]{1,0:T(8,128)S(1)} %get-tuple-element.73), channel_id=1, source_target_pairs={{0,480},{32,64},{64,32},{96,128},{128,96},{160,192},{192,160},{224... | collective-permute-start | bytes 61448 | tf_op jit(solution)/shard_map/ppermute | solution.py:525
  67.2 1.9 %collective-permute-start.11 = (f32[20,256]{1,0:T(8,128)S(1)}, f32[20,256]{1,0:T(8,128)S(1)}, u32[]{:S(2)}, u32[]{:S(2)}) collective-permute-start(f32[20,256]{1,0:T(8,128)S(1)} %get-tuple-element.74), channel_id=1, source_target_pairs={{0,32},{32,0},{64,96},{96,64},{128,160},{160,128},{192,224},{224,1... | collective-permute-start | bytes 61448 | tf_op jit(solution)/shard_map/ppermute | solution.py:524
  69.1 1.3 %collective-permute-done.10.from_odd_ref = f32[20,256]{1,0:T(8,128)S(1)} collective-permute-done((f32[20,256]{1,0:T(8,128)S(1)}, f32[20,256]{1,0:T(8,128)S(1)}, u32[]{:S(2)}, u32[]{:S(2)}) %collective-permute-start.10) | collective-permute-done | bytes 20512 | tf_op jit(solution)/shard_map/ppermute | solution.py:525
  70.4 3.4 %collective-permute-done.11.from_even_ref = f32[20,256]{1,0:T(8,128)S(1)} collective-permute-done((f32[20,256]{1,0:T(8,128)S(1)}, f32[20,256]{1,0:T(8,128)S(1)}, u32[]{:S(2)}, u32[]{:S(2)}) %collective-permute-start.11) | collective-permute-done | bytes 20512 | tf_op jit(solution)/shard_map/ppermute | solution.py:524
  73.8 0.9 %shift2.1 = (f32[2,48,256]{2,1,0:T(8,128)S(1)}, f32[24,256]{1,0:T(8,128)S(1)}, f32[12,256]{1,0:T(8,128)S(1)}, f32[12,256]{1,0:T(8,128)S(1)}) custom-call(s32[4,3]{1,0:T(4,128)S(1)} %copy-done, f32[40,256]{1,0:T(8,128)S(1)} %get-tuple-element.72.sums_ref, f32[20,256]{1,0:T(8,128)S(1)} %collective-permute-done.10.from_odd_ref, ...), custom_call_target="tpu_custom_call" | custom-call | tf_op jit(solution)/shard_map/shift2/pallas_call | solution.py:592
  74.7 3.3 %collective-permute-start.12 = (f32[12,256]{1,0:T(8,128)S(1)}, f32[12,256]{1,0:T(8,128)S(1)}, u32[]{:S(2)}, u32[]{:S(2)}) collective-permute-start(f32[12,256]{1,0:T(8,128)S(1)} %get-tuple-element.81), channel_id=1, source_target_pairs={{0,480},{32,64},{64,32},{96,128},{128,96},{160,192},{192,160},{224... | collective-permute-start | bytes 36872 | tf_op jit(solution)/shard_map/ppermute | solution.py:525
  78.1 1.9 %collective-permute-start.13 = (f32[12,256]{1,0:T(8,128)S(1)}, f32[12,256]{1,0:T(8,128)S(1)}, u32[]{:S(2)}, u32[]{:S(2)}) collective-permute-start(f32[12,256]{1,0:T(8,128)S(1)} %get-tuple-element.82), channel_id=1, source_target_pairs={{0,32},{32,0},{64,96},{96,64},{128,160},{160,128},{192,224},{224,1... | collective-permute-start | bytes 36872 | tf_op jit(solution)/shard_map/ppermute | solution.py:524
  80.0 1.4 %turn3.1 = (f32[6,128,256]{2,1,0:T(8,128)S(1)}, f32[3,8,256]{2,1,0:T(8,128)S(1)}) custom-call(s32[4,3]{1,0:T(4,128)S(1)} %copy-done, s32[2,128,256]{2,1,0:T(8,128)S(1)} %get-tuple-element.44.code_ref.refs_1_, f32[32,256]{1,0:T(8,128)S(1)} %get-tuple-element.53.refs_2_, f32[6,128,256]{2,1,0:T(8,128)S(1)} %get-tuple-element.69.refs_3_, ...), custom_call_target="tpu_custom_call" | custom-call | bytes 8000000 | tf_op jit(solution)/shard_map/turn3/pallas_call | solution.py:574
  81.4 3.2 %collective-permute-done.12.from_odd_ref = f32[12,256]{1,0:T(8,128)S(1)} collective-permute-done((f32[12,256]{1,0:T(8,128)S(1)}, f32[12,256]{1,0:T(8,128)S(1)}, u32[]{:S(2)}, u32[]{:S(2)}) %collective-permute-start.12) | collective-permute-done | bytes 12320 | tf_op jit(solution)/shard_map/ppermute | solution.py:525
  84.6 0.0 collective-permute-done.13.from_even_ref
  84.6 2.0 %last.1 = (bf16[6,256,128]{2,1,0:T(8,128)(2,1)}, f32[3,2,256]{2,1,0:T(2,128)}) custom-call(s32[4,3]{1,0:T(4,128)S(1)} %copy-done, s32[2,128,256]{2,1,0:T(8,128)S(1)} %get-tuple-element.44.code_ref.refs_1_, f32[6,128,256]{2,1,0:T(8,128)S(1)} %get-tuple-element.79.vel_ref, f32[24,256]{1,0:T(8,128)S(1)} %get-tuple-element.80.sums_ref, ...), custom_call_target="tpu_custom_call" | custom-call | tf_op jit(solution)/shard_map/last/pallas_call | solution.py:587
  (3 shorter events, 0.1 us)
Async XLA Ops:
  0.6 10.0 %copy-start.1 = (s32[4,1,2,256]{3,2,1,0:T(2,128)S(1)}, s32[4,1,2,256]{3,2,1,0:T(2,128)}, u32[]{:S(2)}) copy-start(s32[4,1,2,256]{3,2,1,0:T(2,128)} %param.9) | copy-start | bytes 24580
  3.5 7.2 %collective-permute-start = (f32[13,256]{1,0:T(8,128)S(1)}, f32[13,256]{1,0:T(8,128)S(1)}, u32[]{:S(2)}, u32[]{:S(2)}) collective-permute-start(f32[13,256]{1,0:T(8,128)S(1)} %get-tuple-element.47), channel_id=1, source_target_pairs={{0,31},{1,2},{2,1},{3,4},{4,3},{5,6},{6,5},{7,8},{8,7},{9,10},{10,... | collective-permute-start | bytes 39944 | tf_op jit(solution)/shard_map/ppermute | solution.py:525
  7.1 3.6 %collective-permute-start.1 = (f32[13,256]{1,0:T(8,128)S(1)}, f32[13,256]{1,0:T(8,128)S(1)}, u32[]{:S(2)}, u32[]{:S(2)}) collective-permute-start(f32[13,256]{1,0:T(8,128)S(1)} %get-tuple-element.48), channel_id=1, source_target_pairs={{0,1},{1,0},{2,3},{3,2},{4,5},{5,4},{6,7},{7,6},{8,9},{9,8},{10,11... | collective-permute-start | bytes 39944 | tf_op jit(solution)/shard_map/ppermute | solution.py:524
  10.7 15.1 %copy-start = (s32[4,3]{1,0:T(4,128)S(1)}, s32[4,3]{1,0:T(4,128)}, u32[]{:S(2)}) copy-start(s32[4,3]{1,0:T(4,128)} %shifts_ref.9) | copy-start | bytes 148
  10.7 17.7 %collective-permute-start.2 = (f32[26,256]{1,0:T(8,128)S(1)}, f32[26,256]{1,0:T(8,128)S(1)}, u32[]{:S(2)}, u32[]{:S(2)}) collective-permute-start(f32[26,256]{1,0:T(8,128)S(1)} %get-tuple-element.50), channel_id=1, source_target_pairs={{0,480},{32,64},{64,32},{96,128},{128,96},{160,192},{192,160},{224... | collective-permute-start | bytes 79880 | tf_op jit(solution)/shard_map/ppermute | solution.py:525
  23.9 6.7 %collective-permute-start.3 = (f32[26,256]{1,0:T(8,128)S(1)}, f32[26,256]{1,0:T(8,128)S(1)}, u32[]{:S(2)}, u32[]{:S(2)}) collective-permute-start(f32[26,256]{1,0:T(8,128)S(1)} %get-tuple-element.51), channel_id=1, source_target_pairs={{0,32},{32,0},{64,96},{96,64},{128,160},{160,128},{192,224},{224,1... | collective-permute-start | bytes 79880 | tf_op jit(solution)/shard_map/ppermute | solution.py:524
  32.9 7.1 %collective-permute-start.4 = (f32[8,256]{1,0:T(8,128)S(1)}, f32[8,256]{1,0:T(8,128)S(1)}, u32[]{:S(2)}, u32[]{:S(2)}) collective-permute-start(f32[8,256]{1,0:T(8,128)S(1)} %get-tuple-element.57), channel_id=1, source_target_pairs={{0,31},{1,2},{2,1},{3,4},{4,3},{5,6},{6,5},{7,8},{8,7},{9,10},{10,... | collective-permute-start | bytes 24584 | tf_op jit(solution)/shard_map/ppermute | solution.py:525
  35.1 4.9 %collective-permute-start.5 = (f32[8,256]{1,0:T(8,128)S(1)}, f32[8,256]{1,0:T(8,128)S(1)}, u32[]{:S(2)}, u32[]{:S(2)}) collective-permute-start(f32[8,256]{1,0:T(8,128)S(1)} %get-tuple-element.58), channel_id=1, source_target_pairs={{0,1},{1,0},{2,3},{3,2},{4,5},{5,4},{6,7},{7,6},{8,9},{9,8},{10,11... | collective-permute-start | bytes 24584 | tf_op jit(solution)/shard_map/ppermute | solution.py:524
  40.0 9.9 %collective-permute-start.6 = (f32[12,256]{1,0:T(8,128)S(1)}, f32[12,256]{1,0:T(8,128)S(1)}, u32[]{:S(2)}, u32[]{:S(2)}) collective-permute-start(f32[12,256]{1,0:T(8,128)S(1)} %get-tuple-element.60), channel_id=1, source_target_pairs={{0,480},{32,64},{64,32},{96,128},{128,96},{160,192},{192,160},{224... | collective-permute-start | bytes 36872 | tf_op jit(solution)/shard_map/ppermute | solution.py:525
  43.4 6.5 %collective-permute-start.7 = (f32[12,256]{1,0:T(8,128)S(1)}, f32[12,256]{1,0:T(8,128)S(1)}, u32[]{:S(2)}, u32[]{:S(2)}) collective-permute-start(f32[12,256]{1,0:T(8,128)S(1)} %get-tuple-element.61), channel_id=1, source_target_pairs={{0,32},{32,0},{64,96},{96,64},{128,160},{160,128},{192,224},{224,1... | collective-permute-start | bytes 36872 | tf_op jit(solution)/shard_map/ppermute | solution.py:524
  52.9 7.5 %collective-permute-start.8 = (f32[42,256]{1,0:T(8,128)S(1)}, f32[42,256]{1,0:T(8,128)S(1)}, u32[]{:S(2)}, u32[]{:S(2)}) collective-permute-start(f32[42,256]{1,0:T(8,128)S(1)} %get-tuple-element.70), channel_id=1, source_target_pairs={{0,31},{1,2},{2,1},{3,4},{4,3},{5,6},{6,5},{7,8},{8,7},{9,10},{10,... | collective-permute-start | bytes 129032 | tf_op jit(solution)/shard_map/ppermute | solution.py:525
  55.4 5.0 %collective-permute-start.9 = (f32[42,256]{1,0:T(8,128)S(1)}, f32[42,256]{1,0:T(8,128)S(1)}, u32[]{:S(2)}, u32[]{:S(2)}) collective-permute-start(f32[42,256]{1,0:T(8,128)S(1)} %get-tuple-element.71), channel_id=1, source_target_pairs={{0,1},{1,0},{2,3},{3,2},{4,5},{5,4},{6,7},{7,6},{8,9},{9,8},{10,11... | collective-permute-start | bytes 129032 | tf_op jit(solution)/shard_map/ppermute | solution.py:524
  60.5 9.9 %collective-permute-start.10 = (f32[20,256]{1,0:T(8,128)S(1)}, f32[20,256]{1,0:T(8,128)S(1)}, u32[]{:S(2)}, u32[]{:S(2)}) collective-permute-start(f32[20,256]{1,0:T(8,128)S(1)} %get-tuple-element.73), channel_id=1, source_target_pairs={{0,480},{32,64},{64,32},{96,128},{128,96},{160,192},{192,160},{224... | collective-permute-start | bytes 61448 | tf_op jit(solution)/shard_map/ppermute | solution.py:525
  67.2 6.6 %collective-permute-start.11 = (f32[20,256]{1,0:T(8,128)S(1)}, f32[20,256]{1,0:T(8,128)S(1)}, u32[]{:S(2)}, u32[]{:S(2)}) collective-permute-start(f32[20,256]{1,0:T(8,128)S(1)} %get-tuple-element.74), channel_id=1, source_target_pairs={{0,32},{32,0},{64,96},{96,64},{128,160},{160,128},{192,224},{224,1... | collective-permute-start | bytes 61448 | tf_op jit(solution)/shard_map/ppermute | solution.py:524
  74.7 9.9 %collective-permute-start.12 = (f32[12,256]{1,0:T(8,128)S(1)}, f32[12,256]{1,0:T(8,128)S(1)}, u32[]{:S(2)}, u32[]{:S(2)}) collective-permute-start(f32[12,256]{1,0:T(8,128)S(1)} %get-tuple-element.81), channel_id=1, source_target_pairs={{0,480},{32,64},{64,32},{96,128},{128,96},{160,192},{192,160},{224... | collective-permute-start | bytes 36872 | tf_op jit(solution)/shard_map/ppermute | solution.py:525
  78.1 6.5 %collective-permute-start.13 = (f32[12,256]{1,0:T(8,128)S(1)}, f32[12,256]{1,0:T(8,128)S(1)}, u32[]{:S(2)}, u32[]{:S(2)}) collective-permute-start(f32[12,256]{1,0:T(8,128)S(1)} %get-tuple-element.82), channel_id=1, source_target_pairs={{0,32},{32,0},{64,96},{96,64},{128,160},{160,128},{192,224},{224,1... | collective-permute-start | bytes 36872 | tf_op jit(solution)/shard_map/ppermute | solution.py:524

commit v4 on v3

--- a/solution.py
+++ b/solution.py
@@ -69,14 +69,14 @@
             mom_ref[row : row + 1, lanes] = jnp.sum(acc[comp * 8 + moment], axis=0, keepdims=True)
 
 
-def blocks():
-    for col in range(2):
+def blocks(cols=(0, 1)):
+    for col in cols:
         for half in range(2):
             yield col, slice(half * 128, half * 128 + 128)
 
 
-def deposit(vel_ref, code_ref, shifts_ref, step, mom_ref, counted):
-    for col, lanes in blocks():
+def deposit(vel_ref, code_ref, shifts_ref, step, mom_ref, counted, cols=(0, 1)):
+    for col, lanes in blocks(cols):
 
         def values(rows, code):
             parts = [vel_ref[comp * 2 + col, rows, lanes] for comp in range(3)]
@@ -144,85 +144,77 @@
     for at in range(6):
         copies.append(pltpu.make_async_copy(vel_hbm.at[at], vel_in_ref.at[at], sems.at[2 + at]))
     fetch_occ.start()
-    for copy in copies:
-        copy.start()
+    for at in (0, 2, 4, 6, 1, 3, 5, 7):
+        copies[at].start()
     fetch_ids.start()
     fetch_shifts.start()
     mom_ref[...] = jnp.zeros_like(mom_ref)
     slot = lax.broadcasted_iota(jnp.int32, (128, 256), 0)
     fetch_occ.wait()
+    fetch_shifts.wait()
     for col in range(2):
         filled = slot < occ_ref[col : col + 1, :]
         copies[col].wait()
         code_ref[col] = jnp.where(filled, code_in_ref[col].T, -1)
-    for comp in range(3):
-        for col in range(2):
+        for comp in range(3):
             at = comp * 2 + col
             copies[2 + at].wait()
-            filled = code_ref[col] >= 0
             vel_ref[at] = jnp.where(filled, vel_in_ref[at].astype(F32).T, 0.0)
+        deposit(vel_ref, code_ref, shifts_ref, 0, mom_ref, True, (col,))
     fetch_ids.wait()
-    fetch_shifts.wait()
     for step in range(ITERS):
-        ids = ids_ref[step, 0:1, :].astype(F32)
-        odd_ref[8 + step : 9 + step, :] = ids
-        even_ref[8 + step : 9 + step, :] = ids
-    far = ids_ref[WIDE_STEP, 1:2, :].astype(F32)
-    odd_ref[12:13, :] = far
-    even_ref[12:13, :] = far
-    deposit(vel_ref, code_ref, shifts_ref, 0, mom_ref, True)
+        ids = ids_ref[step].astype(F32)
+        rows = slice(12 + step * 2, 14 + step * 2)
+        odd_ref[rows, :] = ids
+        even_ref[rows, :] = ids
     cell_sums(stored_moment(mom_ref), sums_ref)
-    fill_messages_y(sums_ref, odd_ref, even_ref)
-
-
-def middle_kernel(first, *refs):
-    if first:
-        sums_ref, from_odd_ref, from_even_ref, ids_ref, out_ref, odd_ref, even_ref = refs
-    else:
-        sums_ref, from_odd_ref, from_even_ref, out_ref, odd_ref, even_ref = refs
-    out_ref[0:24, :] = sums_ref[...]
+    fill_messages_x(sums_ref, 12, odd_ref, even_ref)
+
+
+def add_x(sums_ref, from_odd_ref, from_even_ref, out_ref):
+    by_low, by_high = from_sides("gx", from_odd_ref[0:12, :], from_even_ref[0:12, :])
+    out_ref[0:12, :] = sums_ref[0:12, :] + by_low
+    out_ref[12:24, :] = sums_ref[12:24, :] + by_high
+
+
+def add_y(sums_ref, by_left_ref, by_right_ref, out_ref):
     for hop in range(2):
-        rows = slice(hop * 4, hop * 4 + 4)
-        by_left, by_right = from_sides("gy", from_odd_ref[rows, :], from_even_ref[rows, :])
-        left = slice(hop * 12, hop * 12 + 4)
-        right = slice(hop * 12 + 8, hop * 12 + 12)
-        out_ref[left, :] = out_ref[left, :] + by_left
-        out_ref[right, :] = out_ref[right, :] + by_right
-    fill_messages_x(out_ref, 12, odd_ref, even_ref)
-    if first:
-        for step in range(ITERS):
-            row = 24 + step * 3
-            out_ref[row : row + 2, :] = ids_ref[step].astype(F32)
-            _, by_right = from_sides("gy", from_odd_ref[8 + step : 9 + step, :], from_even_ref[8 + step : 9 + step, :])
-            out_ref[row + 2 : row + 3, :] = by_right
-        by_left, by_right = from_sides("gy", from_odd_ref[12:13, :], from_even_ref[12:13, :])
-        out_ref[36:37, :] = by_left
-        out_ref[37:38, :] = by_right
-        own = out_ref[24:38, :]
-        odd_ref[12:26, :] = own
-        even_ref[12:26, :] = own
-
-
-def wide_middle_kernel(sums_ref, from_odd_ref, from_even_ref, out_ref, odd_ref, even_ref):
-    for hop in range(2):
-        at, own = hop * 20, hop * 12
-        rows = slice(hop * 8, hop * 8 + 8)
-        by_left, by_right = from_sides("gy", from_odd_ref[rows, :], from_even_ref[rows, :])
-        out_ref[at : at + 8, :] = by_left
-        out_ref[at + 12 : at + 20, :] = by_right
+        at, own, rows = hop * 20, hop * 12, slice(hop * 8, hop * 8 + 8)
+        out_ref[at : at + 8, :] = by_left_ref[rows, :]
+        out_ref[at + 12 : at + 20, :] = by_right_ref[rows, :]
         out_ref[at + 8 : at + 12, :] = sums_ref[own + 4 : own + 8, :]
         out_ref[at + 4 : at + 8, :] = out_ref[at + 4 : at + 8, :] + sums_ref[own : own + 4, :]
         out_ref[at + 12 : at + 16, :] = out_ref[at + 12 : at + 16, :] + sums_ref[own + 8 : own + 12, :]
-    fill_messages_x(out_ref, 20, odd_ref, even_ref)
-
-
-def cell_means(sums_ref, from_odd_ref, from_even_ref, work_ref, tot_ref, width=3):
-    size = width * 4
-    by_low, by_high = from_sides("gx", from_odd_ref[0:size, :], from_even_ref[0:size, :])
-    work_ref[0:size, :] = sums_ref[0:size, :] + by_low
-    work_ref[size : 2 * size, :] = sums_ref[size : 2 * size, :] + by_high
+
+
+def first_middle_kernel(sums_ref, from_odd_ref, from_even_ref, ids_ref, ghost_odd_ref, ghost_even_ref, out_ref, both_ref, odd_ref, even_ref):
+    add_x(sums_ref, from_odd_ref, from_even_ref, out_ref)
+    fill_messages_y(out_ref, odd_ref, even_ref, 2)
+    for step in range(ITERS):
+        both_ref[step * 2 : step * 2 + 2, :] = ids_ref[step].astype(F32)
+    _, by_high = from_sides("gx", from_odd_ref[12:20, :], from_even_ref[12:20, :])
+    both_ref[8:16, :] = by_high
+    for ref in (odd_ref, even_ref):
+        for x in range(2):
+            for step in range(ITERS):
+                ref[16 + x * 4 + step : 17 + x * 4 + step, :] = both_ref[x * 8 + step * 2 : x * 8 + step * 2 + 1, :]
+            for k, step in enumerate((0, WIDE_STEP)):
+                ref[24 + x * 2 + k : 25 + x * 2 + k, :] = both_ref[x * 8 + step * 2 + 1 : x * 8 + step * 2 + 2, :]
+    odd_ref[28:100, :] = ghost_odd_ref[...]
+    even_ref[28:100, :] = ghost_even_ref[...]
+
+
+def wide_middle_kernel(sums_ref, from_odd_ref, from_even_ref, turned_ref, joint_odd_ref, joint_even_ref, out_ref, odd_ref, even_ref):
+    add_x(sums_ref, from_odd_ref, from_even_ref, out_ref)
+    fill_messages_y(out_ref, odd_ref, even_ref, 2)
+    fill_messages_y(turned_ref, odd_ref, even_ref, 1, 16)
+    odd_ref[24:42, :] = joint_odd_ref[...]
+    even_ref[24:42, :] = joint_even_ref[...]
+
+
+def cell_means(work_ref, tot_ref, cells=6):
     tot_ref[...] = jnp.zeros_like(tot_ref)
-    for cell in range(2 * width):
+    for cell in range(cells):
         for comp in range(4):
             tot_ref[comp, cell : cell + 1, :] = work_ref[cell * 4 + comp : cell * 4 + comp + 1, :]
     count = jnp.maximum(tot_ref[3], 1.0)
@@ -277,42 +269,104 @@
     lax.fori_loop(0, 128 // CHUNK, run, 0, unroll=128 // CHUNK)
 
 
-def first_kernel(shifts_ref, vel_ref, code_ref, sums_ref, from_odd_ref, from_even_ref, joint_ref, out_ref, ids_ref, far_ids_ref, new_ref, odd_ref, even_ref, mom_ref, work_ref, tot_ref, table_ref):
+def first_kernel(shifts_ref, vel_ref, code_ref, sums_ref, from_odd_ref, from_even_ref, both_ref, out_ref, ids_ref, far_ids_ref, new_ref, odd_ref, even_ref, mom_ref, work_ref, tot_ref, axis_ref, shift_ref, far_ref, turn_ref, left_ref, right_ref):
+    by_left, by_right = from_sides("gy", from_odd_ref[...], from_even_ref[...])
+    left_ref[...] = by_left
+    right_ref[...] = by_right
     ids_ref[...] = jnp.zeros_like(ids_ref)
+    for x in range(2):
+        for t in range(ITERS):
+            row = t * 8 + x * 3
+            ids_ref[row : row + 2, :] = both_ref[x * 8 + t * 2 : x * 8 + t * 2 + 2, :]
+            ids_ref[row + 2 : row + 3, :] = right_ref[16 + x * 4 + t : 17 + x * 4 + t, :]
     far_ids_ref[...] = jnp.zeros_like(far_ids_ref)
-    _, by_high = from_sides("gx", from_odd_ref[12:26, :], from_even_ref[12:26, :])
-    work_ref[0:14, :] = by_high
-    for t in range(ITERS):
-        ids_ref[t * 8 : t * 8 + 3, :] = sums_ref[24 + t * 3 : 27 + t * 3, :]
-        ids_ref[t * 8 + 3 : t * 8 + 6, :] = work_ref[t * 3 : t * 3 + 3, :]
-    far_ids_ref[0:1, :] = sums_ref[36:37, :]
-    far_ids_ref[1:4, :] = sums_ref[24 + WIDE_STEP * 3 : 27 + WIDE_STEP * 3, :]
-    far_ids_ref[4:5, :] = sums_ref[37:38, :]
-    far_ids_ref[5:6, :] = work_ref[12:13, :]
-    far_ids_ref[6:9, :] = work_ref[WIDE_STEP * 3 : WIDE_STEP * 3 + 3, :]
-    far_ids_ref[9:10, :] = work_ref[13:14, :]
-    means = cell_means(sums_ref, from_odd_ref, from_even_ref, work_ref, tot_ref)
-    axes = cell_axes(ids_ref[0:8, :])
-    turn = turned(axes, means)
-    table_ref[...] = jnp.zeros_like(table_ref)
-    store_cells(table_ref, axes + [means[comp] - turn[comp] for comp in range(3)])
+    for k, t in enumerate((0, WIDE_STEP)):
+        for x in range(2):
+            row, outer = k * 16 + x * 5, slice(24 + x * 2 + k, 25 + x * 2 + k)
+            far_ids_ref[row : row + 1, :] = left_ref[outer, :]
+            far_ids_ref[row + 1 : row + 4, :] = ids_ref[t * 8 + x * 3 : t * 8 + x * 3 + 3, :]
+            far_ids_ref[row + 4 : row + 5, :] = right_ref[outer, :]
+    add_y(sums_ref, left_ref, right_ref, work_ref)
+    means = cell_means(work_ref, tot_ref, 10)
+    axes = cell_axes(far_ids_ref[0:16, :])
+    far_ref[...] = jnp.zeros_like(far_ref)
+    store_cells(far_ref, shifts_of(means, axes), 10)
+    for table_ref in (shift_ref, axis_ref, turn_ref):
+        table_ref[...] = jnp.zeros_like(table_ref)
+    own_cells(far_ref, shift_ref)
+    store_cells(axis_ref, cell_axes(ids_ref[0:8, :]))
     for col, lanes in blocks():
 
         def body(rows):
             code = code_ref[col, rows, lanes]
             masks = hop_masks(code, shifts_ref, 0)
             vel = [vel_ref[comp * 2 + col, rows, lanes] for comp in range(3)]
-            turn = turned([pick(table_ref, comp, col, lanes, masks) for comp in range(3)], vel)
+            turn = turned([pick(axis_ref, comp, col, lanes, masks) for comp in range(3)], vel)
             filled = code >= 0
             for comp in range(3):
-                value = turn[comp] + pick(table_ref, 3 + comp, col, lanes, masks)
+                value = turn[comp] + pick(shift_ref, comp, col, lanes, masks)
                 out_ref[comp * 2 + col, rows, lanes] = jnp.where(filled, value, 0.0)
 
         over_slots(body)
     mom_ref[...] = jnp.zeros_like(mom_ref)
     deposit(out_ref, code_ref, shifts_ref, 1, mom_ref, True)
     cell_sums(stored_moment(mom_ref), new_ref)
-    fill_messages_y(new_ref, odd_ref, even_ref)
+    zero = jnp.zeros((16, 256), F32)
+    for k in range(3):
+        unit = [zero + (1.0 if comp == k else 0.0) for comp in range(3)]
+        store_cells(turn_ref.at[k], turned(axes, unit), 10)
+    nested = nested_hops(0, shifts_ref)
+    for side, came_ref in enumerate((left_ref, right_ref)):
+        cells = side_cells(side)
+        sources = [(28, corner_differences(far_ref, cells))]
+        sources += [(46 + k * 18, corner_differences(turn_ref.at[k], cells)) for k in range(3)]
+        add_side(new_ref, side, came_ref, sources, nested)
+    fill_messages_x(new_ref, 12, odd_ref, even_ref)
+
+
+def ghost_kernel(shifts_ref, vel_ref, code_ref, odd_ref, even_ref, left_ref, right_ref):
+    for col, lanes in blocks():
+        side_ref = right_ref if col else left_ref
+
+        def classes(value, now, later):
+            out = []
+            for by_x in (value, jnp.where(now[0], value, 0), jnp.where(later[0], value, 0)):
+                for by_y in (by_x, jnp.where(now[1], by_x, 0)):
+                    out.append(by_y)
+            return out
+
+        def body(comps, counts, i, acc):
+            rows = pl.ds(pl.multiple_of(i * 8, 8), 8)
+            code = code_ref[col, rows, lanes]
+            now, later = hop_masks(code, shifts_ref, 0), hop_masks(code, shifts_ref, 1)
+            kept = later[1] if col else jnp.logical_not(later[1])
+            out = []
+            for comp in comps:
+                for value in classes(jnp.where(kept, vel_ref[comp * 2 + col, rows, lanes], 0.0), now, later):
+                    out += [value, jnp.where(now[2], value, 0.0), jnp.where(later[2], value, 0.0)]
+            if counts:
+                word = jnp.where(now[2], 1 + 256, 1) + jnp.where(later[2], 65536, 0)
+                out += classes(jnp.where(jnp.logical_and(kept, code >= 0), word, 0), now, later)
+            return tuple(a + b for a, b in zip(acc, out))
+
+        zero, none = jnp.zeros((8, 128), F32), jnp.zeros((8, 128), jnp.int32)
+        for comps, counts in (((0, 1), False), ((2,), True)):
+            start = (zero,) * (18 * len(comps)) + ((none,) * 6 if counts else ())
+            acc = lax.fori_loop(0, 16, functools.partial(body, comps, counts), start, unroll=8)
+            for n, comp in enumerate(comps):
+                for at in range(18):
+                    row = 18 + comp * 18 + at
+                    side_ref[row : row + 1, lanes] = jnp.sum(acc[n * 18 + at], axis=0, keepdims=True)
+            if counts:
+                for at in range(6):
+                    word = acc[18 * len(comps) + at]
+                    for z in range(3):
+                        part = lax.shift_right_logical(word, 8 * z) & 255
+                        row = at * 3 + z
+                        side_ref[row : row + 1, lanes] = jnp.sum(part.astype(F32), axis=0, keepdims=True)
+    odd = is_odd("gy")
+    odd_ref[...] = jnp.where(odd, right_ref[...], left_ref[...])
+    even_ref[...] = jnp.where(odd, left_ref[...], right_ref[...])
 
 
 def joint_kernel(shifts_ref, code_ref, first_ref, second_ref, odd_ref, even_ref):
@@ -355,8 +409,8 @@
     else:
         shifts_ref, code_ref, ids_ref, vel_ref, last_ref, *refs = refs
     if step == WIDE_STEP:
-        far_ids_ref, joint_odd_ref, joint_even_ref, now_ref, out_ref, axes_ref, sums_ref, odd_ref, even_ref, table_ref, mom_ref = refs
-        for comp, axis in enumerate(cell_axes(far_ids_ref[...])):
+        far_ids_ref, out_ref, axes_ref, sums_ref, table_ref, mom_ref = refs
+        for comp, axis in enumerate(cell_axes(far_ids_ref[16:32, :])):
             axes_ref[comp] = axis
     elif step < ITERS - 1:
         out_ref, axes_ref, mom_ref, table_ref = refs
@@ -388,10 +442,6 @@
         deposit(out_ref, code_ref, shifts_ref, step + 1, mom_ref, False)
     if step == WIDE_STEP:
         cell_sums(stored_moment(mom_ref), sums_ref)
-        fill_messages_y(now_ref, odd_ref, even_ref, 2)
-        fill_messages_y(sums_ref, odd_ref, even_ref, 1, 16)
-        odd_ref[24:42, :] = joint_odd_ref[...]
-        even_ref[24:42, :] = joint_even_ref[...]
 
 
 def nested_hops(step, shifts_ref):
@@ -431,9 +481,37 @@
     return [means[comp] - turn[comp] for comp in range(3)] + [jnp.ones_like(means[0])]
 
 
-def shift_kernel(step, shifts_ref, sums_ref, from_odd_ref, from_even_ref, axes_ref, mom_ref, joint_ref, shift_ref, new_ref, *refs):
-    *messages, work_ref, tot_ref, next_ref = refs
-    means = cell_means(sums_ref, from_odd_ref, from_even_ref, work_ref, tot_ref)
+def own_cells(far_ref, out_ref):
+    for hop in range(2):
+        for side in range(2):
+            out_ref[side, hop * 24 : hop * 24 + 24, :] = far_ref[side, hop * 40 + 8 : hop * 40 + 32, :]
+
+
+def side_cells(side):
+    first = side * 3
+    return ((first, first + 1), (first + 5, first + 6))
+
+
+def add_side(new_ref, side, came_ref, sources, nested):
+    def moment_of(later):
+        total = None
+        for row, parts in sources:
+            term = shift_moment(came_ref, row, parts, later, nested, (6, 3, 1))
+            total = term if total is None else total + term
+        return total
+
+    quads = []
+    for moment in (0, 4):
+        up = moment_of(moment + 1)
+        quads.append(moment_of(moment) - up + pltpu.roll(up, 1, 1))
+    for hop, piece in enumerate((quads[0] - quads[1], quads[1])):
+        rows = slice(hop * 12 + side * 8, hop * 12 + side * 8 + 4)
+        new_ref[rows, :] = new_ref[rows, :] + piece[0:4, :]
+
+
+def shift_kernel(step, shifts_ref, sums_ref, from_odd_ref, from_even_ref, axes_ref, mom_ref, joint_ref, shift_ref, new_ref, odd_ref, even_ref, work_ref, tot_ref, next_ref):
+    add_x(sums_ref, from_odd_ref, from_even_ref, work_ref)
+    means = cell_means(work_ref, tot_ref)
     shift_ref[...] = jnp.zeros_like(shift_ref)
     store_cells(shift_ref, shifts_of(means, [axes_ref[comp] for comp in range(3)]))
     nested = nested_hops(step, shifts_ref)
@@ -443,17 +521,18 @@
             row = (col * 8 + later) * 8
             next_ref[row : row + 8, :] = mom_ref[row : row + 8, :] + shift_moment(joint_ref, col * 27, parts, later, nested)
     cell_sums(stored_moment(next_ref), new_ref)
-    if messages:
-        fill_messages_y(new_ref, *messages)
-
-
-def wide_shift_kernel(step, shifts_ref, sums_ref, from_odd_ref, from_even_ref, axes_ref, turned_ref, joint_ref, y_odd_ref, y_even_ref, shift_ref, new_ref, odd_ref, even_ref, work_ref, tot_ref, next_ref, far_ref, side_ref):
-    means = cell_means(sums_ref, from_odd_ref, from_even_ref, work_ref, tot_ref, 5)
+    fill_messages_x(new_ref, 12, odd_ref, even_ref)
+
+
+def wide_shift_kernel(step, shifts_ref, sums_ref, from_odd_ref, from_even_ref, axes_ref, turned_ref, joint_ref, shift_ref, new_ref, odd_ref, even_ref, work_ref, tot_ref, next_ref, far_ref, left_ref, right_ref):
+    by_left, by_right = from_sides("gy", from_odd_ref[...], from_even_ref[...])
+    left_ref[...] = by_left
+    right_ref[...] = by_right
+    add_y(sums_ref, left_ref, right_ref, work_ref)
+    means = cell_means(work_ref, tot_ref, 10)
     far_ref[...] = jnp.zeros_like(far_ref)
     store_cells(far_ref, shifts_of(means, [axes_ref[comp] for comp in range(3)]), 10)
-    for hop in range(2):
-        for side in range(2):
-            shift_ref[side, hop * 24 : hop * 24 + 24, :] = far_ref[side, hop * 40 + 8 : hop * 40 + 32, :]
+    own_cells(far_ref, shift_ref)
     nested = nested_hops(step, shifts_ref)
     for col in range(2):
         parts = corner_differences(far_ref, ((col + 1, col + 2), (col + 6, col + 7)))
@@ -462,40 +541,43 @@
             next_ref[row : row + 8, :] = shift_moment(joint_ref, col * 27, parts, later, nested)
     cell_sums(stored_moment(next_ref), new_ref)
     new_ref[...] = new_ref[...] + turned_ref[...]
-    for side, came in enumerate(from_sides("gy", y_odd_ref[16:42, :], y_even_ref[16:42, :])):
-        side_ref[...] = came
-        first = side * 3
-        parts = corner_differences(far_ref, ((first, first + 1), (first + 5, first + 6)))
-        quads = []
-        for moment in (0, 4):
-            up = shift_moment(side_ref, 8, parts, moment + 1, nested, (6, 3, 1))
-            quads.append(shift_moment(side_ref, 8, parts, moment, nested, (6, 3, 1)) - up + pltpu.roll(up, 1, 1))
-        for hop, piece in enumerate((quads[0] - quads[1], quads[1])):
+    for side, came_ref in enumerate((left_ref, right_ref)):
+        for hop in range(2):
             rows = slice(hop * 12 + side * 8, hop * 12 + side * 8 + 4)
-            new_ref[rows, :] = new_ref[rows, :] + piece[0:4, :] + side_ref[hop * 4 : hop * 4 + 4, :]
+            new_ref[rows, :] = new_ref[rows, :] + came_ref[16 + hop * 4 : 20 + hop * 4, :]
+        add_side(new_ref, side, came_ref, [(24, corner_differences(far_ref, side_cells(side)))], nested)
     fill_messages_x(new_ref, 12, odd_ref, even_ref)
 
 
-def last_kernel(shifts_ref, code_ref, vel_ref, sums_ref, from_odd_ref, from_even_ref, axes_ref, out_ref, means_ref, work_ref, tot_ref, table_ref, end_ref):
-    means = cell_means(sums_ref, from_odd_ref, from_even_ref, work_ref, tot_ref)
+def last_kernel(shifts_ref, code_ref, vel_ref, sums_ref, from_odd_ref, from_even_ref, axes_ref, out_hbm, means_hbm, work_ref, tot_ref, table_ref, end_ref, out_ref, means_ref, sems):
+    add_x(sums_ref, from_odd_ref, from_even_ref, work_ref)
+    means = cell_means(work_ref, tot_ref)
     turn = turned([axes_ref[comp] for comp in range(3)], means)
     table_ref[...] = jnp.zeros_like(table_ref)
     store_cells(table_ref, [means[comp] - turn[comp] for comp in range(3)])
     for comp in range(3):
         means_ref[comp] = means[comp][0:2, :]
-    for col, lanes in blocks():
-
-        def body(rows):
-            code = code_ref[col, rows, lanes]
-            masks = hop_masks(code, shifts_ref, ITERS - 1)
-            filled = code >= 0
-            for comp in range(3):
-                value = vel_ref[comp * 2 + col, rows, lanes] + pick(table_ref, comp, col, lanes, masks)
-                end_ref[comp * 2 + col, rows, lanes] = jnp.where(filled, value, 0.0)
-
-        over_slots(body)
-    for at in range(6):
-        out_ref[at] = end_ref[at].T.astype(jnp.bfloat16)
+    saves = [pltpu.make_async_copy(means_ref, means_hbm, sems.at[6])]
+    saves[0].start()
+    for col in range(2):
+        for _, lanes in blocks((col,)):
+
+            def body(rows):
+                code = code_ref[col, rows, lanes]
+                masks = hop_masks(code, shifts_ref, ITERS - 1)
+                filled = code >= 0
+                for comp in range(3):
+                    value = vel_ref[comp * 2 + col, rows, lanes] + pick(table_ref, comp, col, lanes, masks)
+                    end_ref[comp * 2 + col, rows, lanes] = jnp.where(filled, value, 0.0)
+
+            over_slots(body)
+        for comp in range(3):
+            at = comp * 2 + col
+            out_ref[at] = end_ref[at].T.astype(jnp.bfloat16)
+            saves.append(pltpu.make_async_copy(out_ref.at[at], out_hbm.at[at], sems.at[at]))
+            saves[-1].start()
+    for save in saves:
+        save.wait()
 
 
 VMEM = pl.BlockSpec(memory_space=pltpu.VMEM)
@@ -504,12 +586,12 @@
 BYTES = 8_000_000
 
 
-def call(kernel, name, in_specs, shapes, scratch, cost=0):
+def call(kernel, name, in_specs, shapes, scratch, cost=0, out_specs=None):
     return pl.pallas_call(
         kernel,
         out_shape=[jax.ShapeDtypeStruct(s, d) for s, d in shapes],
         in_specs=in_specs,
-        out_specs=[VMEM] * len(shapes),
+        out_specs=out_specs or [VMEM] * len(shapes),
         scratch_shapes=scratch,
         compiler_params=pltpu.CompilerParams(vmem_limit_bytes=16 * 1024 * 1024),
         cost_estimate=pl.CostEstimate(flops=0, bytes_accessed=cost, transcendentals=0) if cost else None,
@@ -542,66 +624,65 @@
     table_shape, axes_shape = ((2, WIDE, 256), F32), ((3, 8, 256), F32)
     moments, table = room(128, 256), room(2, WIDE, 256)
     small = [room(24, 256), room(4, 8, 256)]
+    wide_small, far = [room(40, 256), room(4, 16, 256)], room(2, 80, 256)
 
     vel, code, sums, odd, even = call(
-        start_kernel, "start", [HBM] * 5, [vel_shape, code_shape, rows(24), rows(13), rows(13)],
+        start_kernel, "start", [HBM] * 5, [vel_shape, code_shape, rows(24), rows(20), rows(20)],
         [moments, pltpu.VMEM((6, 256, 128), jnp.bfloat16), pltpu.VMEM((2, 256, 128), jnp.int32), pltpu.VMEM((2, 256), jnp.int32), pltpu.VMEM((ITERS, 2, 256), jnp.int32), pltpu.SMEM((ITERS, 3), jnp.int32), pltpu.SemaphoreType.DMA((11,))],
     )(*(pltpu.with_memory_space_constraint(x, pltpu.HBM) for x in (shifts, vel_in, code_in, occ, ids_in)))
 
+    from_odd, from_even = swap(odd, even, "gx")
+    ghost_odd, ghost_even = call(
+        ghost_kernel, "ghost", [SMEM, VMEM, VMEM], [rows(72), rows(72)], [room(72, 256), room(72, 256)], BYTES
+    )(shifts, vel, code)
+    sums, both, odd, even = call(
+        first_middle_kernel, "middle0", [VMEM] * 6, [rows(24), rows(16), rows(100), rows(100)], [],
+    )(sums, from_odd, from_even, ids_in, ghost_odd, ghost_even)
     from_odd, from_even = swap(odd, even, "gy")
-    sums, odd, even = call(
-        functools.partial(middle_kernel, True), "middle0", [VMEM] * 4, [rows(38), rows(26), rows(26)], [],
-    )(sums, from_odd, from_even, ids_in)
-    from_odd, from_even = swap(odd, even, "gx")
-    *joints, joint_odd, joint_even = call(
-        joint_kernel, "joint", [SMEM, VMEM], [rows(56), rows(56), rows(18), rows(18)], [], BYTES
-    )(shifts, code)
     vel, ids, far_ids, sums, odd, even = call(
-        first_kernel, "first", [SMEM] + [VMEM] * 6, [vel_shape, rows(32), rows(16), rows(24), rows(8), rows(8)], [moments, *small, table],
-    )(shifts, vel, code, sums, from_odd, from_even, joints[0])
+        first_kernel, "first", [SMEM] + [VMEM] * 6, [vel_shape, rows(32), rows(32), rows(24), rows(12), rows(12)],
+        [moments, *wide_small, table, table, far, room(3, 2, 80, 256), room(100, 256), room(100, 256)],
+    )(shifts, vel, code, sums, from_odd, from_even, both)
 
     shift = None
     for step in range(1, ITERS):
-        last, wide, after_wide = step == ITERS - 1, step == WIDE_STEP, step == WIDE_STEP + 1
+        last, wide = step == ITERS - 1, step == WIDE_STEP
+        from_odd, from_even = swap(odd, even, "gx")
         args = [shifts, code, ids, vel] + ([] if step == 1 else [shift])
         shapes, scratch = [vel_shape, axes_shape], [table]
         if wide:
-            args += [far_ids, joint_odd, joint_even, sums]
-            shapes = [vel_shape, ((3, 16, 256), F32), rows(24), rows(42), rows(42)]
+            args.append(far_ids)
+            shapes = [vel_shape, ((3, 16, 256), F32), rows(24)]
             scratch = [table, moments]
         elif not last:
             shapes.append(rows(128))
         vel, axes, *more = call(
             functools.partial(turn_kernel, step), f"turn{step}", [SMEM] + [VMEM] * (len(args) - 1), shapes, scratch, BYTES,
         )(*args)
-        if wide:
-            own, odd, even = more
-        if not after_wide:
-            y_odd, y_even = swap(odd, even, "gy")
-            sums, odd, even = call(
-                wide_middle_kernel if wide else functools.partial(middle_kernel, False), f"middle{step}", [VMEM] * 3,
-                [rows(40), rows(20), rows(20)] if wide else [rows(24), rows(12), rows(12)], [],
-            )(sums, y_odd, y_even)
-        from_odd, from_even = swap(odd, even, "gx")
+        if step == 1:
+            *joints, joint_odd, joint_even = call(
+                joint_kernel, "joint", [SMEM, VMEM], [rows(56), rows(56), rows(18), rows(18)], [], BYTES
+            )(shifts, code)
         if last:
             out, out_means = call(
                 last_kernel, "last", [SMEM] + [VMEM] * 6, [((6, 256, 128), jnp.bfloat16), ((3, 2, 256), F32)],
-                [*small, table, room(6, 128, 256)],
+                [*small, table, room(6, 128, 256), pltpu.VMEM((6, 256, 128), jnp.bfloat16), room(3, 2, 256), pltpu.SemaphoreType.DMA((7,))],
+                out_specs=[HBM, HBM],
             )(shifts, code, vel, sums, from_odd, from_even, axes)
         elif wide:
+            sums, odd, even = call(
+                wide_middle_kernel, f"middle{step}", [VMEM] * 6, [rows(24), rows(42), rows(42)], [],
+            )(sums, from_odd, from_even, more[0], joint_odd, joint_even)
+            from_odd, from_even = swap(odd, even, "gy")
             shift, sums, odd, even = call(
-                functools.partial(wide_shift_kernel, step), f"shift{step}", [SMEM] + [VMEM] * 8,
-                [table_shape, rows(24), rows(12), rows(12)],
-                [room(40, 256), room(4, 16, 256), moments, room(2, 80, 256), room(26, 256)],
-            )(shifts, sums, from_odd, from_even, axes, own, joints[step - 1], y_odd, y_even)
+                functools.partial(wide_shift_kernel, step), f"shift{step}", [SMEM] + [VMEM] * 6,
+                [table_shape, rows(24), rows(12), rows(12)], [*wide_small, moments, far, room(42, 256), room(42, 256)],
+            )(shifts, sums, from_odd, from_even, axes, more[0], joints[step - 1])
         else:
-            messages = [] if step + 1 == WIDE_STEP else [rows(8), rows(8)]
-            shift, sums, *pair = call(
+            shift, sums, odd, even = call(
                 functools.partial(shift_kernel, step), f"shift{step}", [SMEM] + [VMEM] * 6,
-                [table_shape, rows(24), *messages], [*small, moments],
+                [table_shape, rows(24), rows(12), rows(12)], [*small, moments],
             )(shifts, sums, from_odd, from_even, axes, more[0], joints[step - 1])
-            if pair:
-                odd, even = pair
     return out.reshape(velocity.shape), out_means.reshape(3, *occupancy.shape)
 
 

time: 87.1 us -> 78.7 us (0.904)
  waiting for transfers between devices: 19.9 us -> 14.1 us
  starting transfers between devices: 49 us -> 44.1 us
  Pallas kernels: 16.9 us -> 19.3 us
    ppermute x7 -> x6, waiting for transfers between devices: 14.3 us -> 9.23 us  [swap(): from_odd = lax.ppermute(odd, axis, odds)]
    ppermute x7 -> x6, starting transfers between devices: 34.8 us -> 30.4 us  [swap(): from_odd = lax.ppermute(odd, axis, odds)]
    pallas_call x3, Pallas kernels: 0.08 us -> 2.48 us  [the longest x1 2.41 us: on_device(): call(ghost_kernel, 'ghost', [SMEM, VMEM, VMEM], [rows(72), rows(72)], [ro...]
    ppermute x7 -> x6, waiting for transfers between devices: 5.57 us -> 4.83 us  [swap(): from_even = lax.ppermute(even, axis, evens)]
    ppermute x7 -> x6, starting transfers between devices: 14.2 us -> 13.6 us  [swap(): from_even = lax.ppermute(even, axis, evens)]
  transfers between devices with their start and end apart: 14 -> 12, of which waited for: 8 -> 7; matrix products, arithmetic and copies ran while one was open for 0% -> 0% of each run, Pallas kernels for 7% -> 13%
where the time goes in v4:
time: 78.7 us; the launch traced here: 78.3 us
  starting transfers between devices  44.1 us (56%)
  Pallas kernels  19.3 us (25%)
  waiting for transfers between devices  14.1 us (18%)
  between operations  0.82 us (1%)
    ppermute x6, starting transfers between devices, swap(): from_odd = lax.ppermute(odd, axis, odds)  30.4 us
    ppermute x6, starting transfers between devices, swap(): from_even = lax.ppermute(even, axis, evens)  13.6 us
    ppermute x6, waiting for transfers between devices, swap(): from_odd = lax.ppermute(odd, axis, odds)  9.23 us
    pallas_call x3, Pallas kernels, on_device(): call(functools.partial(turn_kernel, step), f'turn{step}', [SMEM] + [VMEM]...  5.19 us
    ppermute x6, waiting for transfers between devices, swap(): from_even = lax.ppermute(even, axis, evens)  4.83 us
    pallas_call x1, Pallas kernels, on_device(): call(first_kernel, 'first', [SMEM] + [VMEM] * 6, [vel_shape, rows(32), ro...  2.82 us
    pallas_call x1, Pallas kernels, on_device(): call(joint_kernel, 'joint', [SMEM, VMEM], [rows(56), rows(56), rows(18),...  2.62 us
    pallas_call x1, Pallas kernels, on_device(): call(start_kernel, 'start', [HBM] * 5, [vel_shape, code_shape, rows(24),...  2.55 us
  transfers between devices with their start and end apart: 12, of which 7 were waited for; matrix products, arithmetic and copies ran while one was open for 0% of the time, Pallas kernels for 13%

profile of v4, /device:TPU:32, one launch (start us, length us, event | category | flops | bytes accessed | tf_op | source)
XLA Modules:
  0.0 78.3 jit_solution(1400599313495002680)
XLA Ops:
  0.6 2.5 %start.1 = (f32[6,128,256]{2,1,0:T(8,128)S(1)}, s32[2,128,256]{2,1,0:T(8,128)S(1)}, f32[24,256]{1,0:T(8,128)S(1)}, f32[20,256]{1,0:T(8,128)S(1)}, f32[20,256]{1,0:T(8,128)S(1)}) custom-call(s32[4,3]{1,0:T(4,128)} %shifts_ref.11, bf16[6,256,128]{2,1,0:T(8,128)(2,1)} %bitcast.12, s32[2,256,128]{2,1,0:T(8,128)} %bitcast.13, s32[2,256]{1,0:T(2,128)} %bitcast.14, ...), custom_call_target="tpu_custom_call" | custom-call | tf_op jit(solution)/shard_map/start/pallas_call | solution.py:629
  3.2 13.1 %collective-permute-start = (f32[20,256]{1,0:T(8,128)S(1)}, f32[20,256]{1,0:T(8,128)S(1)}, u32[]{:S(2)}, u32[]{:S(2)}) collective-permute-start(f32[20,256]{1,0:T(8,128)S(1)} %get-tuple-element.47), channel_id=1, source_target_pairs={{0,480},{32,64},{64,32},{96,128},{128,96},{160,192},{192,160},{224... | collective-permute-start | bytes 61448 | tf_op jit(solution)/shard_map/ppermute | solution.py:607
  16.3 0.0 copy-start
  16.3 1.9 %collective-permute-start.1 = (f32[20,256]{1,0:T(8,128)S(1)}, f32[20,256]{1,0:T(8,128)S(1)}, u32[]{:S(2)}, u32[]{:S(2)}) collective-permute-start(f32[20,256]{1,0:T(8,128)S(1)} %get-tuple-element.48), channel_id=1, source_target_pairs={{0,32},{32,0},{64,96},{96,64},{128,160},{160,128},{192,224},{224,1... | collective-permute-start | bytes 61448 | tf_op jit(solution)/shard_map/ppermute | solution.py:606
  18.3 0.0 copy-done
  18.3 0.0 copy-start.1
  18.3 2.4 %ghost.1 = (f32[72,256]{1,0:T(8,128)S(1)}, f32[72,256]{1,0:T(8,128)S(1)}) custom-call(s32[4,3]{1,0:T(4,128)S(1)} %copy-done, f32[6,128,256]{2,1,0:T(8,128)S(1)} %get-tuple-element.45.vel_ref, s32[2,128,256]{2,1,0:T(8,128)S(1)} %get-tuple-element.44.code_ref.refs_1_), custom_call_target="tpu_custom_call" | custom-call | bytes 8000000 | tf_op jit(solution)/shard_map/ghost/pallas_call | solution.py:635
  20.7 0.0 collective-permute-done.from_odd_ref
  20.7 2.2 %collective-permute-done.1.from_even_ref = f32[20,256]{1,0:T(8,128)S(1)} collective-permute-done((f32[20,256]{1,0:T(8,128)S(1)}, f32[20,256]{1,0:T(8,128)S(1)}, u32[]{:S(2)}, u32[]{:S(2)}) %collective-permute-start.1) | collective-permute-done | bytes 20512 | tf_op jit(solution)/shard_map/ppermute | solution.py:606
  23.0 0.0 copy-done.1
  23.0 1.9 %collective-permute-start.2 = (f32[100,256]{1,0:T(8,128)S(1)}, f32[100,256]{1,0:T(8,128)S(1)}, u32[]{:S(2)}, u32[]{:S(2)}) collective-permute-start(f32[100,256]{1,0:T(8,128)S(1)} %get-tuple-element.52), channel_id=1, source_target_pairs={{0,31},{1,2},{2,1},{3,4},{4,3},{5,6},{6,5},{7,8},{8,7},{9,10},{10,... | collective-permute-start | bytes 307208 | tf_op jit(solution)/shard_map/ppermute | solution.py:607
  24.9 3.5 %collective-permute-start.3 = (f32[100,256]{1,0:T(8,128)S(1)}, f32[100,256]{1,0:T(8,128)S(1)}, u32[]{:S(2)}, u32[]{:S(2)}) collective-permute-start(f32[100,256]{1,0:T(8,128)S(1)} %get-tuple-element.53), channel_id=1, source_target_pairs={{0,1},{1,0},{2,3},{3,2},{4,5},{5,4},{6,7},{7,6},{8,9},{9,8},{10,11... | collective-permute-start | bytes 307208 | tf_op jit(solution)/shard_map/ppermute | solution.py:606
  28.4 2.7 %collective-permute-done.2.from_odd_ref = f32[100,256]{1,0:T(8,128)S(1)} collective-permute-done((f32[100,256]{1,0:T(8,128)S(1)}, f32[100,256]{1,0:T(8,128)S(1)}, u32[]{:S(2)}, u32[]{:S(2)}) %collective-permute-start.2) | collective-permute-done | bytes 102432 | tf_op jit(solution)/shard_map/ppermute | solution.py:607
  31.1 0.0 collective-permute-done.3.from_even_ref
  31.1 2.8 %first.1 = (f32[6,128,256]{2,1,0:T(8,128)S(1)}, f32[32,256]{1,0:T(8,128)S(1)}, f32[32,256]{1,0:T(8,128)S(1)}, f32[24,256]{1,0:T(8,128)S(1)}, f32[12,256]{1,0:T(8,128)S(1)}, /*index=5*/f32[12,256]{1,0:T(8,128)S(1)}) custom-call(s32[4,3]{1,0:T(4,128)S(1)} %copy-done, f32[6,128,256]{2,1,0:T(8,128)S(1)} %get-tuple-element.45.vel_ref, ...), custom_call_target="tpu_custom_call" | custom-call | tf_op jit(solution)/shard_map/first/pallas_call | solution.py:642
  34.0 3.3 %collective-permute-start.4 = (f32[12,256]{1,0:T(8,128)S(1)}, f32[12,256]{1,0:T(8,128)S(1)}, u32[]{:S(2)}, u32[]{:S(2)}) collective-permute-start(f32[12,256]{1,0:T(8,128)S(1)} %get-tuple-element.59), channel_id=1, source_target_pairs={{0,480},{32,64},{64,32},{96,128},{128,96},{160,192},{192,160},{224... | collective-permute-start | bytes 36872 | tf_op jit(solution)/shard_map/ppermute | solution.py:607
  37.3 1.9 %collective-permute-start.5 = (f32[12,256]{1,0:T(8,128)S(1)}, f32[12,256]{1,0:T(8,128)S(1)}, u32[]{:S(2)}, u32[]{:S(2)}) collective-permute-start(f32[12,256]{1,0:T(8,128)S(1)} %get-tuple-element.60), channel_id=1, source_target_pairs={{0,32},{32,0},{64,96},{96,64},{128,160},{160,128},{192,224},{224,1... | collective-permute-start | bytes 36872 | tf_op jit(solution)/shard_map/ppermute | solution.py:606
  39.2 2.6 %joint.1 = (f32[56,256]{1,0:T(8,128)S(1)}, f32[56,256]{1,0:T(8,128)S(1)}, f32[18,256]{1,0:T(8,128)S(1)}, f32[18,256]{1,0:T(8,128)S(1)}) custom-call(s32[4,3]{1,0:T(4,128)S(1)} %copy-done, s32[2,128,256]{2,1,0:T(8,128)S(1)} %get-tuple-element.44.code_ref.refs_1_), custom_call_target="tpu_custom_call" | custom-call | bytes 8000000 | tf_op jit(solution)/shard_map/joint/pallas_call | solution.py:663
  41.9 1.7 %turn1.1 = (f32[6,128,256]{2,1,0:T(8,128)S(1)}, f32[3,8,256]{2,1,0:T(8,128)S(1)}, f32[128,256]{1,0:T(8,128)S(1)}) custom-call(s32[4,3]{1,0:T(4,128)S(1)} %copy-done, s32[2,128,256]{2,1,0:T(8,128)S(1)} %get-tuple-element.44.code_ref.refs_1_, f32[32,256]{1,0:T(8,128)S(1)} %get-tuple-element.55.refs_2_, f32[6,128,256]{2,1,0:T(8,128)S(1)} %get-tuple-element.56.refs_3_), custom_call_target="tpu_custom_call" | custom-call | bytes 8000000 | tf_op jit(solution)/shard_map/turn1/pallas_call | solution.py:659
  43.5 0.3 collective-permute-done.4.from_odd_ref
  43.8 0.0 collective-permute-done.5.from_even_ref
  43.8 0.8 %shift1.1 = (f32[2,48,256]{2,1,0:T(8,128)S(1)}, f32[24,256]{1,0:T(8,128)S(1)}, f32[12,256]{1,0:T(8,128)S(1)}, f32[12,256]{1,0:T(8,128)S(1)}) custom-call(s32[4,3]{1,0:T(4,128)S(1)} %copy-done, f32[24,256]{1,0:T(8,128)S(1)} %get-tuple-element.58.sums_ref, f32[12,256]{1,0:T(8,128)S(1)} %collective-permute-done.4.from_odd_ref, ...), custom_call_target="tpu_custom_call" | custom-call | tf_op jit(solution)/shard_map/shift1/pallas_call | solution.py:682
  44.7 6.7 %collective-permute-start.6 = (f32[12,256]{1,0:T(8,128)S(1)}, f32[12,256]{1,0:T(8,128)S(1)}, u32[]{:S(2)}, u32[]{:S(2)}) collective-permute-start(f32[12,256]{1,0:T(8,128)S(1)} %get-tuple-element.68), channel_id=1, source_target_pairs={{0,480},{32,64},{64,32},{96,128},{128,96},{160,192},{192,160},{224... | collective-permute-start | bytes 36872 | tf_op jit(solution)/shard_map/ppermute | solution.py:607
  51.4 1.9 %collective-permute-start.7 = (f32[12,256]{1,0:T(8,128)S(1)}, f32[12,256]{1,0:T(8,128)S(1)}, u32[]{:S(2)}, u32[]{:S(2)}) collective-permute-start(f32[12,256]{1,0:T(8,128)S(1)} %get-tuple-element.69), channel_id=1, source_target_pairs={{0,32},{32,0},{64,96},{96,64},{128,160},{160,128},{192,224},{224,1... | collective-permute-start | bytes 36872 | tf_op jit(solution)/shard_map/ppermute | solution.py:606
  53.3 2.1 %turn2.1 = (f32[6,128,256]{2,1,0:T(8,128)S(1)}, f32[3,16,256]{2,1,0:T(8,128)S(1)}, f32[24,256]{1,0:T(8,128)S(1)}) custom-call(s32[4,3]{1,0:T(4,128)S(1)} %copy-done, s32[2,128,256]{2,1,0:T(8,128)S(1)} %get-tuple-element.44.code_ref.refs_1_, f32[32,256]{1,0:T(8,128)S(1)} %get-tuple-element.55.refs_2_, f32[6,128,256]{2,1,0:T(8,128)S(1)} %get-tuple-element.57.refs_3_, ...), custom_call_target="tpu_custom_call" | custom-call | bytes 8000000 | tf_op jit(solution)/shard_map/turn2/pallas_call | solution.py:659
  55.5 0.0 collective-permute-done.6.from_odd_ref
  55.5 2.4 %collective-permute-done.7.from_even_ref = f32[12,256]{1,0:T(8,128)S(1)} collective-permute-done((f32[12,256]{1,0:T(8,128)S(1)}, f32[12,256]{1,0:T(8,128)S(1)}, u32[]{:S(2)}, u32[]{:S(2)}) %collective-permute-start.7) | collective-permute-done | bytes 12320 | tf_op jit(solution)/shard_map/ppermute | solution.py:606
  58.0 1.9 %collective-permute-start.8 = (f32[42,256]{1,0:T(8,128)S(1)}, f32[42,256]{1,0:T(8,128)S(1)}, u32[]{:S(2)}, u32[]{:S(2)}) collective-permute-start(f32[42,256]{1,0:T(8,128)S(1)} %get-tuple-element.74), channel_id=1, source_target_pairs={{0,31},{1,2},{2,1},{3,4},{4,3},{5,6},{6,5},{7,8},{8,7},{9,10},{10,... | collective-permute-start | bytes 129032 | tf_op jit(solution)/shard_map/ppermute | solution.py:607
  59.9 2.0 %collective-permute-start.9 = (f32[42,256]{1,0:T(8,128)S(1)}, f32[42,256]{1,0:T(8,128)S(1)}, u32[]{:S(2)}, u32[]{:S(2)}) collective-permute-start(f32[42,256]{1,0:T(8,128)S(1)} %get-tuple-element.75), channel_id=1, source_target_pairs={{0,1},{1,0},{2,3},{3,2},{4,5},{5,4},{6,7},{7,6},{8,9},{9,8},{10,11... | collective-permute-start | bytes 129032 | tf_op jit(solution)/shard_map/ppermute | solution.py:606
  61.9 3.6 %collective-permute-done.8.from_odd_ref = f32[42,256]{1,0:T(8,128)S(1)} collective-permute-done((f32[42,256]{1,0:T(8,128)S(1)}, f32[42,256]{1,0:T(8,128)S(1)}, u32[]{:S(2)}, u32[]{:S(2)}) %collective-permute-start.8) | collective-permute-done | bytes 43040 | tf_op jit(solution)/shard_map/ppermute | solution.py:607
  65.5 0.0 collective-permute-done.9.from_even_ref
  65.5 0.9 %shift2.1 = (f32[2,48,256]{2,1,0:T(8,128)S(1)}, f32[24,256]{1,0:T(8,128)S(1)}, f32[12,256]{1,0:T(8,128)S(1)}, f32[12,256]{1,0:T(8,128)S(1)}) custom-call(s32[4,3]{1,0:T(4,128)S(1)} %copy-done, f32[24,256]{1,0:T(8,128)S(1)} %get-tuple-element.73.sums_ref, f32[42,256]{1,0:T(8,128)S(1)} %collective-permute-done.8.from_odd_ref, ...), custom_call_target="tpu_custom_call" | custom-call | tf_op jit(solution)/shard_map/shift2/pallas_call | solution.py:677
  66.4 3.4 %collective-permute-start.10 = (f32[12,256]{1,0:T(8,128)S(1)}, f32[12,256]{1,0:T(8,128)S(1)}, u32[]{:S(2)}, u32[]{:S(2)}) collective-permute-start(f32[12,256]{1,0:T(8,128)S(1)} %get-tuple-element.81), channel_id=1, source_target_pairs={{0,480},{32,64},{64,32},{96,128},{128,96},{160,192},{192,160},{224... | collective-permute-start | bytes 36872 | tf_op jit(solution)/shard_map/ppermute | solution.py:607
  69.8 2.4 %collective-permute-start.11 = (f32[12,256]{1,0:T(8,128)S(1)}, f32[12,256]{1,0:T(8,128)S(1)}, u32[]{:S(2)}, u32[]{:S(2)}) collective-permute-start(f32[12,256]{1,0:T(8,128)S(1)} %get-tuple-element.82), channel_id=1, source_target_pairs={{0,32},{32,0},{64,96},{96,64},{128,160},{160,128},{192,224},{224,1... | collective-permute-start | bytes 36872 | tf_op jit(solution)/shard_map/ppermute | solution.py:606
  72.2 1.4 %turn3.1 = (f32[6,128,256]{2,1,0:T(8,128)S(1)}, f32[3,8,256]{2,1,0:T(8,128)S(1)}) custom-call(s32[4,3]{1,0:T(4,128)S(1)} %copy-done, s32[2,128,256]{2,1,0:T(8,128)S(1)} %get-tuple-element.44.code_ref.refs_1_, f32[32,256]{1,0:T(8,128)S(1)} %get-tuple-element.55.refs_2_, f32[6,128,256]{2,1,0:T(8,128)S(1)} %get-tuple-element.66.refs_3_, ...), custom_call_target="tpu_custom_call" | custom-call | bytes 8000000 | tf_op jit(solution)/shard_map/turn3/pallas_call | solution.py:659
  73.6 2.6 %collective-permute-done.10.from_odd_ref = f32[12,256]{1,0:T(8,128)S(1)} collective-permute-done((f32[12,256]{1,0:T(8,128)S(1)}, f32[12,256]{1,0:T(8,128)S(1)}, u32[]{:S(2)}, u32[]{:S(2)}) %collective-permute-start.10) | collective-permute-done | bytes 12320 | tf_op jit(solution)/shard_map/ppermute | solution.py:607
  76.2 0.1 collective-permute-done.11.from_even_ref
  76.3 1.9 %last.1 = (bf16[6,256,128]{2,1,0:T(8,128)(2,1)}, f32[3,2,256]{2,1,0:T(2,128)}) custom-call(s32[4,3]{1,0:T(4,128)S(1)} %copy-done, s32[2,128,256]{2,1,0:T(8,128)S(1)} %get-tuple-element.44.code_ref.refs_1_, f32[6,128,256]{2,1,0:T(8,128)S(1)} %get-tuple-element.79.vel_ref, f32[24,256]{1,0:T(8,128)S(1)} %get-tuple-element.80.sums_ref, ...), custom_call_target="tpu_custom_call" | custom-call | tf_op jit(solution)/shard_map/last/pallas_call | solution.py:667
  (2 shorter events, 0.1 us)
Async XLA Ops:
  3.2 17.5 %collective-permute-start = (f32[20,256]{1,0:T(8,128)S(1)}, f32[20,256]{1,0:T(8,128)S(1)}, u32[]{:S(2)}, u32[]{:S(2)}) collective-permute-start(f32[20,256]{1,0:T(8,128)S(1)} %get-tuple-element.47), channel_id=1, source_target_pairs={{0,480},{32,64},{64,32},{96,128},{128,96},{160,192},{192,160},{224... | collective-permute-start | bytes 61448 | tf_op jit(solution)/shard_map/ppermute | solution.py:607
  16.3 1.9 %copy-start = (s32[4,3]{1,0:T(4,128)S(1)}, s32[4,3]{1,0:T(4,128)}, u32[]{:S(2)}) copy-start(s32[4,3]{1,0:T(4,128)} %shifts_ref.11) | copy-start | bytes 148
  16.3 6.6 %collective-permute-start.1 = (f32[20,256]{1,0:T(8,128)S(1)}, f32[20,256]{1,0:T(8,128)S(1)}, u32[]{:S(2)}, u32[]{:S(2)}) collective-permute-start(f32[20,256]{1,0:T(8,128)S(1)} %get-tuple-element.48), channel_id=1, source_target_pairs={{0,32},{32,0},{64,96},{96,64},{128,160},{160,128},{192,224},{224,1... | collective-permute-start | bytes 61448 | tf_op jit(solution)/shard_map/ppermute | solution.py:606
  18.3 4.7 %copy-start.1 = (s32[4,1,2,256]{3,2,1,0:T(2,128)S(1)}, s32[4,1,2,256]{3,2,1,0:T(2,128)}, u32[]{:S(2)}) copy-start(s32[4,1,2,256]{3,2,1,0:T(2,128)} %param.9) | copy-start | bytes 24580
  23.0 8.1 %collective-permute-start.2 = (f32[100,256]{1,0:T(8,128)S(1)}, f32[100,256]{1,0:T(8,128)S(1)}, u32[]{:S(2)}, u32[]{:S(2)}) collective-permute-start(f32[100,256]{1,0:T(8,128)S(1)} %get-tuple-element.52), channel_id=1, source_target_pairs={{0,31},{1,2},{2,1},{3,4},{4,3},{5,6},{6,5},{7,8},{8,7},{9,10},{10,... | collective-permute-start | bytes 307208 | tf_op jit(solution)/shard_map/ppermute | solution.py:607
  24.9 6.2 %collective-permute-start.3 = (f32[100,256]{1,0:T(8,128)S(1)}, f32[100,256]{1,0:T(8,128)S(1)}, u32[]{:S(2)}, u32[]{:S(2)}) collective-permute-start(f32[100,256]{1,0:T(8,128)S(1)} %get-tuple-element.53), channel_id=1, source_target_pairs={{0,1},{1,0},{2,3},{3,2},{4,5},{5,4},{6,7},{7,6},{8,9},{9,8},{10,11... | collective-permute-start | bytes 307208 | tf_op jit(solution)/shard_map/ppermute | solution.py:606
  34.0 9.8 %collective-permute-start.4 = (f32[12,256]{1,0:T(8,128)S(1)}, f32[12,256]{1,0:T(8,128)S(1)}, u32[]{:S(2)}, u32[]{:S(2)}) collective-permute-start(f32[12,256]{1,0:T(8,128)S(1)} %get-tuple-element.59), channel_id=1, source_target_pairs={{0,480},{32,64},{64,32},{96,128},{128,96},{160,192},{192,160},{224... | collective-permute-start | bytes 36872 | tf_op jit(solution)/shard_map/ppermute | solution.py:607
  37.3 6.5 %collective-permute-start.5 = (f32[12,256]{1,0:T(8,128)S(1)}, f32[12,256]{1,0:T(8,128)S(1)}, u32[]{:S(2)}, u32[]{:S(2)}) collective-permute-start(f32[12,256]{1,0:T(8,128)S(1)} %get-tuple-element.60), channel_id=1, source_target_pairs={{0,32},{32,0},{64,96},{96,64},{128,160},{160,128},{192,224},{224,1... | collective-permute-start | bytes 36872 | tf_op jit(solution)/shard_map/ppermute | solution.py:606
  44.7 10.8 %collective-permute-start.6 = (f32[12,256]{1,0:T(8,128)S(1)}, f32[12,256]{1,0:T(8,128)S(1)}, u32[]{:S(2)}, u32[]{:S(2)}) collective-permute-start(f32[12,256]{1,0:T(8,128)S(1)} %get-tuple-element.68), channel_id=1, source_target_pairs={{0,480},{32,64},{64,32},{96,128},{128,96},{160,192},{192,160},{224... | collective-permute-start | bytes 36872 | tf_op jit(solution)/shard_map/ppermute | solution.py:607
  51.4 6.5 %collective-permute-start.7 = (f32[12,256]{1,0:T(8,128)S(1)}, f32[12,256]{1,0:T(8,128)S(1)}, u32[]{:S(2)}, u32[]{:S(2)}) collective-permute-start(f32[12,256]{1,0:T(8,128)S(1)} %get-tuple-element.69), channel_id=1, source_target_pairs={{0,32},{32,0},{64,96},{96,64},{128,160},{160,128},{192,224},{224,1... | collective-permute-start | bytes 36872 | tf_op jit(solution)/shard_map/ppermute | solution.py:606
  58.0 7.5 %collective-permute-start.8 = (f32[42,256]{1,0:T(8,128)S(1)}, f32[42,256]{1,0:T(8,128)S(1)}, u32[]{:S(2)}, u32[]{:S(2)}) collective-permute-start(f32[42,256]{1,0:T(8,128)S(1)} %get-tuple-element.74), channel_id=1, source_target_pairs={{0,31},{1,2},{2,1},{3,4},{4,3},{5,6},{6,5},{7,8},{8,7},{9,10},{10,... | collective-permute-start | bytes 129032 | tf_op jit(solution)/shard_map/ppermute | solution.py:607
  59.9 5.6 %collective-permute-start.9 = (f32[42,256]{1,0:T(8,128)S(1)}, f32[42,256]{1,0:T(8,128)S(1)}, u32[]{:S(2)}, u32[]{:S(2)}) collective-permute-start(f32[42,256]{1,0:T(8,128)S(1)} %get-tuple-element.75), channel_id=1, source_target_pairs={{0,1},{1,0},{2,3},{3,2},{4,5},{5,4},{6,7},{7,6},{8,9},{9,8},{10,11... | collective-permute-start | bytes 129032 | tf_op jit(solution)/shard_map/ppermute | solution.py:606
  66.4 9.9 %collective-permute-start.10 = (f32[12,256]{1,0:T(8,128)S(1)}, f32[12,256]{1,0:T(8,128)S(1)}, u32[]{:S(2)}, u32[]{:S(2)}) collective-permute-start(f32[12,256]{1,0:T(8,128)S(1)} %get-tuple-element.81), channel_id=1, source_target_pairs={{0,480},{32,64},{64,32},{96,128},{128,96},{160,192},{192,160},{224... | collective-permute-start | bytes 36872 | tf_op jit(solution)/shard_map/ppermute | solution.py:607
  69.8 6.5 %collective-permute-start.11 = (f32[12,256]{1,0:T(8,128)S(1)}, f32[12,256]{1,0:T(8,128)S(1)}, u32[]{:S(2)}, u32[]{:S(2)}) collective-permute-start(f32[12,256]{1,0:T(8,128)S(1)} %get-tuple-element.82), channel_id=1, source_target_pairs={{0,32},{32,0},{64,96},{96,64},{128,160},{160,128},{192,224},{224,1... | collective-permute-start | bytes 36872 | tf_op jit(solution)/shard_map/ppermute | solution.py:606

commit v5 on v4

--- a/solution.py
+++ b/solution.py
@@ -269,7 +269,7 @@
     lax.fori_loop(0, 128 // CHUNK, run, 0, unroll=128 // CHUNK)
 
 
-def first_kernel(shifts_ref, vel_ref, code_ref, sums_ref, from_odd_ref, from_even_ref, both_ref, out_ref, ids_ref, far_ids_ref, new_ref, odd_ref, even_ref, mom_ref, work_ref, tot_ref, axis_ref, shift_ref, far_ref, turn_ref, left_ref, right_ref):
+def first_kernel(shifts_ref, sums_ref, from_odd_ref, from_even_ref, both_ref, joint_ref, _, ids_ref, far_ids_ref, shift_ref, new_ref, odd_ref, even_ref, next_ref, work_ref, tot_ref, far_ref, turn_ref, left_ref, right_ref):
     by_left, by_right = from_sides("gy", from_odd_ref[...], from_even_ref[...])
     left_ref[...] = by_left
     right_ref[...] = by_right
@@ -291,123 +291,98 @@
     axes = cell_axes(far_ids_ref[0:16, :])
     far_ref[...] = jnp.zeros_like(far_ref)
     store_cells(far_ref, shifts_of(means, axes), 10)
-    for table_ref in (shift_ref, axis_ref, turn_ref):
-        table_ref[...] = jnp.zeros_like(table_ref)
     own_cells(far_ref, shift_ref)
-    store_cells(axis_ref, cell_axes(ids_ref[0:8, :]))
-    for col, lanes in blocks():
-
-        def body(rows):
-            code = code_ref[col, rows, lanes]
-            masks = hop_masks(code, shifts_ref, 0)
-            vel = [vel_ref[comp * 2 + col, rows, lanes] for comp in range(3)]
-            turn = turned([pick(axis_ref, comp, col, lanes, masks) for comp in range(3)], vel)
-            filled = code >= 0
-            for comp in range(3):
-                value = turn[comp] + pick(shift_ref, comp, col, lanes, masks)
-                out_ref[comp * 2 + col, rows, lanes] = jnp.where(filled, value, 0.0)
-
-        over_slots(body)
-    mom_ref[...] = jnp.zeros_like(mom_ref)
-    deposit(out_ref, code_ref, shifts_ref, 1, mom_ref, True)
-    cell_sums(stored_moment(mom_ref), new_ref)
+    turn_ref[...] = jnp.zeros_like(turn_ref)
     zero = jnp.zeros((16, 256), F32)
     for k in range(3):
         unit = [zero + (1.0 if comp == k else 0.0) for comp in range(3)]
         store_cells(turn_ref.at[k], turned(axes, unit), 10)
     nested = nested_hops(0, shifts_ref)
+
+    def sources_of(cells, first, size):
+        tables = [far_ref] + [turn_ref.at[k] for k in range(3)]
+        return [(first + at * size, corner_differences(table, cells)) for at, table in enumerate(tables)]
+
+    for col in range(2):
+        sources = sources_of(((col + 1, col + 2), (col + 6, col + 7)), col * 27, 54)
+        for later in range(8):
+            row = (col * 8 + later) * 8
+            next_ref[row : row + 8, :] = joint_moment(joint_ref, sources, later, nested, (9, 3, 1))
+    cell_sums(stored_moment(next_ref), new_ref)
     for side, came_ref in enumerate((left_ref, right_ref)):
-        cells = side_cells(side)
-        sources = [(28, corner_differences(far_ref, cells))]
-        sources += [(46 + k * 18, corner_differences(turn_ref.at[k], cells)) for k in range(3)]
-        add_side(new_ref, side, came_ref, sources, nested)
+        add_side(new_ref, side, came_ref, sources_of(side_cells(side), 28, 18), nested)
     fill_messages_x(new_ref, 12, odd_ref, even_ref)
 
 
-def ghost_kernel(shifts_ref, vel_ref, code_ref, odd_ref, even_ref, left_ref, right_ref):
+def joint_sums(vel_ref, code_ref, shifts_ref, t, out_ref):
+    def classes(value, now, later):
+        out = []
+        for by_x in (value, jnp.where(now[0], value, 0), jnp.where(later[0], value, 0)):
+            out += [by_x, jnp.where(now[1], by_x, 0), jnp.where(later[1], by_x, 0)]
+        return out
+
+    def body(col, lanes, comp, counts, i, acc):
+        rows = pl.ds(pl.multiple_of(i * 8, 8), 8)
+        code = code_ref[col, rows, lanes]
+        now, later = hop_masks(code, shifts_ref, t), hop_masks(code, shifts_ref, t + 1)
+        out = []
+        if comp is not None:
+            for value in classes(vel_ref[comp * 2 + col, rows, lanes], now, later):
+                out += [value, jnp.where(now[2], value, 0.0), jnp.where(later[2], value, 0.0)]
+        if counts:
+            word = jnp.where(now[2], 1 + 256, 1) + jnp.where(later[2], 65536, 0)
+            out += classes(jnp.where(code >= 0, word, 0), now, later)
+        return tuple(a + b for a, b in zip(acc, out))
+
+    zero, none = (jnp.zeros((8, 128), F32),) * 27, (jnp.zeros((8, 128), jnp.int32),) * 9
     for col, lanes in blocks():
-        side_ref = right_ref if col else left_ref
-
-        def classes(value, now, later):
-            out = []
-            for by_x in (value, jnp.where(now[0], value, 0), jnp.where(later[0], value, 0)):
-                for by_y in (by_x, jnp.where(now[1], by_x, 0)):
-                    out.append(by_y)
-            return out
-
-        def body(comps, counts, i, acc):
-            rows = pl.ds(pl.multiple_of(i * 8, 8), 8)
-            code = code_ref[col, rows, lanes]
-            now, later = hop_masks(code, shifts_ref, 0), hop_masks(code, shifts_ref, 1)
-            kept = later[1] if col else jnp.logical_not(later[1])
-            out = []
-            for comp in comps:
-                for value in classes(jnp.where(kept, vel_ref[comp * 2 + col, rows, lanes], 0.0), now, later):
-                    out += [value, jnp.where(now[2], value, 0.0), jnp.where(later[2], value, 0.0)]
+        for comp, counts in ((None, True),) if vel_ref is None else ((0, False), (1, False), (2, True)):
+            start = (() if comp is None else zero) + (none if counts else ())
+            acc = lax.fori_loop(0, 16, functools.partial(body, col, lanes, comp, counts), start, unroll=8)
+            if comp is not None:
+                for at in range(27):
+                    row = 54 + comp * 54 + col * 27 + at
+                    out_ref[row : row + 1, lanes] = jnp.sum(acc[at], axis=0, keepdims=True)
             if counts:
-                word = jnp.where(now[2], 1 + 256, 1) + jnp.where(later[2], 65536, 0)
-                out += classes(jnp.where(jnp.logical_and(kept, code >= 0), word, 0), now, later)
-            return tuple(a + b for a, b in zip(acc, out))
-
-        zero, none = jnp.zeros((8, 128), F32), jnp.zeros((8, 128), jnp.int32)
-        for comps, counts in (((0, 1), False), ((2,), True)):
-            start = (zero,) * (18 * len(comps)) + ((none,) * 6 if counts else ())
-            acc = lax.fori_loop(0, 16, functools.partial(body, comps, counts), start, unroll=8)
-            for n, comp in enumerate(comps):
-                for at in range(18):
-                    row = 18 + comp * 18 + at
-                    side_ref[row : row + 1, lanes] = jnp.sum(acc[n * 18 + at], axis=0, keepdims=True)
-            if counts:
-                for at in range(6):
-                    word = acc[18 * len(comps) + at]
+                for at, word in enumerate(acc[-9:]):
                     for z in range(3):
                         part = lax.shift_right_logical(word, 8 * z) & 255
-                        row = at * 3 + z
-                        side_ref[row : row + 1, lanes] = jnp.sum(part.astype(F32), axis=0, keepdims=True)
+                        row = col * 27 + at * 3 + z
+                        out_ref[row : row + 1, lanes] = jnp.sum(part.astype(F32), axis=0, keepdims=True)
+
+
+def boundary_sums(joint_ref, kinds, nested, odd_ref, even_ref):
     odd = is_odd("gy")
-    odd_ref[...] = jnp.where(odd, right_ref[...], left_ref[...])
-    even_ref[...] = jnp.where(odd, left_ref[...], right_ref[...])
+    for kind in range(kinds):
+        for x in range(3):
+            for y in range(2):
+                for z in range(3):
+                    first = kind * 54 + x * 9 + z
+                    hopped = (nested[1] if y else 2) * 3
+                    left = joint_ref[first + y * 3 : first + y * 3 + 1, :] - joint_ref[pl.ds(first + hopped, 1), :]
+                    right = joint_ref[pl.ds(27 + first + hopped, 1), :]
+                    row = kind * 18 + x * 6 + y * 3 + z
+                    odd_ref[row : row + 1, :] = jnp.where(odd, right, left)
+                    even_ref[row : row + 1, :] = jnp.where(odd, left, right)
+
+
+def class_kernel(shifts_ref, vel_ref, code_ref, out_ref, odd_ref, even_ref):
+    joint_sums(vel_ref, code_ref, shifts_ref, 0, out_ref)
+    boundary_sums(out_ref, 4, nested_hops(0, shifts_ref), odd_ref, even_ref)
 
 
 def joint_kernel(shifts_ref, code_ref, first_ref, second_ref, odd_ref, even_ref):
-    for t, out_ref in ((1, first_ref), (2, second_ref)):
-        out_ref[...] = jnp.zeros_like(out_ref)
-        for col, lanes in blocks():
-
-            def body(i, acc):
-                rows = pl.ds(pl.multiple_of(i * 8, 8), 8)
-                code = code_ref[col, rows, lanes]
-                now, later = hop_masks(code, shifts_ref, t), hop_masks(code, shifts_ref, t + 1)
-                out, at = list(acc), 0
-                one = jnp.where(code >= 0, 1.0, 0.0)
-                for by_x in (one, jnp.where(now[0], one, 0.0), jnp.where(later[0], one, 0.0)):
-                    for by_y in (by_x, jnp.where(now[1], by_x, 0.0), jnp.where(later[1], by_x, 0.0)):
-                        for by_z in (by_y, jnp.where(now[2], by_y, 0.0), jnp.where(later[2], by_y, 0.0)):
-                            out[at] = out[at] + by_z
-                            at += 1
-                return tuple(out)
-
-            acc = lax.fori_loop(0, 16, body, (jnp.zeros((8, 128), F32),) * 27, unroll=2)
-            for at in range(27):
-                out_ref[col * 27 + at : col * 27 + at + 1, lanes] = jnp.sum(acc[at], axis=0, keepdims=True)
-    odd = is_odd("gy")
-    nested = nested_hops(WIDE_STEP, shifts_ref)
-    for x in range(3):
-        for y in range(2):
-            for z in range(3):
-                hopped = nested[1] if y else 2
-                left = second_ref[x * 9 + y * 3 + z : x * 9 + y * 3 + z + 1, :] - second_ref[pl.ds(x * 9 + hopped * 3 + z, 1), :]
-                right = second_ref[pl.ds(27 + x * 9 + hopped * 3 + z, 1), :]
-                row = x * 6 + y * 3 + z
-                odd_ref[row : row + 1, :] = jnp.where(odd, right, left)
-                even_ref[row : row + 1, :] = jnp.where(odd, left, right)
+    joint_sums(None, code_ref, shifts_ref, 1, first_ref)
+    joint_sums(None, code_ref, shifts_ref, 2, second_ref)
+    boundary_sums(second_ref, 1, nested_hops(WIDE_STEP, shifts_ref), odd_ref, even_ref)
 
 
 def turn_kernel(step, *refs):
+    shifts_ref, code_ref, ids_ref, vel_ref, last_ref, *refs = refs
     if step == 1:
-        shifts_ref, code_ref, ids_ref, vel_ref, *refs = refs
-    else:
-        shifts_ref, code_ref, ids_ref, vel_ref, last_ref, *refs = refs
+        *refs, before_ref = refs
+        before_ref[...] = jnp.zeros_like(before_ref)
+        store_cells(before_ref, cell_axes(ids_ref[0:8, :]))
     if step == WIDE_STEP:
         far_ids_ref, out_ref, axes_ref, sums_ref, table_ref, mom_ref = refs
         for comp, axis in enumerate(cell_axes(far_ids_ref[16:32, :])):
@@ -427,10 +402,11 @@
         def body(rows):
             code = code_ref[col, rows, lanes]
             vel = [vel_ref[comp * 2 + col, rows, lanes] for comp in range(3)]
-            if step > 1:
-                masks = hop_masks(code, shifts_ref, step - 1)
-                filled = code >= 0
-                vel = [jnp.where(filled, vel[comp] + pick(last_ref, comp, col, lanes, masks), 0.0) for comp in range(3)]
+            masks = hop_masks(code, shifts_ref, step - 1)
+            if step == 1:
+                vel = turned([pick(before_ref, comp, col, lanes, masks) for comp in range(3)], vel)
+            filled = code >= 0
+            vel = [jnp.where(filled, vel[comp] + pick(last_ref, comp, col, lanes, masks), 0.0) for comp in range(3)]
             masks = hop_masks(code, shifts_ref, step)
             turn = turned([pick(table_ref, comp, col, lanes, masks) for comp in range(3)], vel)
             for comp in range(3):
@@ -460,10 +436,10 @@
     return parts
 
 
-def shift_moment(joint_ref, first, parts, later, nested, weights=(9, 3, 1)):
+def joint_moment(joint_ref, sources, later, nested, weights):
     total = None
     for now in range(8):
-        at = first
+        at = 0
         for dim, (bit, weight) in enumerate(zip((4, 2, 1), weights)):
             if now & bit and later & bit:
                 at = at + nested[dim] * weight
@@ -471,8 +447,9 @@
                 at = at + weight
             elif later & bit:
                 at = at + 2 * weight
-        term = joint_ref[pl.ds(at, 1), :] * parts[now]
-        total = term if total is None else total + term
+        for first, parts in sources:
+            term = joint_ref[pl.ds(first + at, 1), :] * parts[now]
+            total = term if total is None else total + term
     return total
 
 
@@ -494,11 +471,7 @@
 
 def add_side(new_ref, side, came_ref, sources, nested):
     def moment_of(later):
-        total = None
-        for row, parts in sources:
-            term = shift_moment(came_ref, row, parts, later, nested, (6, 3, 1))
-            total = term if total is None else total + term
-        return total
+        return joint_moment(came_ref, sources, later, nested, (6, 3, 1))
 
     quads = []
     for moment in (0, 4):
@@ -519,7 +492,7 @@
         parts = corner_differences(shift_ref, ((col, col + 1), (3 + col, 4 + col)))
         for later in range(8):
             row = (col * 8 + later) * 8
-            next_ref[row : row + 8, :] = mom_ref[row : row + 8, :] + shift_moment(joint_ref, col * 27, parts, later, nested)
+            next_ref[row : row + 8, :] = mom_ref[row : row + 8, :] + joint_moment(joint_ref, [(col * 27, parts)], later, nested, (9, 3, 1))
     cell_sums(stored_moment(next_ref), new_ref)
     fill_messages_x(new_ref, 12, odd_ref, even_ref)
 
@@ -538,7 +511,7 @@
         parts = corner_differences(far_ref, ((col + 1, col + 2), (col + 6, col + 7)))
         for later in range(8):
             row = (col * 8 + later) * 8
-            next_ref[row : row + 8, :] = shift_moment(joint_ref, col * 27, parts, later, nested)
+            next_ref[row : row + 8, :] = joint_moment(joint_ref, [(col * 27, parts)], later, nested, (9, 3, 1))
     cell_sums(stored_moment(next_ref), new_ref)
     new_ref[...] = new_ref[...] + turned_ref[...]
     for side, came_ref in enumerate((left_ref, right_ref)):
@@ -632,24 +605,26 @@
     )(*(pltpu.with_memory_space_constraint(x, pltpu.HBM) for x in (shifts, vel_in, code_in, occ, ids_in)))
 
     from_odd, from_even = swap(odd, even, "gx")
-    ghost_odd, ghost_even = call(
-        ghost_kernel, "ghost", [SMEM, VMEM, VMEM], [rows(72), rows(72)], [room(72, 256), room(72, 256)], BYTES
+    classes, class_odd, class_even = call(
+        class_kernel, "classes", [SMEM, VMEM, VMEM], [rows(216), rows(72), rows(72)], [], BYTES
     )(shifts, vel, code)
     sums, both, odd, even = call(
         first_middle_kernel, "middle0", [VMEM] * 6, [rows(24), rows(16), rows(100), rows(100)], [],
-    )(sums, from_odd, from_even, ids_in, ghost_odd, ghost_even)
+    )(sums, from_odd, from_even, ids_in, class_odd, class_even)
     from_odd, from_even = swap(odd, even, "gy")
-    vel, ids, far_ids, sums, odd, even = call(
-        first_kernel, "first", [SMEM] + [VMEM] * 6, [vel_shape, rows(32), rows(32), rows(24), rows(12), rows(12)],
-        [moments, *wide_small, table, table, far, room(3, 2, 80, 256), room(100, 256), room(100, 256)],
-    )(shifts, vel, code, sums, from_odd, from_even, both)
-
-    shift = None
+    *joints, joint_odd, joint_even = call(
+        joint_kernel, "joint", [SMEM, VMEM], [rows(54), rows(54), rows(18), rows(18)], [], BYTES
+    )(shifts, code)
+    ids, far_ids, shift, sums, odd, even = call(
+        first_kernel, "first", [SMEM] + [VMEM] * 6, [rows(32), rows(32), table_shape, rows(24), rows(12), rows(12)],
+        [moments, *wide_small, far, room(3, 2, 80, 256), room(100, 256), room(100, 256)],
+    )(shifts, sums, from_odd, from_even, both, classes, joints[0])
+
     for step in range(1, ITERS):
         last, wide = step == ITERS - 1, step == WIDE_STEP
         from_odd, from_even = swap(odd, even, "gx")
-        args = [shifts, code, ids, vel] + ([] if step == 1 else [shift])
-        shapes, scratch = [vel_shape, axes_shape], [table]
+        args = [shifts, code, ids, vel, shift]
+        shapes, scratch = [vel_shape, axes_shape], [table] * (2 if step == 1 else 1)
         if wide:
             args.append(far_ids)
             shapes = [vel_shape, ((3, 16, 256), F32), rows(24)]
@@ -659,10 +634,6 @@
         vel, axes, *more = call(
             functools.partial(turn_kernel, step), f"turn{step}", [SMEM] + [VMEM] * (len(args) - 1), shapes, scratch, BYTES,
         )(*args)
-        if step == 1:
-            *joints, joint_odd, joint_even = call(
-                joint_kernel, "joint", [SMEM, VMEM], [rows(56), rows(56), rows(18), rows(18)], [], BYTES
-            )(shifts, code)
         if last:
             out, out_means = call(
                 last_kernel, "last", [SMEM] + [VMEM] * 6, [((6, 256, 128), jnp.bfloat16), ((3, 2, 256), F32)],

time: 78.7 us -> 77.5 us (0.985)
    pallas_call x3, Pallas kernels: 7.85 us -> 6.53 us  [the longest x1 3.33 us: on_device(): call(class_kernel, 'classes', [SMEM, VMEM, VMEM], [rows(216), rows(72), r...]
    ppermute x6, waiting for transfers between devices: 4.83 us -> 3.82 us  [swap(): from_even = lax.ppermute(even, axis, evens)]
  transfers between devices with their start and end apart: 12 -> 12, of which waited for: 7 -> 6; matrix products, arithmetic and copies ran while one was open for 0% -> 0% of each run, Pallas kernels for 13% -> 14%
where the time goes in v5:
time: 77.5 us; the launch traced here: 77 us
  starting transfers between devices  43.7 us (56%)
  Pallas kernels  18.7 us (24%)
  waiting for transfers between devices  13.8 us (18%)
  between operations  0.83 us (1%)
    ppermute x6, starting transfers between devices, swap(): from_odd = lax.ppermute(odd, axis, odds)  30.4 us
    ppermute x6, starting transfers between devices, swap(): from_even = lax.ppermute(even, axis, evens)  13.3 us
    ppermute x6, waiting for transfers between devices, swap(): from_odd = lax.ppermute(odd, axis, odds)  9.94 us
    pallas_call x3, Pallas kernels, on_device(): call(functools.partial(turn_kernel, step), f'turn{step}', [SMEM] + [VMEM]...  5.92 us
    ppermute x6, waiting for transfers between devices, swap(): from_even = lax.ppermute(even, axis, evens)  3.82 us
    pallas_call x1, Pallas kernels, on_device(): call(class_kernel, 'classes', [SMEM, VMEM, VMEM], [rows(216), rows(72), r...  3.33 us
    pallas_call x1, Pallas kernels, on_device(): call(start_kernel, 'start', [HBM] * 5, [vel_shape, code_shape, rows(24),...  2.55 us
    pallas_call x1, Pallas kernels, on_device(): call(last_kernel, 'last', [SMEM] + [VMEM] * 6, [((6, 256, 128), jnp.bfloa...  1.94 us
  transfers between devices with their start and end apart: 12, of which 6 were waited for; matrix products, arithmetic and copies ran while one was open for 0% of the time, Pallas kernels for 14%

profile of v5, /device:TPU:32, one launch (start us, length us, event | category | flops | bytes accessed | tf_op | source)
XLA Modules:
  0.0 77.0 jit_solution(10685968876431006630)
XLA Ops:
  0.6 2.5 %start.1 = (f32[6,128,256]{2,1,0:T(8,128)S(1)}, s32[2,128,256]{2,1,0:T(8,128)S(1)}, f32[24,256]{1,0:T(8,128)S(1)}, f32[20,256]{1,0:T(8,128)S(1)}, f32[20,256]{1,0:T(8,128)S(1)}) custom-call(s32[4,3]{1,0:T(4,128)} %shifts_ref.11, bf16[6,256,128]{2,1,0:T(8,128)(2,1)} %bitcast.12, s32[2,256,128]{2,1,0:T(8,128)} %bitcast.13, s32[2,256]{1,0:T(2,128)} %bitcast.14, ...), custom_call_target="tpu_custom_call" | custom-call | tf_op jit(solution)/shard_map/start/pallas_call | solution.py:602
  3.2 13.1 %collective-permute-start = (f32[20,256]{1,0:T(8,128)S(1)}, f32[20,256]{1,0:T(8,128)S(1)}, u32[]{:S(2)}, u32[]{:S(2)}) collective-permute-start(f32[20,256]{1,0:T(8,128)S(1)} %get-tuple-element.47), channel_id=1, source_target_pairs={{0,480},{32,64},{64,32},{96,128},{128,96},{160,192},{192,160},{224... | collective-permute-start | bytes 61448 | tf_op jit(solution)/shard_map/ppermute | solution.py:580
  16.3 0.0 copy-start
  16.3 1.9 %collective-permute-start.1 = (f32[20,256]{1,0:T(8,128)S(1)}, f32[20,256]{1,0:T(8,128)S(1)}, u32[]{:S(2)}, u32[]{:S(2)}) collective-permute-start(f32[20,256]{1,0:T(8,128)S(1)} %get-tuple-element.48), channel_id=1, source_target_pairs={{0,32},{32,0},{64,96},{96,64},{128,160},{160,128},{192,224},{224,1... | collective-permute-start | bytes 61448 | tf_op jit(solution)/shard_map/ppermute | solution.py:579
  18.3 0.0 copy-done
  18.3 0.0 copy-start.1
  18.3 3.3 %classes.1 = (f32[216,256]{1,0:T(8,128)S(1)}, f32[72,256]{1,0:T(8,128)S(1)}, f32[72,256]{1,0:T(8,128)S(1)}) custom-call(s32[4,3]{1,0:T(4,128)S(1)} %copy-done, f32[6,128,256]{2,1,0:T(8,128)S(1)} %get-tuple-element.49.vel_ref.refs_3_, s32[2,128,256]{2,1,0:T(8,128)S(1)} %get-tuple-element.45.code_ref.refs_1_), custom_call_target="tpu_custom_call" | custom-call | bytes 8000000 | tf_op jit(solution)/shard_map/classes/pallas_call | solution.py:608
  21.6 0.0 collective-permute-done.from_odd_ref
  21.6 1.3 %collective-permute-done.1.from_even_ref = f32[20,256]{1,0:T(8,128)S(1)} collective-permute-done((f32[20,256]{1,0:T(8,128)S(1)}, f32[20,256]{1,0:T(8,128)S(1)}, u32[]{:S(2)}, u32[]{:S(2)}) %collective-permute-start.1) | collective-permute-done | bytes 20512 | tf_op jit(solution)/shard_map/ppermute | solution.py:579
  23.0 0.0 copy-done.1
  23.0 1.9 %collective-permute-start.2 = (f32[100,256]{1,0:T(8,128)S(1)}, f32[100,256]{1,0:T(8,128)S(1)}, u32[]{:S(2)}, u32[]{:S(2)}) collective-permute-start(f32[100,256]{1,0:T(8,128)S(1)} %get-tuple-element.53), channel_id=1, source_target_pairs={{0,31},{1,2},{2,1},{3,4},{4,3},{5,6},{6,5},{7,8},{8,7},{9,10},{10,... | collective-permute-start | bytes 307208 | tf_op jit(solution)/shard_map/ppermute | solution.py:580
  24.9 3.5 %collective-permute-start.3 = (f32[100,256]{1,0:T(8,128)S(1)}, f32[100,256]{1,0:T(8,128)S(1)}, u32[]{:S(2)}, u32[]{:S(2)}) collective-permute-start(f32[100,256]{1,0:T(8,128)S(1)} %get-tuple-element.54), channel_id=1, source_target_pairs={{0,1},{1,0},{2,3},{3,2},{4,5},{5,4},{6,7},{7,6},{8,9},{9,8},{10,11... | collective-permute-start | bytes 307208 | tf_op jit(solution)/shard_map/ppermute | solution.py:579
  28.4 1.5 %joint.1 = (f32[54,256]{1,0:T(8,128)S(1)}, f32[54,256]{1,0:T(8,128)S(1)}, f32[18,256]{1,0:T(8,128)S(1)}, f32[18,256]{1,0:T(8,128)S(1)}) custom-call(s32[4,3]{1,0:T(4,128)S(1)} %copy-done, s32[2,128,256]{2,1,0:T(8,128)S(1)} %get-tuple-element.45.code_ref.refs_1_), custom_call_target="tpu_custom_call" | custom-call | bytes 8000000 | tf_op jit(solution)/shard_map/joint/pallas_call | solution.py:615
  30.0 1.2 %collective-permute-done.2.from_odd_ref = f32[100,256]{1,0:T(8,128)S(1)} collective-permute-done((f32[100,256]{1,0:T(8,128)S(1)}, f32[100,256]{1,0:T(8,128)S(1)}, u32[]{:S(2)}, u32[]{:S(2)}) %collective-permute-start.2) | collective-permute-done | bytes 102432 | tf_op jit(solution)/shard_map/ppermute | solution.py:580
  31.1 0.0 collective-permute-done.3.from_even_ref
  31.1 1.7 %first.1 = (f32[32,256]{1,0:T(8,128)S(1)}, f32[32,256]{1,0:T(8,128)S(1)}, f32[2,48,256]{2,1,0:T(8,128)S(1)}, f32[24,256]{1,0:T(8,128)S(1)}, f32[12,256]{1,0:T(8,128)S(1)}, /*index=5*/f32[12,256]{1,0:T(8,128)S(1)}) custom-call(s32[4,3]{1,0:T(4,128)S(1)} %copy-done, f32[24,256]{1,0:T(8,128)S(1)} %get-tuple-element.52.sums_ref, ...), custom_call_target="tpu_custom_call" | custom-call | tf_op jit(solution)/shard_map/first/pallas_call | solution.py:618
  32.8 3.3 %collective-permute-start.4 = (f32[12,256]{1,0:T(8,128)S(1)}, f32[12,256]{1,0:T(8,128)S(1)}, u32[]{:S(2)}, u32[]{:S(2)}) collective-permute-start(f32[12,256]{1,0:T(8,128)S(1)} %get-tuple-element.62), channel_id=1, source_target_pairs={{0,480},{32,64},{64,32},{96,128},{128,96},{160,192},{192,160},{224... | collective-permute-start | bytes 36872 | tf_op jit(solution)/shard_map/ppermute | solution.py:580
  36.1 2.1 %collective-permute-start.5 = (f32[12,256]{1,0:T(8,128)S(1)}, f32[12,256]{1,0:T(8,128)S(1)}, u32[]{:S(2)}, u32[]{:S(2)}) collective-permute-start(f32[12,256]{1,0:T(8,128)S(1)} %get-tuple-element.63), channel_id=1, source_target_pairs={{0,32},{32,0},{64,96},{96,64},{128,160},{160,128},{192,224},{224,1... | collective-permute-start | bytes 36872 | tf_op jit(solution)/shard_map/ppermute | solution.py:579
  38.2 2.4 %turn1.1 = (f32[6,128,256]{2,1,0:T(8,128)S(1)}, f32[3,8,256]{2,1,0:T(8,128)S(1)}, f32[128,256]{1,0:T(8,128)S(1)}) custom-call(s32[4,3]{1,0:T(4,128)S(1)} %copy-done, s32[2,128,256]{2,1,0:T(8,128)S(1)} %get-tuple-element.45.code_ref.refs_1_, f32[32,256]{1,0:T(8,128)S(1)} %get-tuple-element.58.refs_2_, f32[6,128,256]{2,1,0:T(8,128)S(1)} %get-tuple-element.49.vel_ref.refs_3_, ...), custom_call_target="tpu_custom_call" | custom-call | bytes 8000000 | tf_op jit(solution)/shard_map/turn1/pallas_call | solution.py:634
  40.6 2.0 %collective-permute-done.4.from_odd_ref = f32[12,256]{1,0:T(8,128)S(1)} collective-permute-done((f32[12,256]{1,0:T(8,128)S(1)}, f32[12,256]{1,0:T(8,128)S(1)}, u32[]{:S(2)}, u32[]{:S(2)}) %collective-permute-start.4) | collective-permute-done | bytes 12320 | tf_op jit(solution)/shard_map/ppermute | solution.py:580
  42.6 0.0 collective-permute-done.5.from_even_ref
  42.7 0.8 %shift1.1 = (f32[2,48,256]{2,1,0:T(8,128)S(1)}, f32[24,256]{1,0:T(8,128)S(1)}, f32[12,256]{1,0:T(8,128)S(1)}, f32[12,256]{1,0:T(8,128)S(1)}) custom-call(s32[4,3]{1,0:T(4,128)S(1)} %copy-done, f32[24,256]{1,0:T(8,128)S(1)} %get-tuple-element.61.sums_ref, f32[12,256]{1,0:T(8,128)S(1)} %collective-permute-done.4.from_odd_ref, ...), custom_call_target="tpu_custom_call" | custom-call | tf_op jit(solution)/shard_map/shift1/pallas_call | solution.py:653
  43.5 6.7 %collective-permute-start.6 = (f32[12,256]{1,0:T(8,128)S(1)}, f32[12,256]{1,0:T(8,128)S(1)}, u32[]{:S(2)}, u32[]{:S(2)}) collective-permute-start(f32[12,256]{1,0:T(8,128)S(1)} %get-tuple-element.70), channel_id=1, source_target_pairs={{0,480},{32,64},{64,32},{96,128},{128,96},{160,192},{192,160},{224... | collective-permute-start | bytes 36872 | tf_op jit(solution)/shard_map/ppermute | solution.py:580
  50.2 1.9 %collective-permute-start.7 = (f32[12,256]{1,0:T(8,128)S(1)}, f32[12,256]{1,0:T(8,128)S(1)}, u32[]{:S(2)}, u32[]{:S(2)}) collective-permute-start(f32[12,256]{1,0:T(8,128)S(1)} %get-tuple-element.71), channel_id=1, source_target_pairs={{0,32},{32,0},{64,96},{96,64},{128,160},{160,128},{192,224},{224,1... | collective-permute-start | bytes 36872 | tf_op jit(solution)/shard_map/ppermute | solution.py:579
  52.2 2.2 %turn2.1 = (f32[6,128,256]{2,1,0:T(8,128)S(1)}, f32[3,16,256]{2,1,0:T(8,128)S(1)}, f32[24,256]{1,0:T(8,128)S(1)}) custom-call(s32[4,3]{1,0:T(4,128)S(1)} %copy-done, s32[2,128,256]{2,1,0:T(8,128)S(1)} %get-tuple-element.45.code_ref.refs_1_, f32[32,256]{1,0:T(8,128)S(1)} %get-tuple-element.58.refs_2_, f32[6,128,256]{2,1,0:T(8,128)S(1)} %get-tuple-element.60.refs_3_, ...), custom_call_target="tpu_custom_call" | custom-call | bytes 8000000 | tf_op jit(solution)/shard_map/turn2/pallas_call | solution.py:634
  54.3 0.0 collective-permute-done.6.from_odd_ref
  54.3 2.4 %collective-permute-done.7.from_even_ref = f32[12,256]{1,0:T(8,128)S(1)} collective-permute-done((f32[12,256]{1,0:T(8,128)S(1)}, f32[12,256]{1,0:T(8,128)S(1)}, u32[]{:S(2)}, u32[]{:S(2)}) %collective-permute-start.7) | collective-permute-done | bytes 12320 | tf_op jit(solution)/shard_map/ppermute | solution.py:579
  56.8 1.9 %collective-permute-start.8 = (f32[42,256]{1,0:T(8,128)S(1)}, f32[42,256]{1,0:T(8,128)S(1)}, u32[]{:S(2)}, u32[]{:S(2)}) collective-permute-start(f32[42,256]{1,0:T(8,128)S(1)} %get-tuple-element.76), channel_id=1, source_target_pairs={{0,31},{1,2},{2,1},{3,4},{4,3},{5,6},{6,5},{7,8},{8,7},{9,10},{10,... | collective-permute-start | bytes 129032 | tf_op jit(solution)/shard_map/ppermute | solution.py:580
  58.7 2.0 %collective-permute-start.9 = (f32[42,256]{1,0:T(8,128)S(1)}, f32[42,256]{1,0:T(8,128)S(1)}, u32[]{:S(2)}, u32[]{:S(2)}) collective-permute-start(f32[42,256]{1,0:T(8,128)S(1)} %get-tuple-element.77), channel_id=1, source_target_pairs={{0,1},{1,0},{2,3},{3,2},{4,5},{5,4},{6,7},{7,6},{8,9},{9,8},{10,11... | collective-permute-start | bytes 129032 | tf_op jit(solution)/shard_map/ppermute | solution.py:579
  60.7 3.6 %collective-permute-done.8.from_odd_ref = f32[42,256]{1,0:T(8,128)S(1)} collective-permute-done((f32[42,256]{1,0:T(8,128)S(1)}, f32[42,256]{1,0:T(8,128)S(1)}, u32[]{:S(2)}, u32[]{:S(2)}) %collective-permute-start.8) | collective-permute-done | bytes 43040 | tf_op jit(solution)/shard_map/ppermute | solution.py:580
  64.3 0.0 collective-permute-done.9.from_even_ref
  64.3 0.9 %shift2.1 = (f32[2,48,256]{2,1,0:T(8,128)S(1)}, f32[24,256]{1,0:T(8,128)S(1)}, f32[12,256]{1,0:T(8,128)S(1)}, f32[12,256]{1,0:T(8,128)S(1)}) custom-call(s32[4,3]{1,0:T(4,128)S(1)} %copy-done, f32[24,256]{1,0:T(8,128)S(1)} %get-tuple-element.75.sums_ref, f32[42,256]{1,0:T(8,128)S(1)} %collective-permute-done.8.from_odd_ref, ...), custom_call_target="tpu_custom_call" | custom-call | tf_op jit(solution)/shard_map/shift2/pallas_call | solution.py:648
  65.2 3.3 %collective-permute-start.10 = (f32[12,256]{1,0:T(8,128)S(1)}, f32[12,256]{1,0:T(8,128)S(1)}, u32[]{:S(2)}, u32[]{:S(2)}) collective-permute-start(f32[12,256]{1,0:T(8,128)S(1)} %get-tuple-element.83), channel_id=1, source_target_pairs={{0,480},{32,64},{64,32},{96,128},{128,96},{160,192},{192,160},{224... | collective-permute-start | bytes 36872 | tf_op jit(solution)/shard_map/ppermute | solution.py:580
  68.6 1.9 %collective-permute-start.11 = (f32[12,256]{1,0:T(8,128)S(1)}, f32[12,256]{1,0:T(8,128)S(1)}, u32[]{:S(2)}, u32[]{:S(2)}) collective-permute-start(f32[12,256]{1,0:T(8,128)S(1)} %get-tuple-element.84), channel_id=1, source_target_pairs={{0,32},{32,0},{64,96},{96,64},{128,160},{160,128},{192,224},{224,1... | collective-permute-start | bytes 36872 | tf_op jit(solution)/shard_map/ppermute | solution.py:579
  70.5 1.4 %turn3.1 = (f32[6,128,256]{2,1,0:T(8,128)S(1)}, f32[3,8,256]{2,1,0:T(8,128)S(1)}) custom-call(s32[4,3]{1,0:T(4,128)S(1)} %copy-done, s32[2,128,256]{2,1,0:T(8,128)S(1)} %get-tuple-element.45.code_ref.refs_1_, f32[32,256]{1,0:T(8,128)S(1)} %get-tuple-element.58.refs_2_, f32[6,128,256]{2,1,0:T(8,128)S(1)} %get-tuple-element.68.refs_3_, ...), custom_call_target="tpu_custom_call" | custom-call | bytes 8000000 | tf_op jit(solution)/shard_map/turn3/pallas_call | solution.py:634
  71.9 3.2 %collective-permute-done.10.from_odd_ref = f32[12,256]{1,0:T(8,128)S(1)} collective-permute-done((f32[12,256]{1,0:T(8,128)S(1)}, f32[12,256]{1,0:T(8,128)S(1)}, u32[]{:S(2)}, u32[]{:S(2)}) %collective-permute-start.10) | collective-permute-done | bytes 12320 | tf_op jit(solution)/shard_map/ppermute | solution.py:580
  75.1 0.0 collective-permute-done.11.from_even_ref
  75.1 1.9 %last.1 = (bf16[6,256,128]{2,1,0:T(8,128)(2,1)}, f32[3,2,256]{2,1,0:T(2,128)}) custom-call(s32[4,3]{1,0:T(4,128)S(1)} %copy-done, s32[2,128,256]{2,1,0:T(8,128)S(1)} %get-tuple-element.45.code_ref.refs_1_, f32[6,128,256]{2,1,0:T(8,128)S(1)} %get-tuple-element.81.vel_ref, f32[24,256]{1,0:T(8,128)S(1)} %get-tuple-element.82.sums_ref, ...), custom_call_target="tpu_custom_call" | custom-call | tf_op jit(solution)/shard_map/last/pallas_call | solution.py:638
  (2 shorter events, 0.1 us)
Async XLA Ops:
  3.2 18.4 %collective-permute-start = (f32[20,256]{1,0:T(8,128)S(1)}, f32[20,256]{1,0:T(8,128)S(1)}, u32[]{:S(2)}, u32[]{:S(2)}) collective-permute-start(f32[20,256]{1,0:T(8,128)S(1)} %get-tuple-element.47), channel_id=1, source_target_pairs={{0,480},{32,64},{64,32},{96,128},{128,96},{160,192},{192,160},{224... | collective-permute-start | bytes 61448 | tf_op jit(solution)/shard_map/ppermute | solution.py:580
  16.3 1.9 %copy-start = (s32[4,3]{1,0:T(4,128)S(1)}, s32[4,3]{1,0:T(4,128)}, u32[]{:S(2)}) copy-start(s32[4,3]{1,0:T(4,128)} %shifts_ref.11) | copy-start | bytes 148
  16.3 6.6 %collective-permute-start.1 = (f32[20,256]{1,0:T(8,128)S(1)}, f32[20,256]{1,0:T(8,128)S(1)}, u32[]{:S(2)}, u32[]{:S(2)}) collective-permute-start(f32[20,256]{1,0:T(8,128)S(1)} %get-tuple-element.48), channel_id=1, source_target_pairs={{0,32},{32,0},{64,96},{96,64},{128,160},{160,128},{192,224},{224,1... | collective-permute-start | bytes 61448 | tf_op jit(solution)/shard_map/ppermute | solution.py:579
  18.3 4.7 %copy-start.1 = (s32[4,1,2,256]{3,2,1,0:T(2,128)S(1)}, s32[4,1,2,256]{3,2,1,0:T(2,128)}, u32[]{:S(2)}) copy-start(s32[4,1,2,256]{3,2,1,0:T(2,128)} %param.9) | copy-start | bytes 24580
  23.0 8.1 %collective-permute-start.2 = (f32[100,256]{1,0:T(8,128)S(1)}, f32[100,256]{1,0:T(8,128)S(1)}, u32[]{:S(2)}, u32[]{:S(2)}) collective-permute-start(f32[100,256]{1,0:T(8,128)S(1)} %get-tuple-element.53), channel_id=1, source_target_pairs={{0,31},{1,2},{2,1},{3,4},{4,3},{5,6},{6,5},{7,8},{8,7},{9,10},{10,... | collective-permute-start | bytes 307208 | tf_op jit(solution)/shard_map/ppermute | solution.py:580
  24.9 6.2 %collective-permute-start.3 = (f32[100,256]{1,0:T(8,128)S(1)}, f32[100,256]{1,0:T(8,128)S(1)}, u32[]{:S(2)}, u32[]{:S(2)}) collective-permute-start(f32[100,256]{1,0:T(8,128)S(1)} %get-tuple-element.54), channel_id=1, source_target_pairs={{0,1},{1,0},{2,3},{3,2},{4,5},{5,4},{6,7},{7,6},{8,9},{9,8},{10,11... | collective-permute-start | bytes 307208 | tf_op jit(solution)/shard_map/ppermute | solution.py:579
  32.8 9.8 %collective-permute-start.4 = (f32[12,256]{1,0:T(8,128)S(1)}, f32[12,256]{1,0:T(8,128)S(1)}, u32[]{:S(2)}, u32[]{:S(2)}) collective-permute-start(f32[12,256]{1,0:T(8,128)S(1)} %get-tuple-element.62), channel_id=1, source_target_pairs={{0,480},{32,64},{64,32},{96,128},{128,96},{160,192},{192,160},{224... | collective-permute-start | bytes 36872 | tf_op jit(solution)/shard_map/ppermute | solution.py:580
  36.1 6.5 %collective-permute-start.5 = (f32[12,256]{1,0:T(8,128)S(1)}, f32[12,256]{1,0:T(8,128)S(1)}, u32[]{:S(2)}, u32[]{:S(2)}) collective-permute-start(f32[12,256]{1,0:T(8,128)S(1)} %get-tuple-element.63), channel_id=1, source_target_pairs={{0,32},{32,0},{64,96},{96,64},{128,160},{160,128},{192,224},{224,1... | collective-permute-start | bytes 36872 | tf_op jit(solution)/shard_map/ppermute | solution.py:579
  43.5 10.8 %collective-permute-start.6 = (f32[12,256]{1,0:T(8,128)S(1)}, f32[12,256]{1,0:T(8,128)S(1)}, u32[]{:S(2)}, u32[]{:S(2)}) collective-permute-start(f32[12,256]{1,0:T(8,128)S(1)} %get-tuple-element.70), channel_id=1, source_target_pairs={{0,480},{32,64},{64,32},{96,128},{128,96},{160,192},{192,160},{224... | collective-permute-start | bytes 36872 | tf_op jit(solution)/shard_map/ppermute | solution.py:580
  50.2 6.5 %collective-permute-start.7 = (f32[12,256]{1,0:T(8,128)S(1)}, f32[12,256]{1,0:T(8,128)S(1)}, u32[]{:S(2)}, u32[]{:S(2)}) collective-permute-start(f32[12,256]{1,0:T(8,128)S(1)} %get-tuple-element.71), channel_id=1, source_target_pairs={{0,32},{32,0},{64,96},{96,64},{128,160},{160,128},{192,224},{224,1... | collective-permute-start | bytes 36872 | tf_op jit(solution)/shard_map/ppermute | solution.py:579
  56.8 7.5 %collective-permute-start.8 = (f32[42,256]{1,0:T(8,128)S(1)}, f32[42,256]{1,0:T(8,128)S(1)}, u32[]{:S(2)}, u32[]{:S(2)}) collective-permute-start(f32[42,256]{1,0:T(8,128)S(1)} %get-tuple-element.76), channel_id=1, source_target_pairs={{0,31},{1,2},{2,1},{3,4},{4,3},{5,6},{6,5},{7,8},{8,7},{9,10},{10,... | collective-permute-start | bytes 129032 | tf_op jit(solution)/shard_map/ppermute | solution.py:580
  58.7 5.6 %collective-permute-start.9 = (f32[42,256]{1,0:T(8,128)S(1)}, f32[42,256]{1,0:T(8,128)S(1)}, u32[]{:S(2)}, u32[]{:S(2)}) collective-permute-start(f32[42,256]{1,0:T(8,128)S(1)} %get-tuple-element.77), channel_id=1, source_target_pairs={{0,1},{1,0},{2,3},{3,2},{4,5},{5,4},{6,7},{7,6},{8,9},{9,8},{10,11... | collective-permute-start | bytes 129032 | tf_op jit(solution)/shard_map/ppermute | solution.py:579
  65.2 9.9 %collective-permute-start.10 = (f32[12,256]{1,0:T(8,128)S(1)}, f32[12,256]{1,0:T(8,128)S(1)}, u32[]{:S(2)}, u32[]{:S(2)}) collective-permute-start(f32[12,256]{1,0:T(8,128)S(1)} %get-tuple-element.83), channel_id=1, source_target_pairs={{0,480},{32,64},{64,32},{96,128},{128,96},{160,192},{192,160},{224... | collective-permute-start | bytes 36872 | tf_op jit(solution)/shard_map/ppermute | solution.py:580
  68.6 6.5 %collective-permute-start.11 = (f32[12,256]{1,0:T(8,128)S(1)}, f32[12,256]{1,0:T(8,128)S(1)}, u32[]{:S(2)}, u32[]{:S(2)}) collective-permute-start(f32[12,256]{1,0:T(8,128)S(1)} %get-tuple-element.84), channel_id=1, source_target_pairs={{0,32},{32,0},{64,96},{96,64},{128,160},{160,128},{192,224},{224,1... | collective-permute-start | bytes 36872 | tf_op jit(solution)/shard_map/ppermute | solution.py:579

commit v6 on v5

--- a/solution.py
+++ b/solution.py
@@ -38,10 +38,14 @@
     return lax.rem(lax.axis_index(axis), 2) == 1
 
 
-def hop_masks(code, shifts_ref, step):
-    hop_x = code >= (SUBDIV - shifts_ref[step, 0]) * (SUBDIV * SUBDIV)
-    hop_y = (code & (SUBDIV * SUBDIV - 1)) >= (SUBDIV - shifts_ref[step, 1]) * SUBDIV
-    hop_z = (code & (SUBDIV - 1)) >= SUBDIV - shifts_ref[step, 2]
+def hop_limits(shifts_ref, step):
+    return [(SUBDIV - shifts_ref[step, dim]) * SUBDIV ** (2 - dim) for dim in range(3)]
+
+
+def hop_masks(code, limits):
+    hop_x = code >= limits[0]
+    hop_y = (code & (SUBDIV * SUBDIV - 1)) >= limits[1]
+    hop_z = (code & (SUBDIV - 1)) >= limits[2]
     return hop_x, hop_y, hop_z
 
 
@@ -49,7 +53,7 @@
     def body(i, acc):
         rows = pl.ds(pl.multiple_of(i * 8, 8), 8)
         code = code_ref[col, rows, lanes]
-        hop_x, hop_y, hop_z = hop_masks(code, shifts_ref, step)
+        hop_x, hop_y, hop_z = hop_masks(code, hop_limits(shifts_ref, step))
         out = list(acc)
         for comp, value in enumerate(values(rows, code)):
             with_x = jnp.where(hop_x, value, 0.0)
@@ -321,10 +325,12 @@
             out += [by_x, jnp.where(now[1], by_x, 0), jnp.where(later[1], by_x, 0)]
         return out
 
+    now_limits, later_limits = hop_limits(shifts_ref, t), hop_limits(shifts_ref, t + 1)
+
     def body(col, lanes, comp, counts, i, acc):
         rows = pl.ds(pl.multiple_of(i * 8, 8), 8)
         code = code_ref[col, rows, lanes]
-        now, later = hop_masks(code, shifts_ref, t), hop_masks(code, shifts_ref, t + 1)
+        now, later = hop_masks(code, now_limits), hop_masks(code, later_limits)
         out = []
         if comp is not None:
             for value in classes(vel_ref[comp * 2 + col, rows, lanes], now, later):
@@ -402,12 +408,12 @@
         def body(rows):
             code = code_ref[col, rows, lanes]
             vel = [vel_ref[comp * 2 + col, rows, lanes] for comp in range(3)]
-            masks = hop_masks(code, shifts_ref, step - 1)
+            masks = hop_masks(code, hop_limits(shifts_ref, step - 1))
             if step == 1:
                 vel = turned([pick(before_ref, comp, col, lanes, masks) for comp in range(3)], vel)
             filled = code >= 0
             vel = [jnp.where(filled, vel[comp] + pick(last_ref, comp, col, lanes, masks), 0.0) for comp in range(3)]
-            masks = hop_masks(code, shifts_ref, step)
+            masks = hop_masks(code, hop_limits(shifts_ref, step))
             turn = turned([pick(table_ref, comp, col, lanes, masks) for comp in range(3)], vel)
             for comp in range(3):
                 out_ref[comp * 2 + col, rows, lanes] = turn[comp]
@@ -532,12 +538,13 @@
         means_ref[comp] = means[comp][0:2, :]
     saves = [pltpu.make_async_copy(means_ref, means_hbm, sems.at[6])]
     saves[0].start()
+    limits = hop_limits(shifts_ref, ITERS - 1)
     for col in range(2):
         for _, lanes in blocks((col,)):
 
             def body(rows):
                 code = code_ref[col, rows, lanes]
-                masks = hop_masks(code, shifts_ref, ITERS - 1)
+                masks = hop_masks(code, limits)
                 filled = code >= 0
                 for comp in range(3):
                     value = vel_ref[comp * 2 + col, rows, lanes] + pick(table_ref, comp, col, lanes, masks)
@@ -554,7 +561,6 @@
 
 
 VMEM = pl.BlockSpec(memory_space=pltpu.VMEM)
-SMEM = pl.BlockSpec(memory_space=pltpu.SMEM)
 HBM = pl.BlockSpec(memory_space=pltpu.HBM)
 BYTES = 8_000_000
 
@@ -606,17 +612,17 @@
 
     from_odd, from_even = swap(odd, even, "gx")
     classes, class_odd, class_even = call(
-        class_kernel, "classes", [SMEM, VMEM, VMEM], [rows(216), rows(72), rows(72)], [], BYTES
+        class_kernel, "classes", [VMEM] * 3, [rows(216), rows(72), rows(72)], [], BYTES
     )(shifts, vel, code)
     sums, both, odd, even = call(
         first_middle_kernel, "middle0", [VMEM] * 6, [rows(24), rows(16), rows(100), rows(100)], [],
     )(sums, from_odd, from_even, ids_in, class_odd, class_even)
     from_odd, from_even = swap(odd, even, "gy")
     *joints, joint_odd, joint_even = call(
-        joint_kernel, "joint", [SMEM, VMEM], [rows(54), rows(54), rows(18), rows(18)], [], BYTES
+        joint_kernel, "joint", [VMEM] * 2, [rows(54), rows(54), rows(18), rows(18)], [], BYTES
     )(shifts, code)
     ids, far_ids, shift, sums, odd, even = call(
-        first_kernel, "first", [SMEM] + [VMEM] * 6, [rows(32), rows(32), table_shape, rows(24), rows(12), rows(12)],
+        first_kernel, "first", [VMEM] * 7, [rows(32), rows(32), table_shape, rows(24), rows(12), rows(12)],
         [moments, *wide_small, far, room(3, 2, 80, 256), room(100, 256), room(100, 256)],
     )(shifts, sums, from_odd, from_even, both, classes, joints[0])
 
@@ -632,11 +638,11 @@
         elif not last:
             shapes.append(rows(128))
         vel, axes, *more = call(
-            functools.partial(turn_kernel, step), f"turn{step}", [SMEM] + [VMEM] * (len(args) - 1), shapes, scratch, BYTES,
+            functools.partial(turn_kernel, step), f"turn{step}", [VMEM] * len(args), shapes, scratch, BYTES,
         )(*args)
         if last:
             out, out_means = call(
-                last_kernel, "last", [SMEM] + [VMEM] * 6, [((6, 256, 128), jnp.bfloat16), ((3, 2, 256), F32)],
+                last_kernel, "last", [VMEM] * 7, [((6, 256, 128), jnp.bfloat16), ((3, 2, 256), F32)],
                 [*small, table, room(6, 128, 256), pltpu.VMEM((6, 256, 128), jnp.bfloat16), room(3, 2, 256), pltpu.SemaphoreType.DMA((7,))],
                 out_specs=[HBM, HBM],
             )(shifts, code, vel, sums, from_odd, from_even, axes)
@@ -646,12 +652,12 @@
             )(sums, from_odd, from_even, more[0], joint_odd, joint_even)
             from_odd, from_even = swap(odd, even, "gy")
             shift, sums, odd, even = call(
-                functools.partial(wide_shift_kernel, step), f"shift{step}", [SMEM] + [VMEM] * 6,
+                functools.partial(wide_shift_kernel, step), f"shift{step}", [VMEM] * 7,
                 [table_shape, rows(24), rows(12), rows(12)], [*wide_small, moments, far, room(42, 256), room(42, 256)],
             )(shifts, sums, from_odd, from_even, axes, more[0], joints[step - 1])
         else:
             shift, sums, odd, even = call(
-                functools.partial(shift_kernel, step), f"shift{step}", [SMEM] + [VMEM] * 6,
+                functools.partial(shift_kernel, step), f"shift{step}", [VMEM] * 7,
                 [table_shape, rows(24), rows(12), rows(12)], [*small, moments],
             )(shifts, sums, from_odd, from_even, axes, more[0], joints[step - 1])
     return out.reshape(velocity.shape), out_means.reshape(3, *occupancy.shape)

time: 77.5 us -> 75.3 us (0.972)
  Pallas kernels: 18.7 us -> 14.7 us
  waiting for transfers between devices: 13.8 us -> 15.7 us
    pallas_call x9, Pallas kernels: 16.1 us -> 12.1 us  [the longest x3 4.89 us: on_device(): call(functools.partial(turn_kernel, step), f'turn{step}', [VMEM] * len(ar...]
    ppermute x6, waiting for transfers between devices: 9.94 us -> 11.1 us  [swap(): from_odd = lax.ppermute(odd, axis, odds)]
    ppermute x6, waiting for transfers between devices: 3.82 us -> 4.64 us  [swap(): from_even = lax.ppermute(even, axis, evens)]
  transfers between devices with their start and end apart: 12 -> 12, of which waited for: 6 -> 6; matrix products, arithmetic and copies ran while one was open for 0% -> 0% of each run, Pallas kernels for 14% -> 12%
where the time goes in v6:
time: 75.3 us; the launch traced here: 74.8 us
  starting transfers between devices  43.5 us (58%)
  waiting for transfers between devices  15.7 us (21%)
  Pallas kernels  14.7 us (20%)
  between operations  0.81 us (1%)
    ppermute x6, starting transfers between devices, swap(): from_odd = lax.ppermute(odd, axis, odds)  30.4 us
    ppermute x6, starting transfers between devices, swap(): from_even = lax.ppermute(even, axis, evens)  13.2 us
    ppermute x6, waiting for transfers between devices, swap(): from_odd = lax.ppermute(odd, axis, odds)  11.1 us
    pallas_call x3, Pallas kernels, on_device(): call(functools.partial(turn_kernel, step), f'turn{step}', [VMEM] * len(ar...  4.89 us
    ppermute x6, waiting for transfers between devices, swap(): from_even = lax.ppermute(even, axis, evens)  4.64 us
    pallas_call x1, Pallas kernels, on_device(): call(class_kernel, 'classes', [VMEM] * 3, [rows(216), rows(72), rows(72)]...  2.97 us
    pallas_call x1, Pallas kernels, on_device(): call(start_kernel, 'start', [HBM] * 5, [vel_shape, code_shape, rows(24),...  2.55 us
  transfers between devices with their start and end apart: 12, of which 6 were waited for; matrix products, arithmetic and copies ran while one was open for 0% of the time, Pallas kernels for 12%

profile of v6, /device:TPU:32, one launch (start us, length us, event | category | flops | bytes accessed | tf_op | source)
XLA Modules:
  0.0 74.8 jit_solution(4182901882499390424)
XLA Ops:
  0.6 2.5 %start.1 = (f32[6,128,256]{2,1,0:T(8,128)S(1)}, s32[2,128,256]{2,1,0:T(8,128)S(1)}, f32[24,256]{1,0:T(8,128)S(1)}, f32[20,256]{1,0:T(8,128)S(1)}, f32[20,256]{1,0:T(8,128)S(1)}) custom-call(s32[4,3]{1,0:T(4,128)} %shifts_ref.11, bf16[6,256,128]{2,1,0:T(8,128)(2,1)} %bitcast.12, s32[2,256,128]{2,1,0:T(8,128)} %bitcast.13, s32[2,256]{1,0:T(2,128)} %bitcast.14, ...), custom_call_target="tpu_custom_call" | custom-call | tf_op jit(solution)/shard_map/start/pallas_call | solution.py:608
  3.2 13.1 %collective-permute-start = (f32[20,256]{1,0:T(8,128)S(1)}, f32[20,256]{1,0:T(8,128)S(1)}, u32[]{:S(2)}, u32[]{:S(2)}) collective-permute-start(f32[20,256]{1,0:T(8,128)S(1)} %get-tuple-element.47), channel_id=1, source_target_pairs={{0,480},{32,64},{64,32},{96,128},{128,96},{160,192},{192,160},{224... | collective-permute-start | bytes 61448 | tf_op jit(solution)/shard_map/ppermute | solution.py:586
  16.3 0.0 copy-start
  16.3 1.9 %collective-permute-start.1 = (f32[20,256]{1,0:T(8,128)S(1)}, f32[20,256]{1,0:T(8,128)S(1)}, u32[]{:S(2)}, u32[]{:S(2)}) collective-permute-start(f32[20,256]{1,0:T(8,128)S(1)} %get-tuple-element.48), channel_id=1, source_target_pairs={{0,32},{32,0},{64,96},{96,64},{128,160},{160,128},{192,224},{224,1... | collective-permute-start | bytes 61448 | tf_op jit(solution)/shard_map/ppermute | solution.py:585
  18.3 0.0 copy-done
  18.3 0.0 copy-start.1
  18.3 3.0 %classes.1 = (f32[216,256]{1,0:T(8,128)S(1)}, f32[72,256]{1,0:T(8,128)S(1)}, f32[72,256]{1,0:T(8,128)S(1)}) custom-call(s32[4,3]{1,0:T(4,128)S(1)} %copy-done, f32[6,128,256]{2,1,0:T(8,128)S(1)} %get-tuple-element.49.vel_ref.refs_3_, s32[2,128,256]{2,1,0:T(8,128)S(1)} %get-tuple-element.45.code_ref.refs_1_), custom_call_target="tpu_custom_call" | custom-call | bytes 8000000 | tf_op jit(solution)/shard_map/classes/pallas_call | solution.py:614
  21.3 0.0 collective-permute-done.from_odd_ref
  21.3 1.7 %collective-permute-done.1.from_even_ref = f32[20,256]{1,0:T(8,128)S(1)} collective-permute-done((f32[20,256]{1,0:T(8,128)S(1)}, f32[20,256]{1,0:T(8,128)S(1)}, u32[]{:S(2)}, u32[]{:S(2)}) %collective-permute-start.1) | collective-permute-done | bytes 20512 | tf_op jit(solution)/shard_map/ppermute | solution.py:585
  23.0 0.0 copy-done.1
  23.0 1.9 %collective-permute-start.2 = (f32[100,256]{1,0:T(8,128)S(1)}, f32[100,256]{1,0:T(8,128)S(1)}, u32[]{:S(2)}, u32[]{:S(2)}) collective-permute-start(f32[100,256]{1,0:T(8,128)S(1)} %get-tuple-element.53), channel_id=1, source_target_pairs={{0,31},{1,2},{2,1},{3,4},{4,3},{5,6},{6,5},{7,8},{8,7},{9,10},{10,... | collective-permute-start | bytes 307208 | tf_op jit(solution)/shard_map/ppermute | solution.py:586
  24.9 3.5 %collective-permute-start.3 = (f32[100,256]{1,0:T(8,128)S(1)}, f32[100,256]{1,0:T(8,128)S(1)}, u32[]{:S(2)}, u32[]{:S(2)}) collective-permute-start(f32[100,256]{1,0:T(8,128)S(1)} %get-tuple-element.54), channel_id=1, source_target_pairs={{0,1},{1,0},{2,3},{3,2},{4,5},{5,4},{6,7},{7,6},{8,9},{9,8},{10,11... | collective-permute-start | bytes 307208 | tf_op jit(solution)/shard_map/ppermute | solution.py:585
  28.4 1.2 %joint.1 = (f32[54,256]{1,0:T(8,128)S(1)}, f32[54,256]{1,0:T(8,128)S(1)}, f32[18,256]{1,0:T(8,128)S(1)}, f32[18,256]{1,0:T(8,128)S(1)}) custom-call(s32[4,3]{1,0:T(4,128)S(1)} %copy-done, s32[2,128,256]{2,1,0:T(8,128)S(1)} %get-tuple-element.45.code_ref.refs_1_), custom_call_target="tpu_custom_call" | custom-call | bytes 8000000 | tf_op jit(solution)/shard_map/joint/pallas_call | solution.py:621
  29.6 1.6 %collective-permute-done.2.from_odd_ref = f32[100,256]{1,0:T(8,128)S(1)} collective-permute-done((f32[100,256]{1,0:T(8,128)S(1)}, f32[100,256]{1,0:T(8,128)S(1)}, u32[]{:S(2)}, u32[]{:S(2)}) %collective-permute-start.2) | collective-permute-done | bytes 102432 | tf_op jit(solution)/shard_map/ppermute | solution.py:586
  31.1 0.0 collective-permute-done.3.from_even_ref
  31.1 1.1 %first.1 = (f32[32,256]{1,0:T(8,128)S(1)}, f32[32,256]{1,0:T(8,128)S(1)}, f32[2,48,256]{2,1,0:T(8,128)S(1)}, f32[24,256]{1,0:T(8,128)S(1)}, f32[12,256]{1,0:T(8,128)S(1)}, /*index=5*/f32[12,256]{1,0:T(8,128)S(1)}) custom-call(s32[4,3]{1,0:T(4,128)S(1)} %copy-done, f32[24,256]{1,0:T(8,128)S(1)} %get-tuple-element.52.sums_ref, ...), custom_call_target="tpu_custom_call" | custom-call | tf_op jit(solution)/shard_map/first/pallas_call | solution.py:624
  32.2 3.3 %collective-permute-start.4 = (f32[12,256]{1,0:T(8,128)S(1)}, f32[12,256]{1,0:T(8,128)S(1)}, u32[]{:S(2)}, u32[]{:S(2)}) collective-permute-start(f32[12,256]{1,0:T(8,128)S(1)} %get-tuple-element.62), channel_id=1, source_target_pairs={{0,480},{32,64},{64,32},{96,128},{128,96},{160,192},{192,160},{224... | collective-permute-start | bytes 36872 | tf_op jit(solution)/shard_map/ppermute | solution.py:586
  35.6 1.9 %collective-permute-start.5 = (f32[12,256]{1,0:T(8,128)S(1)}, f32[12,256]{1,0:T(8,128)S(1)}, u32[]{:S(2)}, u32[]{:S(2)}) collective-permute-start(f32[12,256]{1,0:T(8,128)S(1)} %get-tuple-element.63), channel_id=1, source_target_pairs={{0,32},{32,0},{64,96},{96,64},{128,160},{160,128},{192,224},{224,1... | collective-permute-start | bytes 36872 | tf_op jit(solution)/shard_map/ppermute | solution.py:585
  37.5 2.2 %turn1.1 = (f32[6,128,256]{2,1,0:T(8,128)S(1)}, f32[3,8,256]{2,1,0:T(8,128)S(1)}, f32[128,256]{1,0:T(8,128)S(1)}) custom-call(s32[4,3]{1,0:T(4,128)S(1)} %copy-done, s32[2,128,256]{2,1,0:T(8,128)S(1)} %get-tuple-element.45.code_ref.refs_1_, f32[32,256]{1,0:T(8,128)S(1)} %get-tuple-element.58.refs_2_, f32[6,128,256]{2,1,0:T(8,128)S(1)} %get-tuple-element.49.vel_ref.refs_3_, ...), custom_call_target="tpu_custom_call" | custom-call | bytes 8000000 | tf_op jit(solution)/shard_map/turn1/pallas_call | solution.py:640
  39.8 2.3 %collective-permute-done.4.from_odd_ref = f32[12,256]{1,0:T(8,128)S(1)} collective-permute-done((f32[12,256]{1,0:T(8,128)S(1)}, f32[12,256]{1,0:T(8,128)S(1)}, u32[]{:S(2)}, u32[]{:S(2)}) %collective-permute-start.4) | collective-permute-done | bytes 12320 | tf_op jit(solution)/shard_map/ppermute | solution.py:586
  42.1 0.0 collective-permute-done.5.from_even_ref
  42.1 0.3 shift1.1
  42.4 6.7 %collective-permute-start.6 = (f32[12,256]{1,0:T(8,128)S(1)}, f32[12,256]{1,0:T(8,128)S(1)}, u32[]{:S(2)}, u32[]{:S(2)}) collective-permute-start(f32[12,256]{1,0:T(8,128)S(1)} %get-tuple-element.70), channel_id=1, source_target_pairs={{0,480},{32,64},{64,32},{96,128},{128,96},{160,192},{192,160},{224... | collective-permute-start | bytes 36872 | tf_op jit(solution)/shard_map/ppermute | solution.py:586
  49.1 1.9 %collective-permute-start.7 = (f32[12,256]{1,0:T(8,128)S(1)}, f32[12,256]{1,0:T(8,128)S(1)}, u32[]{:S(2)}, u32[]{:S(2)}) collective-permute-start(f32[12,256]{1,0:T(8,128)S(1)} %get-tuple-element.71), channel_id=1, source_target_pairs={{0,32},{32,0},{64,96},{96,64},{128,160},{160,128},{192,224},{224,1... | collective-permute-start | bytes 36872 | tf_op jit(solution)/shard_map/ppermute | solution.py:585
  51.1 1.7 %turn2.1 = (f32[6,128,256]{2,1,0:T(8,128)S(1)}, f32[3,16,256]{2,1,0:T(8,128)S(1)}, f32[24,256]{1,0:T(8,128)S(1)}) custom-call(s32[4,3]{1,0:T(4,128)S(1)} %copy-done, s32[2,128,256]{2,1,0:T(8,128)S(1)} %get-tuple-element.45.code_ref.refs_1_, f32[32,256]{1,0:T(8,128)S(1)} %get-tuple-element.58.refs_2_, f32[6,128,256]{2,1,0:T(8,128)S(1)} %get-tuple-element.60.refs_3_, ...), custom_call_target="tpu_custom_call" | custom-call | bytes 8000000 | tf_op jit(solution)/shard_map/turn2/pallas_call | solution.py:640
  52.8 0.0 collective-permute-done.6.from_odd_ref
  52.8 2.9 %collective-permute-done.7.from_even_ref = f32[12,256]{1,0:T(8,128)S(1)} collective-permute-done((f32[12,256]{1,0:T(8,128)S(1)}, f32[12,256]{1,0:T(8,128)S(1)}, u32[]{:S(2)}, u32[]{:S(2)}) %collective-permute-start.7) | collective-permute-done | bytes 12320 | tf_op jit(solution)/shard_map/ppermute | solution.py:585
  55.7 1.9 %collective-permute-start.8 = (f32[42,256]{1,0:T(8,128)S(1)}, f32[42,256]{1,0:T(8,128)S(1)}, u32[]{:S(2)}, u32[]{:S(2)}) collective-permute-start(f32[42,256]{1,0:T(8,128)S(1)} %get-tuple-element.76), channel_id=1, source_target_pairs={{0,31},{1,2},{2,1},{3,4},{4,3},{5,6},{6,5},{7,8},{8,7},{9,10},{10,... | collective-permute-start | bytes 129032 | tf_op jit(solution)/shard_map/ppermute | solution.py:586
  57.6 2.0 %collective-permute-start.9 = (f32[42,256]{1,0:T(8,128)S(1)}, f32[42,256]{1,0:T(8,128)S(1)}, u32[]{:S(2)}, u32[]{:S(2)}) collective-permute-start(f32[42,256]{1,0:T(8,128)S(1)} %get-tuple-element.77), channel_id=1, source_target_pairs={{0,1},{1,0},{2,3},{3,2},{4,5},{5,4},{6,7},{7,6},{8,9},{9,8},{10,11... | collective-permute-start | bytes 129032 | tf_op jit(solution)/shard_map/ppermute | solution.py:585
  59.6 3.6 %collective-permute-done.8.from_odd_ref = f32[42,256]{1,0:T(8,128)S(1)} collective-permute-done((f32[42,256]{1,0:T(8,128)S(1)}, f32[42,256]{1,0:T(8,128)S(1)}, u32[]{:S(2)}, u32[]{:S(2)}) %collective-permute-start.8) | collective-permute-done | bytes 43040 | tf_op jit(solution)/shard_map/ppermute | solution.py:586
  63.2 0.0 collective-permute-done.9.from_even_ref
  63.2 0.3 shift2.1
  63.6 3.3 %collective-permute-start.10 = (f32[12,256]{1,0:T(8,128)S(1)}, f32[12,256]{1,0:T(8,128)S(1)}, u32[]{:S(2)}, u32[]{:S(2)}) collective-permute-start(f32[12,256]{1,0:T(8,128)S(1)} %get-tuple-element.83), channel_id=1, source_target_pairs={{0,480},{32,64},{64,32},{96,128},{128,96},{160,192},{192,160},{224... | collective-permute-start | bytes 36872 | tf_op jit(solution)/shard_map/ppermute | solution.py:586
  66.9 1.9 %collective-permute-start.11 = (f32[12,256]{1,0:T(8,128)S(1)}, f32[12,256]{1,0:T(8,128)S(1)}, u32[]{:S(2)}, u32[]{:S(2)}) collective-permute-start(f32[12,256]{1,0:T(8,128)S(1)} %get-tuple-element.84), channel_id=1, source_target_pairs={{0,32},{32,0},{64,96},{96,64},{128,160},{160,128},{192,224},{224,1... | collective-permute-start | bytes 36872 | tf_op jit(solution)/shard_map/ppermute | solution.py:585
  68.8 0.9 %turn3.1 = (f32[6,128,256]{2,1,0:T(8,128)S(1)}, f32[3,8,256]{2,1,0:T(8,128)S(1)}) custom-call(s32[4,3]{1,0:T(4,128)S(1)} %copy-done, s32[2,128,256]{2,1,0:T(8,128)S(1)} %get-tuple-element.45.code_ref.refs_1_, f32[32,256]{1,0:T(8,128)S(1)} %get-tuple-element.58.refs_2_, f32[6,128,256]{2,1,0:T(8,128)S(1)} %get-tuple-element.68.refs_3_, ...), custom_call_target="tpu_custom_call" | custom-call | bytes 8000000 | tf_op jit(solution)/shard_map/turn3/pallas_call | solution.py:640
  69.8 3.6 %collective-permute-done.10.from_odd_ref = f32[12,256]{1,0:T(8,128)S(1)} collective-permute-done((f32[12,256]{1,0:T(8,128)S(1)}, f32[12,256]{1,0:T(8,128)S(1)}, u32[]{:S(2)}, u32[]{:S(2)}) %collective-permute-start.10) | collective-permute-done | bytes 12320 | tf_op jit(solution)/shard_map/ppermute | solution.py:586
  73.4 0.0 collective-permute-done.11.from_even_ref
  73.4 1.4 %last.1 = (bf16[6,256,128]{2,1,0:T(8,128)(2,1)}, f32[3,2,256]{2,1,0:T(2,128)}) custom-call(s32[4,3]{1,0:T(4,128)S(1)} %copy-done, s32[2,128,256]{2,1,0:T(8,128)S(1)} %get-tuple-element.45.code_ref.refs_1_, f32[6,128,256]{2,1,0:T(8,128)S(1)} %get-tuple-element.81.vel_ref, f32[24,256]{1,0:T(8,128)S(1)} %get-tuple-element.82.sums_ref, ...), custom_call_target="tpu_custom_call" | custom-call | tf_op jit(solution)/shard_map/last/pallas_call | solution.py:644
  (2 shorter events, 0.1 us)
Async XLA Ops:
  3.2 18.1 %collective-permute-start = (f32[20,256]{1,0:T(8,128)S(1)}, f32[20,256]{1,0:T(8,128)S(1)}, u32[]{:S(2)}, u32[]{:S(2)}) collective-permute-start(f32[20,256]{1,0:T(8,128)S(1)} %get-tuple-element.47), channel_id=1, source_target_pairs={{0,480},{32,64},{64,32},{96,128},{128,96},{160,192},{192,160},{224... | collective-permute-start | bytes 61448 | tf_op jit(solution)/shard_map/ppermute | solution.py:586
  16.3 1.9 %copy-start = (s32[4,3]{1,0:T(4,128)S(1)}, s32[4,3]{1,0:T(4,128)}, u32[]{:S(2)}) copy-start(s32[4,3]{1,0:T(4,128)} %shifts_ref.11) | copy-start | bytes 148
  16.3 6.6 %collective-permute-start.1 = (f32[20,256]{1,0:T(8,128)S(1)}, f32[20,256]{1,0:T(8,128)S(1)}, u32[]{:S(2)}, u32[]{:S(2)}) collective-permute-start(f32[20,256]{1,0:T(8,128)S(1)} %get-tuple-element.48), channel_id=1, source_target_pairs={{0,32},{32,0},{64,96},{96,64},{128,160},{160,128},{192,224},{224,1... | collective-permute-start | bytes 61448 | tf_op jit(solution)/shard_map/ppermute | solution.py:585
  18.3 4.7 %copy-start.1 = (s32[4,1,2,256]{3,2,1,0:T(2,128)S(1)}, s32[4,1,2,256]{3,2,1,0:T(2,128)}, u32[]{:S(2)}) copy-start(s32[4,1,2,256]{3,2,1,0:T(2,128)} %param.9) | copy-start | bytes 24580
  23.0 8.1 %collective-permute-start.2 = (f32[100,256]{1,0:T(8,128)S(1)}, f32[100,256]{1,0:T(8,128)S(1)}, u32[]{:S(2)}, u32[]{:S(2)}) collective-permute-start(f32[100,256]{1,0:T(8,128)S(1)} %get-tuple-element.53), channel_id=1, source_target_pairs={{0,31},{1,2},{2,1},{3,4},{4,3},{5,6},{6,5},{7,8},{8,7},{9,10},{10,... | collective-permute-start | bytes 307208 | tf_op jit(solution)/shard_map/ppermute | solution.py:586
  24.9 6.2 %collective-permute-start.3 = (f32[100,256]{1,0:T(8,128)S(1)}, f32[100,256]{1,0:T(8,128)S(1)}, u32[]{:S(2)}, u32[]{:S(2)}) collective-permute-start(f32[100,256]{1,0:T(8,128)S(1)} %get-tuple-element.54), channel_id=1, source_target_pairs={{0,1},{1,0},{2,3},{3,2},{4,5},{5,4},{6,7},{7,6},{8,9},{9,8},{10,11... | collective-permute-start | bytes 307208 | tf_op jit(solution)/shard_map/ppermute | solution.py:585
  32.2 9.9 %collective-permute-start.4 = (f32[12,256]{1,0:T(8,128)S(1)}, f32[12,256]{1,0:T(8,128)S(1)}, u32[]{:S(2)}, u32[]{:S(2)}) collective-permute-start(f32[12,256]{1,0:T(8,128)S(1)} %get-tuple-element.62), channel_id=1, source_target_pairs={{0,480},{32,64},{64,32},{96,128},{128,96},{160,192},{192,160},{224... | collective-permute-start | bytes 36872 | tf_op jit(solution)/shard_map/ppermute | solution.py:586
  35.6 6.5 %collective-permute-start.5 = (f32[12,256]{1,0:T(8,128)S(1)}, f32[12,256]{1,0:T(8,128)S(1)}, u32[]{:S(2)}, u32[]{:S(2)}) collective-permute-start(f32[12,256]{1,0:T(8,128)S(1)} %get-tuple-element.63), channel_id=1, source_target_pairs={{0,32},{32,0},{64,96},{96,64},{128,160},{160,128},{192,224},{224,1... | collective-permute-start | bytes 36872 | tf_op jit(solution)/shard_map/ppermute | solution.py:585
  42.4 10.4 %collective-permute-start.6 = (f32[12,256]{1,0:T(8,128)S(1)}, f32[12,256]{1,0:T(8,128)S(1)}, u32[]{:S(2)}, u32[]{:S(2)}) collective-permute-start(f32[12,256]{1,0:T(8,128)S(1)} %get-tuple-element.70), channel_id=1, source_target_pairs={{0,480},{32,64},{64,32},{96,128},{128,96},{160,192},{192,160},{224... | collective-permute-start | bytes 36872 | tf_op jit(solution)/shard_map/ppermute | solution.py:586
  49.1 6.5 %collective-permute-start.7 = (f32[12,256]{1,0:T(8,128)S(1)}, f32[12,256]{1,0:T(8,128)S(1)}, u32[]{:S(2)}, u32[]{:S(2)}) collective-permute-start(f32[12,256]{1,0:T(8,128)S(1)} %get-tuple-element.71), channel_id=1, source_target_pairs={{0,32},{32,0},{64,96},{96,64},{128,160},{160,128},{192,224},{224,1... | collective-permute-start | bytes 36872 | tf_op jit(solution)/shard_map/ppermute | solution.py:585
  55.7 7.5 %collective-permute-start.8 = (f32[42,256]{1,0:T(8,128)S(1)}, f32[42,256]{1,0:T(8,128)S(1)}, u32[]{:S(2)}, u32[]{:S(2)}) collective-permute-start(f32[42,256]{1,0:T(8,128)S(1)} %get-tuple-element.76), channel_id=1, source_target_pairs={{0,31},{1,2},{2,1},{3,4},{4,3},{5,6},{6,5},{7,8},{8,7},{9,10},{10,... | collective-permute-start | bytes 129032 | tf_op jit(solution)/shard_map/ppermute | solution.py:586
  57.6 5.6 %collective-permute-start.9 = (f32[42,256]{1,0:T(8,128)S(1)}, f32[42,256]{1,0:T(8,128)S(1)}, u32[]{:S(2)}, u32[]{:S(2)}) collective-permute-start(f32[42,256]{1,0:T(8,128)S(1)} %get-tuple-element.77), channel_id=1, source_target_pairs={{0,1},{1,0},{2,3},{3,2},{4,5},{5,4},{6,7},{7,6},{8,9},{9,8},{10,11... | collective-permute-start | bytes 129032 | tf_op jit(solution)/shard_map/ppermute | solution.py:585
  63.6 9.8 %collective-permute-start.10 = (f32[12,256]{1,0:T(8,128)S(1)}, f32[12,256]{1,0:T(8,128)S(1)}, u32[]{:S(2)}, u32[]{:S(2)}) collective-permute-start(f32[12,256]{1,0:T(8,128)S(1)} %get-tuple-element.83), channel_id=1, source_target_pairs={{0,480},{32,64},{64,32},{96,128},{128,96},{160,192},{192,160},{224... | collective-permute-start | bytes 36872 | tf_op jit(solution)/shard_map/ppermute | solution.py:586
  66.9 6.5 %collective-permute-start.11 = (f32[12,256]{1,0:T(8,128)S(1)}, f32[12,256]{1,0:T(8,128)S(1)}, u32[]{:S(2)}, u32[]{:S(2)}) collective-permute-start(f32[12,256]{1,0:T(8,128)S(1)} %get-tuple-element.84), channel_id=1, source_target_pairs={{0,32},{32,0},{64,96},{96,64},{128,160},{160,128},{192,224},{224,1... | collective-permute-start | bytes 36872 | tf_op jit(solution)/shard_map/ppermute | solution.py:585

commit v7 on v6

--- a/solution.py
+++ b/solution.py
@@ -142,28 +142,26 @@
     fetch_shifts = pltpu.make_async_copy(shifts_hbm, shifts_ref, sems.at[10])
     fetch_occ = pltpu.make_async_copy(occ_hbm, occ_ref, sems.at[8])
     fetch_ids = pltpu.make_async_copy(ids_hbm, ids_ref, sems.at[9])
+    fetch_shifts.start()
+    fetch_occ.start()
     copies = []
     for col in range(2):
         copies.append(pltpu.make_async_copy(code_hbm.at[col], code_in_ref.at[col], sems.at[col]))
-    for at in range(6):
-        copies.append(pltpu.make_async_copy(vel_hbm.at[at], vel_in_ref.at[at], sems.at[2 + at]))
-    fetch_occ.start()
-    for at in (0, 2, 4, 6, 1, 3, 5, 7):
-        copies[at].start()
+        copies.append(pltpu.make_async_copy(vel_hbm.at[:, col], vel_in_ref.at[:, col], sems.at[2 + col]))
+    for copy in copies:
+        copy.start()
     fetch_ids.start()
-    fetch_shifts.start()
     mom_ref[...] = jnp.zeros_like(mom_ref)
     slot = lax.broadcasted_iota(jnp.int32, (128, 256), 0)
     fetch_occ.wait()
     fetch_shifts.wait()
     for col in range(2):
         filled = slot < occ_ref[col : col + 1, :]
-        copies[col].wait()
+        copies[2 * col].wait()
         code_ref[col] = jnp.where(filled, code_in_ref[col].T, -1)
+        copies[2 * col + 1].wait()
         for comp in range(3):
-            at = comp * 2 + col
-            copies[2 + at].wait()
-            vel_ref[at] = jnp.where(filled, vel_in_ref[at].astype(F32).T, 0.0)
+            vel_ref[comp * 2 + col] = jnp.where(filled, vel_in_ref[comp, col].astype(F32).T, 0.0)
         deposit(vel_ref, code_ref, shifts_ref, 0, mom_ref, True, (col,))
     fetch_ids.wait()
     for step in range(ITERS):
@@ -588,7 +586,7 @@
 
 
 def on_device(velocity, position_code, occupancy, shifts, axis_ids):
-    vel_in = velocity.reshape(6, 256, 128)
+    vel_in = velocity.reshape(3, 2, 256, 128)
     code_in = position_code.reshape(2, 256, 128)
     occ = occupancy.reshape(2, 256)
     ids_in = axis_ids.reshape(ITERS, 2, 256)
@@ -607,7 +605,7 @@
 
     vel, code, sums, odd, even = call(
         start_kernel, "start", [HBM] * 5, [vel_shape, code_shape, rows(24), rows(20), rows(20)],
-        [moments, pltpu.VMEM((6, 256, 128), jnp.bfloat16), pltpu.VMEM((2, 256, 128), jnp.int32), pltpu.VMEM((2, 256), jnp.int32), pltpu.VMEM((ITERS, 2, 256), jnp.int32), pltpu.SMEM((ITERS, 3), jnp.int32), pltpu.SemaphoreType.DMA((11,))],
+        [moments, pltpu.VMEM((3, 2, 256, 128), jnp.bfloat16), pltpu.VMEM((2, 256, 128), jnp.int32), pltpu.VMEM((2, 256), jnp.int32), pltpu.VMEM((ITERS, 2, 256), jnp.int32), pltpu.SMEM((ITERS, 3), jnp.int32), pltpu.SemaphoreType.DMA((11,))],
     )(*(pltpu.with_memory_space_constraint(x, pltpu.HBM) for x in (shifts, vel_in, code_in, occ, ids_in)))
 
     from_odd, from_even = swap(odd, even, "gx")

time: 75.3 us -> 74.9 us (level)
  no operation moved by 1% of the time
where the time goes in v7:
time: 74.9 us; the launch traced here: 74.5 us
  starting transfers between devices  43.5 us (58%)
  waiting for transfers between devices  15.7 us (21%)
  Pallas kernels  14.4 us (19%)
  between operations  0.81 us (1%)
    ppermute x6, starting transfers between devices, swap(): from_odd = lax.ppermute(odd, axis, odds)  30.4 us
    ppermute x6, starting transfers between devices, swap(): from_even = lax.ppermute(even, axis, evens)  13.2 us
    ppermute x6, waiting for transfers between devices, swap(): from_odd = lax.ppermute(odd, axis, odds)  11.1 us
    pallas_call x3, Pallas kernels, on_device(): call(functools.partial(turn_kernel, step), f'turn{step}', [VMEM] * len(ar...  4.89 us
    ppermute x6, waiting for transfers between devices, swap(): from_even = lax.ppermute(even, axis, evens)  4.64 us
    pallas_call x1, Pallas kernels, on_device(): call(class_kernel, 'classes', [VMEM] * 3, [rows(216), rows(72), rows(72)]...  2.97 us
    pallas_call x1, Pallas kernels, on_device(): call(start_kernel, 'start', [HBM] * 5, [vel_shape, code_shape, rows(24),...  2.22 us
  transfers between devices with their start and end apart: 12, of which 6 were waited for; matrix products, arithmetic and copies ran while one was open for 0% of the time, Pallas kernels for 12%

profile of v7, /device:TPU:32, one launch (start us, length us, event | category | flops | bytes accessed | tf_op | source)
XLA Modules:
  0.0 74.5 jit_solution(15135466691019759636)
XLA Ops:
  0.6 2.2 %start.1 = (f32[6,128,256]{2,1,0:T(8,128)S(1)}, s32[2,128,256]{2,1,0:T(8,128)S(1)}, f32[24,256]{1,0:T(8,128)S(1)}, f32[20,256]{1,0:T(8,128)S(1)}, f32[20,256]{1,0:T(8,128)S(1)}) custom-call(s32[4,3]{1,0:T(4,128)} %shifts_ref.11, bf16[3,2,256,128]{3,2,1,0:T(8,128)(2,1)} %bitcast.12, s32[2,256,128]{2,1,0:T(8,128)} %bitcast.13, s32[2,256]{1,0:T(2,128)} %bitcast.14, ...), custom_call_target="tpu_custom_call" | custom-call | tf_op jit(solution)/shard_map/start/pallas_call | solution.py:606
  2.9 13.1 %collective-permute-start = (f32[20,256]{1,0:T(8,128)S(1)}, f32[20,256]{1,0:T(8,128)S(1)}, u32[]{:S(2)}, u32[]{:S(2)}) collective-permute-start(f32[20,256]{1,0:T(8,128)S(1)} %get-tuple-element.47), channel_id=1, source_target_pairs={{0,480},{32,64},{64,32},{96,128},{128,96},{160,192},{192,160},{224... | collective-permute-start | bytes 61448 | tf_op jit(solution)/shard_map/ppermute | solution.py:584
  16.0 0.0 copy-start
  16.0 1.9 %collective-permute-start.1 = (f32[20,256]{1,0:T(8,128)S(1)}, f32[20,256]{1,0:T(8,128)S(1)}, u32[]{:S(2)}, u32[]{:S(2)}) collective-permute-start(f32[20,256]{1,0:T(8,128)S(1)} %get-tuple-element.48), channel_id=1, source_target_pairs={{0,32},{32,0},{64,96},{96,64},{128,160},{160,128},{192,224},{224,1... | collective-permute-start | bytes 61448 | tf_op jit(solution)/shard_map/ppermute | solution.py:583
  17.9 0.0 copy-done
  17.9 0.0 copy-start.1
  18.0 3.0 %classes.1 = (f32[216,256]{1,0:T(8,128)S(1)}, f32[72,256]{1,0:T(8,128)S(1)}, f32[72,256]{1,0:T(8,128)S(1)}) custom-call(s32[4,3]{1,0:T(4,128)S(1)} %copy-done, f32[6,128,256]{2,1,0:T(8,128)S(1)} %get-tuple-element.49.vel_ref.refs_3_, s32[2,128,256]{2,1,0:T(8,128)S(1)} %get-tuple-element.45.code_ref.refs_1_), custom_call_target="tpu_custom_call" | custom-call | bytes 8000000 | tf_op jit(solution)/shard_map/classes/pallas_call | solution.py:612
  20.9 0.0 collective-permute-done.from_odd_ref
  20.9 1.7 %collective-permute-done.1.from_even_ref = f32[20,256]{1,0:T(8,128)S(1)} collective-permute-done((f32[20,256]{1,0:T(8,128)S(1)}, f32[20,256]{1,0:T(8,128)S(1)}, u32[]{:S(2)}, u32[]{:S(2)}) %collective-permute-start.1) | collective-permute-done | bytes 20512 | tf_op jit(solution)/shard_map/ppermute | solution.py:583
  22.6 0.0 copy-done.1
  22.7 1.9 %collective-permute-start.2 = (f32[100,256]{1,0:T(8,128)S(1)}, f32[100,256]{1,0:T(8,128)S(1)}, u32[]{:S(2)}, u32[]{:S(2)}) collective-permute-start(f32[100,256]{1,0:T(8,128)S(1)} %get-tuple-element.53), channel_id=1, source_target_pairs={{0,31},{1,2},{2,1},{3,4},{4,3},{5,6},{6,5},{7,8},{8,7},{9,10},{10,... | collective-permute-start | bytes 307208 | tf_op jit(solution)/shard_map/ppermute | solution.py:584
  24.6 3.5 %collective-permute-start.3 = (f32[100,256]{1,0:T(8,128)S(1)}, f32[100,256]{1,0:T(8,128)S(1)}, u32[]{:S(2)}, u32[]{:S(2)}) collective-permute-start(f32[100,256]{1,0:T(8,128)S(1)} %get-tuple-element.54), channel_id=1, source_target_pairs={{0,1},{1,0},{2,3},{3,2},{4,5},{5,4},{6,7},{7,6},{8,9},{9,8},{10,11... | collective-permute-start | bytes 307208 | tf_op jit(solution)/shard_map/ppermute | solution.py:583
  28.1 1.2 %joint.1 = (f32[54,256]{1,0:T(8,128)S(1)}, f32[54,256]{1,0:T(8,128)S(1)}, f32[18,256]{1,0:T(8,128)S(1)}, f32[18,256]{1,0:T(8,128)S(1)}) custom-call(s32[4,3]{1,0:T(4,128)S(1)} %copy-done, s32[2,128,256]{2,1,0:T(8,128)S(1)} %get-tuple-element.45.code_ref.refs_1_), custom_call_target="tpu_custom_call" | custom-call | bytes 8000000 | tf_op jit(solution)/shard_map/joint/pallas_call | solution.py:619
  29.3 1.6 %collective-permute-done.2.from_odd_ref = f32[100,256]{1,0:T(8,128)S(1)} collective-permute-done((f32[100,256]{1,0:T(8,128)S(1)}, f32[100,256]{1,0:T(8,128)S(1)}, u32[]{:S(2)}, u32[]{:S(2)}) %collective-permute-start.2) | collective-permute-done | bytes 102432 | tf_op jit(solution)/shard_map/ppermute | solution.py:584
  30.8 0.0 collective-permute-done.3.from_even_ref
  30.8 1.1 %first.1 = (f32[32,256]{1,0:T(8,128)S(1)}, f32[32,256]{1,0:T(8,128)S(1)}, f32[2,48,256]{2,1,0:T(8,128)S(1)}, f32[24,256]{1,0:T(8,128)S(1)}, f32[12,256]{1,0:T(8,128)S(1)}, /*index=5*/f32[12,256]{1,0:T(8,128)S(1)}) custom-call(s32[4,3]{1,0:T(4,128)S(1)} %copy-done, f32[24,256]{1,0:T(8,128)S(1)} %get-tuple-element.52.sums_ref, ...), custom_call_target="tpu_custom_call" | custom-call | tf_op jit(solution)/shard_map/first/pallas_call | solution.py:622
  31.9 3.3 %collective-permute-start.4 = (f32[12,256]{1,0:T(8,128)S(1)}, f32[12,256]{1,0:T(8,128)S(1)}, u32[]{:S(2)}, u32[]{:S(2)}) collective-permute-start(f32[12,256]{1,0:T(8,128)S(1)} %get-tuple-element.62), channel_id=1, source_target_pairs={{0,480},{32,64},{64,32},{96,128},{128,96},{160,192},{192,160},{224... | collective-permute-start | bytes 36872 | tf_op jit(solution)/shard_map/ppermute | solution.py:584
  35.3 1.9 %collective-permute-start.5 = (f32[12,256]{1,0:T(8,128)S(1)}, f32[12,256]{1,0:T(8,128)S(1)}, u32[]{:S(2)}, u32[]{:S(2)}) collective-permute-start(f32[12,256]{1,0:T(8,128)S(1)} %get-tuple-element.63), channel_id=1, source_target_pairs={{0,32},{32,0},{64,96},{96,64},{128,160},{160,128},{192,224},{224,1... | collective-permute-start | bytes 36872 | tf_op jit(solution)/shard_map/ppermute | solution.py:583
  37.2 2.2 %turn1.1 = (f32[6,128,256]{2,1,0:T(8,128)S(1)}, f32[3,8,256]{2,1,0:T(8,128)S(1)}, f32[128,256]{1,0:T(8,128)S(1)}) custom-call(s32[4,3]{1,0:T(4,128)S(1)} %copy-done, s32[2,128,256]{2,1,0:T(8,128)S(1)} %get-tuple-element.45.code_ref.refs_1_, f32[32,256]{1,0:T(8,128)S(1)} %get-tuple-element.58.refs_2_, f32[6,128,256]{2,1,0:T(8,128)S(1)} %get-tuple-element.49.vel_ref.refs_3_, ...), custom_call_target="tpu_custom_call" | custom-call | bytes 8000000 | tf_op jit(solution)/shard_map/turn1/pallas_call | solution.py:638
  39.4 2.3 %collective-permute-done.4.from_odd_ref = f32[12,256]{1,0:T(8,128)S(1)} collective-permute-done((f32[12,256]{1,0:T(8,128)S(1)}, f32[12,256]{1,0:T(8,128)S(1)}, u32[]{:S(2)}, u32[]{:S(2)}) %collective-permute-start.4) | collective-permute-done | bytes 12320 | tf_op jit(solution)/shard_map/ppermute | solution.py:584
  41.8 0.0 collective-permute-done.5.from_even_ref
  41.8 0.3 shift1.1
  42.1 6.7 %collective-permute-start.6 = (f32[12,256]{1,0:T(8,128)S(1)}, f32[12,256]{1,0:T(8,128)S(1)}, u32[]{:S(2)}, u32[]{:S(2)}) collective-permute-start(f32[12,256]{1,0:T(8,128)S(1)} %get-tuple-element.70), channel_id=1, source_target_pairs={{0,480},{32,64},{64,32},{96,128},{128,96},{160,192},{192,160},{224... | collective-permute-start | bytes 36872 | tf_op jit(solution)/shard_map/ppermute | solution.py:584
  48.8 1.9 %collective-permute-start.7 = (f32[12,256]{1,0:T(8,128)S(1)}, f32[12,256]{1,0:T(8,128)S(1)}, u32[]{:S(2)}, u32[]{:S(2)}) collective-permute-start(f32[12,256]{1,0:T(8,128)S(1)} %get-tuple-element.71), channel_id=1, source_target_pairs={{0,32},{32,0},{64,96},{96,64},{128,160},{160,128},{192,224},{224,1... | collective-permute-start | bytes 36872 | tf_op jit(solution)/shard_map/ppermute | solution.py:583
  50.7 1.7 %turn2.1 = (f32[6,128,256]{2,1,0:T(8,128)S(1)}, f32[3,16,256]{2,1,0:T(8,128)S(1)}, f32[24,256]{1,0:T(8,128)S(1)}) custom-call(s32[4,3]{1,0:T(4,128)S(1)} %copy-done, s32[2,128,256]{2,1,0:T(8,128)S(1)} %get-tuple-element.45.code_ref.refs_1_, f32[32,256]{1,0:T(8,128)S(1)} %get-tuple-element.58.refs_2_, f32[6,128,256]{2,1,0:T(8,128)S(1)} %get-tuple-element.60.refs_3_, ...), custom_call_target="tpu_custom_call" | custom-call | bytes 8000000 | tf_op jit(solution)/shard_map/turn2/pallas_call | solution.py:638
  52.4 0.0 collective-permute-done.6.from_odd_ref
  52.4 2.9 %collective-permute-done.7.from_even_ref = f32[12,256]{1,0:T(8,128)S(1)} collective-permute-done((f32[12,256]{1,0:T(8,128)S(1)}, f32[12,256]{1,0:T(8,128)S(1)}, u32[]{:S(2)}, u32[]{:S(2)}) %collective-permute-start.7) | collective-permute-done | bytes 12320 | tf_op jit(solution)/shard_map/ppermute | solution.py:583
  55.4 1.9 %collective-permute-start.8 = (f32[42,256]{1,0:T(8,128)S(1)}, f32[42,256]{1,0:T(8,128)S(1)}, u32[]{:S(2)}, u32[]{:S(2)}) collective-permute-start(f32[42,256]{1,0:T(8,128)S(1)} %get-tuple-element.76), channel_id=1, source_target_pairs={{0,31},{1,2},{2,1},{3,4},{4,3},{5,6},{6,5},{7,8},{8,7},{9,10},{10,... | collective-permute-start | bytes 129032 | tf_op jit(solution)/shard_map/ppermute | solution.py:584
  57.3 2.0 %collective-permute-start.9 = (f32[42,256]{1,0:T(8,128)S(1)}, f32[42,256]{1,0:T(8,128)S(1)}, u32[]{:S(2)}, u32[]{:S(2)}) collective-permute-start(f32[42,256]{1,0:T(8,128)S(1)} %get-tuple-element.77), channel_id=1, source_target_pairs={{0,1},{1,0},{2,3},{3,2},{4,5},{5,4},{6,7},{7,6},{8,9},{9,8},{10,11... | collective-permute-start | bytes 129032 | tf_op jit(solution)/shard_map/ppermute | solution.py:583
  59.3 3.6 %collective-permute-done.8.from_odd_ref = f32[42,256]{1,0:T(8,128)S(1)} collective-permute-done((f32[42,256]{1,0:T(8,128)S(1)}, f32[42,256]{1,0:T(8,128)S(1)}, u32[]{:S(2)}, u32[]{:S(2)}) %collective-permute-start.8) | collective-permute-done | bytes 43040 | tf_op jit(solution)/shard_map/ppermute | solution.py:584
  62.9 0.0 collective-permute-done.9.from_even_ref
  62.9 0.3 shift2.1
  63.2 3.3 %collective-permute-start.10 = (f32[12,256]{1,0:T(8,128)S(1)}, f32[12,256]{1,0:T(8,128)S(1)}, u32[]{:S(2)}, u32[]{:S(2)}) collective-permute-start(f32[12,256]{1,0:T(8,128)S(1)} %get-tuple-element.83), channel_id=1, source_target_pairs={{0,480},{32,64},{64,32},{96,128},{128,96},{160,192},{192,160},{224... | collective-permute-start | bytes 36872 | tf_op jit(solution)/shard_map/ppermute | solution.py:584
  66.6 1.9 %collective-permute-start.11 = (f32[12,256]{1,0:T(8,128)S(1)}, f32[12,256]{1,0:T(8,128)S(1)}, u32[]{:S(2)}, u32[]{:S(2)}) collective-permute-start(f32[12,256]{1,0:T(8,128)S(1)} %get-tuple-element.84), channel_id=1, source_target_pairs={{0,32},{32,0},{64,96},{96,64},{128,160},{160,128},{192,224},{224,1... | collective-permute-start | bytes 36872 | tf_op jit(solution)/shard_map/ppermute | solution.py:583
  68.5 0.9 %turn3.1 = (f32[6,128,256]{2,1,0:T(8,128)S(1)}, f32[3,8,256]{2,1,0:T(8,128)S(1)}) custom-call(s32[4,3]{1,0:T(4,128)S(1)} %copy-done, s32[2,128,256]{2,1,0:T(8,128)S(1)} %get-tuple-element.45.code_ref.refs_1_, f32[32,256]{1,0:T(8,128)S(1)} %get-tuple-element.58.refs_2_, f32[6,128,256]{2,1,0:T(8,128)S(1)} %get-tuple-element.68.refs_3_, ...), custom_call_target="tpu_custom_call" | custom-call | bytes 8000000 | tf_op jit(solution)/shard_map/turn3/pallas_call | solution.py:638
  69.5 3.6 %collective-permute-done.10.from_odd_ref = f32[12,256]{1,0:T(8,128)S(1)} collective-permute-done((f32[12,256]{1,0:T(8,128)S(1)}, f32[12,256]{1,0:T(8,128)S(1)}, u32[]{:S(2)}, u32[]{:S(2)}) %collective-permute-start.10) | collective-permute-done | bytes 12320 | tf_op jit(solution)/shard_map/ppermute | solution.py:584
  73.1 0.0 collective-permute-done.11.from_even_ref
  73.1 1.4 %last.1 = (bf16[6,256,128]{2,1,0:T(8,128)(2,1)}, f32[3,2,256]{2,1,0:T(2,128)}) custom-call(s32[4,3]{1,0:T(4,128)S(1)} %copy-done, s32[2,128,256]{2,1,0:T(8,128)S(1)} %get-tuple-element.45.code_ref.refs_1_, f32[6,128,256]{2,1,0:T(8,128)S(1)} %get-tuple-element.81.vel_ref, f32[24,256]{1,0:T(8,128)S(1)} %get-tuple-element.82.sums_ref, ...), custom_call_target="tpu_custom_call" | custom-call | tf_op jit(solution)/shard_map/last/pallas_call | solution.py:642
  (2 shorter events, 0.1 us)
Async XLA Ops:
  2.9 18.1 %collective-permute-start = (f32[20,256]{1,0:T(8,128)S(1)}, f32[20,256]{1,0:T(8,128)S(1)}, u32[]{:S(2)}, u32[]{:S(2)}) collective-permute-start(f32[20,256]{1,0:T(8,128)S(1)} %get-tuple-element.47), channel_id=1, source_target_pairs={{0,480},{32,64},{64,32},{96,128},{128,96},{160,192},{192,160},{224... | collective-permute-start | bytes 61448 | tf_op jit(solution)/shard_map/ppermute | solution.py:584
  16.0 1.9 %copy-start = (s32[4,3]{1,0:T(4,128)S(1)}, s32[4,3]{1,0:T(4,128)}, u32[]{:S(2)}) copy-start(s32[4,3]{1,0:T(4,128)} %shifts_ref.11) | copy-start | bytes 148
  16.0 6.6 %collective-permute-start.1 = (f32[20,256]{1,0:T(8,128)S(1)}, f32[20,256]{1,0:T(8,128)S(1)}, u32[]{:S(2)}, u32[]{:S(2)}) collective-permute-start(f32[20,256]{1,0:T(8,128)S(1)} %get-tuple-element.48), channel_id=1, source_target_pairs={{0,32},{32,0},{64,96},{96,64},{128,160},{160,128},{192,224},{224,1... | collective-permute-start | bytes 61448 | tf_op jit(solution)/shard_map/ppermute | solution.py:583
  17.9 4.7 %copy-start.1 = (s32[4,1,2,256]{3,2,1,0:T(2,128)S(1)}, s32[4,1,2,256]{3,2,1,0:T(2,128)}, u32[]{:S(2)}) copy-start(s32[4,1,2,256]{3,2,1,0:T(2,128)} %param.9) | copy-start | bytes 24580
  22.7 8.1 %collective-permute-start.2 = (f32[100,256]{1,0:T(8,128)S(1)}, f32[100,256]{1,0:T(8,128)S(1)}, u32[]{:S(2)}, u32[]{:S(2)}) collective-permute-start(f32[100,256]{1,0:T(8,128)S(1)} %get-tuple-element.53), channel_id=1, source_target_pairs={{0,31},{1,2},{2,1},{3,4},{4,3},{5,6},{6,5},{7,8},{8,7},{9,10},{10,... | collective-permute-start | bytes 307208 | tf_op jit(solution)/shard_map/ppermute | solution.py:584
  24.6 6.2 %collective-permute-start.3 = (f32[100,256]{1,0:T(8,128)S(1)}, f32[100,256]{1,0:T(8,128)S(1)}, u32[]{:S(2)}, u32[]{:S(2)}) collective-permute-start(f32[100,256]{1,0:T(8,128)S(1)} %get-tuple-element.54), channel_id=1, source_target_pairs={{0,1},{1,0},{2,3},{3,2},{4,5},{5,4},{6,7},{7,6},{8,9},{9,8},{10,11... | collective-permute-start | bytes 307208 | tf_op jit(solution)/shard_map/ppermute | solution.py:583
  31.9 9.9 %collective-permute-start.4 = (f32[12,256]{1,0:T(8,128)S(1)}, f32[12,256]{1,0:T(8,128)S(1)}, u32[]{:S(2)}, u32[]{:S(2)}) collective-permute-start(f32[12,256]{1,0:T(8,128)S(1)} %get-tuple-element.62), channel_id=1, source_target_pairs={{0,480},{32,64},{64,32},{96,128},{128,96},{160,192},{192,160},{224... | collective-permute-start | bytes 36872 | tf_op jit(solution)/shard_map/ppermute | solution.py:584
  35.3 6.5 %collective-permute-start.5 = (f32[12,256]{1,0:T(8,128)S(1)}, f32[12,256]{1,0:T(8,128)S(1)}, u32[]{:S(2)}, u32[]{:S(2)}) collective-permute-start(f32[12,256]{1,0:T(8,128)S(1)} %get-tuple-element.63), channel_id=1, source_target_pairs={{0,32},{32,0},{64,96},{96,64},{128,160},{160,128},{192,224},{224,1... | collective-permute-start | bytes 36872 | tf_op jit(solution)/shard_map/ppermute | solution.py:583
  42.1 10.4 %collective-permute-start.6 = (f32[12,256]{1,0:T(8,128)S(1)}, f32[12,256]{1,0:T(8,128)S(1)}, u32[]{:S(2)}, u32[]{:S(2)}) collective-permute-start(f32[12,256]{1,0:T(8,128)S(1)} %get-tuple-element.70), channel_id=1, source_target_pairs={{0,480},{32,64},{64,32},{96,128},{128,96},{160,192},{192,160},{224... | collective-permute-start | bytes 36872 | tf_op jit(solution)/shard_map/ppermute | solution.py:584
  48.8 6.5 %collective-permute-start.7 = (f32[12,256]{1,0:T(8,128)S(1)}, f32[12,256]{1,0:T(8,128)S(1)}, u32[]{:S(2)}, u32[]{:S(2)}) collective-permute-start(f32[12,256]{1,0:T(8,128)S(1)} %get-tuple-element.71), channel_id=1, source_target_pairs={{0,32},{32,0},{64,96},{96,64},{128,160},{160,128},{192,224},{224,1... | collective-permute-start | bytes 36872 | tf_op jit(solution)/shard_map/ppermute | solution.py:583
  55.4 7.5 %collective-permute-start.8 = (f32[42,256]{1,0:T(8,128)S(1)}, f32[42,256]{1,0:T(8,128)S(1)}, u32[]{:S(2)}, u32[]{:S(2)}) collective-permute-start(f32[42,256]{1,0:T(8,128)S(1)} %get-tuple-element.76), channel_id=1, source_target_pairs={{0,31},{1,2},{2,1},{3,4},{4,3},{5,6},{6,5},{7,8},{8,7},{9,10},{10,... | collective-permute-start | bytes 129032 | tf_op jit(solution)/shard_map/ppermute | solution.py:584
  57.3 5.6 %collective-permute-start.9 = (f32[42,256]{1,0:T(8,128)S(1)}, f32[42,256]{1,0:T(8,128)S(1)}, u32[]{:S(2)}, u32[]{:S(2)}) collective-permute-start(f32[42,256]{1,0:T(8,128)S(1)} %get-tuple-element.77), channel_id=1, source_target_pairs={{0,1},{1,0},{2,3},{3,2},{4,5},{5,4},{6,7},{7,6},{8,9},{9,8},{10,11... | collective-permute-start | bytes 129032 | tf_op jit(solution)/shard_map/ppermute | solution.py:583
  63.2 9.8 %collective-permute-start.10 = (f32[12,256]{1,0:T(8,128)S(1)}, f32[12,256]{1,0:T(8,128)S(1)}, u32[]{:S(2)}, u32[]{:S(2)}) collective-permute-start(f32[12,256]{1,0:T(8,128)S(1)} %get-tuple-element.83), channel_id=1, source_target_pairs={{0,480},{32,64},{64,32},{96,128},{128,96},{160,192},{192,160},{224... | collective-permute-start | bytes 36872 | tf_op jit(solution)/shard_map/ppermute | solution.py:584
  66.6 6.5 %collective-permute-start.11 = (f32[12,256]{1,0:T(8,128)S(1)}, f32[12,256]{1,0:T(8,128)S(1)}, u32[]{:S(2)}, u32[]{:S(2)}) collective-permute-start(f32[12,256]{1,0:T(8,128)S(1)} %get-tuple-element.84), channel_id=1, source_target_pairs={{0,32},{32,0},{64,96},{96,64},{128,160},{160,128},{192,224},{224,1... | collective-permute-start | bytes 36872 | tf_op jit(solution)/shard_map/ppermute | solution.py:583

commit v8 on v7

--- a/solution.py
+++ b/solution.py
@@ -534,7 +534,7 @@
     store_cells(table_ref, [means[comp] - turn[comp] for comp in range(3)])
     for comp in range(3):
         means_ref[comp] = means[comp][0:2, :]
-    saves = [pltpu.make_async_copy(means_ref, means_hbm, sems.at[6])]
+    saves = [pltpu.make_async_copy(means_ref, means_hbm, sems.at[2])]
     saves[0].start()
     limits = hop_limits(shifts_ref, ITERS - 1)
     for col in range(2):
@@ -550,10 +550,9 @@
 
             over_slots(body)
         for comp in range(3):
-            at = comp * 2 + col
-            out_ref[at] = end_ref[at].T.astype(jnp.bfloat16)
-            saves.append(pltpu.make_async_copy(out_ref.at[at], out_hbm.at[at], sems.at[at]))
-            saves[-1].start()
+            out_ref[comp, col] = end_ref[comp * 2 + col].T.astype(jnp.bfloat16)
+        saves.append(pltpu.make_async_copy(out_ref.at[:, col], out_hbm.at[:, col], sems.at[col]))
+        saves[-1].start()
     for save in saves:
         save.wait()
 
@@ -640,8 +639,8 @@
         )(*args)
         if last:
             out, out_means = call(
-                last_kernel, "last", [VMEM] * 7, [((6, 256, 128), jnp.bfloat16), ((3, 2, 256), F32)],
-                [*small, table, room(6, 128, 256), pltpu.VMEM((6, 256, 128), jnp.bfloat16), room(3, 2, 256), pltpu.SemaphoreType.DMA((7,))],
+                last_kernel, "last", [VMEM] * 7, [((3, 2, 256, 128), jnp.bfloat16), ((3, 2, 256), F32)],
+                [*small, table, room(6, 128, 256), pltpu.VMEM((3, 2, 256, 128), jnp.bfloat16), room(3, 2, 256), pltpu.SemaphoreType.DMA((3,))],
                 out_specs=[HBM, HBM],
             )(shifts, code, vel, sums, from_odd, from_even, axes)
         elif wide:

time: 74.9 us -> 74.9 us (level)
  no operation moved by 1% of the time
where the time goes in v8:
time: 74.9 us; the launch traced here: 74.5 us
  starting transfers between devices  43.5 us (58%)
  waiting for transfers between devices  15.7 us (21%)
  Pallas kernels  14.4 us (19%)
  between operations  0.81 us (1%)
    ppermute x6, starting transfers between devices, swap(): from_odd = lax.ppermute(odd, axis, odds)  30.4 us
    ppermute x6, starting transfers between devices, swap(): from_even = lax.ppermute(even, axis, evens)  13.2 us
    ppermute x6, waiting for transfers between devices, swap(): from_odd = lax.ppermute(odd, axis, odds)  11.1 us
    pallas_call x3, Pallas kernels, on_device(): call(functools.partial(turn_kernel, step), f'turn{step}', [VMEM] * len(ar...  4.89 us
    ppermute x6, waiting for transfers between devices, swap(): from_even = lax.ppermute(even, axis, evens)  4.64 us
    pallas_call x1, Pallas kernels, on_device(): call(class_kernel, 'classes', [VMEM] * 3, [rows(216), rows(72), rows(72)]...  2.97 us
    pallas_call x1, Pallas kernels, on_device(): call(start_kernel, 'start', [HBM] * 5, [vel_shape, code_shape, rows(24),...  2.22 us
  transfers between devices with their start and end apart: 12, of which 6 were waited for; matrix products, arithmetic and copies ran while one was open for 0% of the time, Pallas kernels for 12%

profile of v8, /device:TPU:32, one launch (start us, length us, event | category | flops | bytes accessed | tf_op | source)
XLA Modules:
  0.0 74.5 jit_solution(3533981702973902031)
XLA Ops:
  0.6 2.2 %start.1 = (f32[6,128,256]{2,1,0:T(8,128)S(1)}, s32[2,128,256]{2,1,0:T(8,128)S(1)}, f32[24,256]{1,0:T(8,128)S(1)}, f32[20,256]{1,0:T(8,128)S(1)}, f32[20,256]{1,0:T(8,128)S(1)}) custom-call(s32[4,3]{1,0:T(4,128)} %shifts_ref.11, bf16[3,2,256,128]{3,2,1,0:T(8,128)(2,1)} %bitcast.12, s32[2,256,128]{2,1,0:T(8,128)} %bitcast.13, s32[2,256]{1,0:T(2,128)} %bitcast.14, ...), custom_call_target="tpu_custom_call" | custom-call | tf_op jit(solution)/shard_map/start/pallas_call | solution.py:605
  2.9 13.1 %collective-permute-start = (f32[20,256]{1,0:T(8,128)S(1)}, f32[20,256]{1,0:T(8,128)S(1)}, u32[]{:S(2)}, u32[]{:S(2)}) collective-permute-start(f32[20,256]{1,0:T(8,128)S(1)} %get-tuple-element.47), channel_id=1, source_target_pairs={{0,480},{32,64},{64,32},{96,128},{128,96},{160,192},{192,160},{224... | collective-permute-start | bytes 61448 | tf_op jit(solution)/shard_map/ppermute | solution.py:583
  16.0 0.0 copy-start
  16.0 1.9 %collective-permute-start.1 = (f32[20,256]{1,0:T(8,128)S(1)}, f32[20,256]{1,0:T(8,128)S(1)}, u32[]{:S(2)}, u32[]{:S(2)}) collective-permute-start(f32[20,256]{1,0:T(8,128)S(1)} %get-tuple-element.48), channel_id=1, source_target_pairs={{0,32},{32,0},{64,96},{96,64},{128,160},{160,128},{192,224},{224,1... | collective-permute-start | bytes 61448 | tf_op jit(solution)/shard_map/ppermute | solution.py:582
  17.9 0.0 copy-done
  17.9 0.0 copy-start.1
  18.0 3.0 %classes.1 = (f32[216,256]{1,0:T(8,128)S(1)}, f32[72,256]{1,0:T(8,128)S(1)}, f32[72,256]{1,0:T(8,128)S(1)}) custom-call(s32[4,3]{1,0:T(4,128)S(1)} %copy-done, f32[6,128,256]{2,1,0:T(8,128)S(1)} %get-tuple-element.49.vel_ref.refs_3_, s32[2,128,256]{2,1,0:T(8,128)S(1)} %get-tuple-element.45.code_ref.refs_1_), custom_call_target="tpu_custom_call" | custom-call | bytes 8000000 | tf_op jit(solution)/shard_map/classes/pallas_call | solution.py:611
  20.9 0.0 collective-permute-done.from_odd_ref
  20.9 1.7 %collective-permute-done.1.from_even_ref = f32[20,256]{1,0:T(8,128)S(1)} collective-permute-done((f32[20,256]{1,0:T(8,128)S(1)}, f32[20,256]{1,0:T(8,128)S(1)}, u32[]{:S(2)}, u32[]{:S(2)}) %collective-permute-start.1) | collective-permute-done | bytes 20512 | tf_op jit(solution)/shard_map/ppermute | solution.py:582
  22.6 0.0 copy-done.1
  22.7 1.9 %collective-permute-start.2 = (f32[100,256]{1,0:T(8,128)S(1)}, f32[100,256]{1,0:T(8,128)S(1)}, u32[]{:S(2)}, u32[]{:S(2)}) collective-permute-start(f32[100,256]{1,0:T(8,128)S(1)} %get-tuple-element.53), channel_id=1, source_target_pairs={{0,31},{1,2},{2,1},{3,4},{4,3},{5,6},{6,5},{7,8},{8,7},{9,10},{10,... | collective-permute-start | bytes 307208 | tf_op jit(solution)/shard_map/ppermute | solution.py:583
  24.6 3.5 %collective-permute-start.3 = (f32[100,256]{1,0:T(8,128)S(1)}, f32[100,256]{1,0:T(8,128)S(1)}, u32[]{:S(2)}, u32[]{:S(2)}) collective-permute-start(f32[100,256]{1,0:T(8,128)S(1)} %get-tuple-element.54), channel_id=1, source_target_pairs={{0,1},{1,0},{2,3},{3,2},{4,5},{5,4},{6,7},{7,6},{8,9},{9,8},{10,11... | collective-permute-start | bytes 307208 | tf_op jit(solution)/shard_map/ppermute | solution.py:582
  28.1 1.2 %joint.1 = (f32[54,256]{1,0:T(8,128)S(1)}, f32[54,256]{1,0:T(8,128)S(1)}, f32[18,256]{1,0:T(8,128)S(1)}, f32[18,256]{1,0:T(8,128)S(1)}) custom-call(s32[4,3]{1,0:T(4,128)S(1)} %copy-done, s32[2,128,256]{2,1,0:T(8,128)S(1)} %get-tuple-element.45.code_ref.refs_1_), custom_call_target="tpu_custom_call" | custom-call | bytes 8000000 | tf_op jit(solution)/shard_map/joint/pallas_call | solution.py:618
  29.3 1.6 %collective-permute-done.2.from_odd_ref = f32[100,256]{1,0:T(8,128)S(1)} collective-permute-done((f32[100,256]{1,0:T(8,128)S(1)}, f32[100,256]{1,0:T(8,128)S(1)}, u32[]{:S(2)}, u32[]{:S(2)}) %collective-permute-start.2) | collective-permute-done | bytes 102432 | tf_op jit(solution)/shard_map/ppermute | solution.py:583
  30.8 0.0 collective-permute-done.3.from_even_ref
  30.8 1.1 %first.1 = (f32[32,256]{1,0:T(8,128)S(1)}, f32[32,256]{1,0:T(8,128)S(1)}, f32[2,48,256]{2,1,0:T(8,128)S(1)}, f32[24,256]{1,0:T(8,128)S(1)}, f32[12,256]{1,0:T(8,128)S(1)}, /*index=5*/f32[12,256]{1,0:T(8,128)S(1)}) custom-call(s32[4,3]{1,0:T(4,128)S(1)} %copy-done, f32[24,256]{1,0:T(8,128)S(1)} %get-tuple-element.52.sums_ref, ...), custom_call_target="tpu_custom_call" | custom-call | tf_op jit(solution)/shard_map/first/pallas_call | solution.py:621
  31.9 3.3 %collective-permute-start.4 = (f32[12,256]{1,0:T(8,128)S(1)}, f32[12,256]{1,0:T(8,128)S(1)}, u32[]{:S(2)}, u32[]{:S(2)}) collective-permute-start(f32[12,256]{1,0:T(8,128)S(1)} %get-tuple-element.62), channel_id=1, source_target_pairs={{0,480},{32,64},{64,32},{96,128},{128,96},{160,192},{192,160},{224... | collective-permute-start | bytes 36872 | tf_op jit(solution)/shard_map/ppermute | solution.py:583
  35.3 1.9 %collective-permute-start.5 = (f32[12,256]{1,0:T(8,128)S(1)}, f32[12,256]{1,0:T(8,128)S(1)}, u32[]{:S(2)}, u32[]{:S(2)}) collective-permute-start(f32[12,256]{1,0:T(8,128)S(1)} %get-tuple-element.63), channel_id=1, source_target_pairs={{0,32},{32,0},{64,96},{96,64},{128,160},{160,128},{192,224},{224,1... | collective-permute-start | bytes 36872 | tf_op jit(solution)/shard_map/ppermute | solution.py:582
  37.2 2.2 %turn1.1 = (f32[6,128,256]{2,1,0:T(8,128)S(1)}, f32[3,8,256]{2,1,0:T(8,128)S(1)}, f32[128,256]{1,0:T(8,128)S(1)}) custom-call(s32[4,3]{1,0:T(4,128)S(1)} %copy-done, s32[2,128,256]{2,1,0:T(8,128)S(1)} %get-tuple-element.45.code_ref.refs_1_, f32[32,256]{1,0:T(8,128)S(1)} %get-tuple-element.58.refs_2_, f32[6,128,256]{2,1,0:T(8,128)S(1)} %get-tuple-element.49.vel_ref.refs_3_, ...), custom_call_target="tpu_custom_call" | custom-call | bytes 8000000 | tf_op jit(solution)/shard_map/turn1/pallas_call | solution.py:637
  39.4 2.3 %collective-permute-done.4.from_odd_ref = f32[12,256]{1,0:T(8,128)S(1)} collective-permute-done((f32[12,256]{1,0:T(8,128)S(1)}, f32[12,256]{1,0:T(8,128)S(1)}, u32[]{:S(2)}, u32[]{:S(2)}) %collective-permute-start.4) | collective-permute-done | bytes 12320 | tf_op jit(solution)/shard_map/ppermute | solution.py:583
  41.8 0.0 collective-permute-done.5.from_even_ref
  41.8 0.3 shift1.1
  42.1 6.7 %collective-permute-start.6 = (f32[12,256]{1,0:T(8,128)S(1)}, f32[12,256]{1,0:T(8,128)S(1)}, u32[]{:S(2)}, u32[]{:S(2)}) collective-permute-start(f32[12,256]{1,0:T(8,128)S(1)} %get-tuple-element.70), channel_id=1, source_target_pairs={{0,480},{32,64},{64,32},{96,128},{128,96},{160,192},{192,160},{224... | collective-permute-start | bytes 36872 | tf_op jit(solution)/shard_map/ppermute | solution.py:583
  48.8 1.9 %collective-permute-start.7 = (f32[12,256]{1,0:T(8,128)S(1)}, f32[12,256]{1,0:T(8,128)S(1)}, u32[]{:S(2)}, u32[]{:S(2)}) collective-permute-start(f32[12,256]{1,0:T(8,128)S(1)} %get-tuple-element.71), channel_id=1, source_target_pairs={{0,32},{32,0},{64,96},{96,64},{128,160},{160,128},{192,224},{224,1... | collective-permute-start | bytes 36872 | tf_op jit(solution)/shard_map/ppermute | solution.py:582
  50.7 1.7 %turn2.1 = (f32[6,128,256]{2,1,0:T(8,128)S(1)}, f32[3,16,256]{2,1,0:T(8,128)S(1)}, f32[24,256]{1,0:T(8,128)S(1)}) custom-call(s32[4,3]{1,0:T(4,128)S(1)} %copy-done, s32[2,128,256]{2,1,0:T(8,128)S(1)} %get-tuple-element.45.code_ref.refs_1_, f32[32,256]{1,0:T(8,128)S(1)} %get-tuple-element.58.refs_2_, f32[6,128,256]{2,1,0:T(8,128)S(1)} %get-tuple-element.60.refs_3_, ...), custom_call_target="tpu_custom_call" | custom-call | bytes 8000000 | tf_op jit(solution)/shard_map/turn2/pallas_call | solution.py:637
  52.4 0.0 collective-permute-done.6.from_odd_ref
  52.4 2.9 %collective-permute-done.7.from_even_ref = f32[12,256]{1,0:T(8,128)S(1)} collective-permute-done((f32[12,256]{1,0:T(8,128)S(1)}, f32[12,256]{1,0:T(8,128)S(1)}, u32[]{:S(2)}, u32[]{:S(2)}) %collective-permute-start.7) | collective-permute-done | bytes 12320 | tf_op jit(solution)/shard_map/ppermute | solution.py:582
  55.4 1.9 %collective-permute-start.8 = (f32[42,256]{1,0:T(8,128)S(1)}, f32[42,256]{1,0:T(8,128)S(1)}, u32[]{:S(2)}, u32[]{:S(2)}) collective-permute-start(f32[42,256]{1,0:T(8,128)S(1)} %get-tuple-element.76), channel_id=1, source_target_pairs={{0,31},{1,2},{2,1},{3,4},{4,3},{5,6},{6,5},{7,8},{8,7},{9,10},{10,... | collective-permute-start | bytes 129032 | tf_op jit(solution)/shard_map/ppermute | solution.py:583
  57.3 2.0 %collective-permute-start.9 = (f32[42,256]{1,0:T(8,128)S(1)}, f32[42,256]{1,0:T(8,128)S(1)}, u32[]{:S(2)}, u32[]{:S(2)}) collective-permute-start(f32[42,256]{1,0:T(8,128)S(1)} %get-tuple-element.77), channel_id=1, source_target_pairs={{0,1},{1,0},{2,3},{3,2},{4,5},{5,4},{6,7},{7,6},{8,9},{9,8},{10,11... | collective-permute-start | bytes 129032 | tf_op jit(solution)/shard_map/ppermute | solution.py:582
  59.3 3.6 %collective-permute-done.8.from_odd_ref = f32[42,256]{1,0:T(8,128)S(1)} collective-permute-done((f32[42,256]{1,0:T(8,128)S(1)}, f32[42,256]{1,0:T(8,128)S(1)}, u32[]{:S(2)}, u32[]{:S(2)}) %collective-permute-start.8) | collective-permute-done | bytes 43040 | tf_op jit(solution)/shard_map/ppermute | solution.py:583
  62.9 0.0 collective-permute-done.9.from_even_ref
  62.9 0.3 shift2.1
  63.2 3.3 %collective-permute-start.10 = (f32[12,256]{1,0:T(8,128)S(1)}, f32[12,256]{1,0:T(8,128)S(1)}, u32[]{:S(2)}, u32[]{:S(2)}) collective-permute-start(f32[12,256]{1,0:T(8,128)S(1)} %get-tuple-element.83), channel_id=1, source_target_pairs={{0,480},{32,64},{64,32},{96,128},{128,96},{160,192},{192,160},{224... | collective-permute-start | bytes 36872 | tf_op jit(solution)/shard_map/ppermute | solution.py:583
  66.6 1.9 %collective-permute-start.11 = (f32[12,256]{1,0:T(8,128)S(1)}, f32[12,256]{1,0:T(8,128)S(1)}, u32[]{:S(2)}, u32[]{:S(2)}) collective-permute-start(f32[12,256]{1,0:T(8,128)S(1)} %get-tuple-element.84), channel_id=1, source_target_pairs={{0,32},{32,0},{64,96},{96,64},{128,160},{160,128},{192,224},{224,1... | collective-permute-start | bytes 36872 | tf_op jit(solution)/shard_map/ppermute | solution.py:582
  68.5 0.9 %turn3.1 = (f32[6,128,256]{2,1,0:T(8,128)S(1)}, f32[3,8,256]{2,1,0:T(8,128)S(1)}) custom-call(s32[4,3]{1,0:T(4,128)S(1)} %copy-done, s32[2,128,256]{2,1,0:T(8,128)S(1)} %get-tuple-element.45.code_ref.refs_1_, f32[32,256]{1,0:T(8,128)S(1)} %get-tuple-element.58.refs_2_, f32[6,128,256]{2,1,0:T(8,128)S(1)} %get-tuple-element.68.refs_3_, ...), custom_call_target="tpu_custom_call" | custom-call | bytes 8000000 | tf_op jit(solution)/shard_map/turn3/pallas_call | solution.py:637
  69.5 3.6 %collective-permute-done.10.from_odd_ref = f32[12,256]{1,0:T(8,128)S(1)} collective-permute-done((f32[12,256]{1,0:T(8,128)S(1)}, f32[12,256]{1,0:T(8,128)S(1)}, u32[]{:S(2)}, u32[]{:S(2)}) %collective-permute-start.10) | collective-permute-done | bytes 12320 | tf_op jit(solution)/shard_map/ppermute | solution.py:583
  73.1 0.0 collective-permute-done.11.from_even_ref
  73.1 1.4 %last.1 = (bf16[3,2,256,128]{3,2,1,0:T(8,128)(2,1)}, f32[3,2,256]{2,1,0:T(2,128)}) custom-call(s32[4,3]{1,0:T(4,128)S(1)} %copy-done, s32[2,128,256]{2,1,0:T(8,128)S(1)} %get-tuple-element.45.code_ref.refs_1_, f32[6,128,256]{2,1,0:T(8,128)S(1)} %get-tuple-element.81.vel_ref, f32[24,256]{1,0:T(8,128)S(1)} %get-tuple-element.82.sums_ref, ...), custom_call_target="tpu_custom_call" | custom-call | tf_op jit(solution)/shard_map/last/pallas_call | solution.py:641
  (2 shorter events, 0.1 us)
Async XLA Ops:
  2.9 18.1 %collective-permute-start = (f32[20,256]{1,0:T(8,128)S(1)}, f32[20,256]{1,0:T(8,128)S(1)}, u32[]{:S(2)}, u32[]{:S(2)}) collective-permute-start(f32[20,256]{1,0:T(8,128)S(1)} %get-tuple-element.47), channel_id=1, source_target_pairs={{0,480},{32,64},{64,32},{96,128},{128,96},{160,192},{192,160},{224... | collective-permute-start | bytes 61448 | tf_op jit(solution)/shard_map/ppermute | solution.py:583
  16.0 1.9 %copy-start = (s32[4,3]{1,0:T(4,128)S(1)}, s32[4,3]{1,0:T(4,128)}, u32[]{:S(2)}) copy-start(s32[4,3]{1,0:T(4,128)} %shifts_ref.11) | copy-start | bytes 148
  16.0 6.6 %collective-permute-start.1 = (f32[20,256]{1,0:T(8,128)S(1)}, f32[20,256]{1,0:T(8,128)S(1)}, u32[]{:S(2)}, u32[]{:S(2)}) collective-permute-start(f32[20,256]{1,0:T(8,128)S(1)} %get-tuple-element.48), channel_id=1, source_target_pairs={{0,32},{32,0},{64,96},{96,64},{128,160},{160,128},{192,224},{224,1... | collective-permute-start | bytes 61448 | tf_op jit(solution)/shard_map/ppermute | solution.py:582
  17.9 4.7 %copy-start.1 = (s32[4,1,2,256]{3,2,1,0:T(2,128)S(1)}, s32[4,1,2,256]{3,2,1,0:T(2,128)}, u32[]{:S(2)}) copy-start(s32[4,1,2,256]{3,2,1,0:T(2,128)} %param.9) | copy-start | bytes 24580
  22.7 8.1 %collective-permute-start.2 = (f32[100,256]{1,0:T(8,128)S(1)}, f32[100,256]{1,0:T(8,128)S(1)}, u32[]{:S(2)}, u32[]{:S(2)}) collective-permute-start(f32[100,256]{1,0:T(8,128)S(1)} %get-tuple-element.53), channel_id=1, source_target_pairs={{0,31},{1,2},{2,1},{3,4},{4,3},{5,6},{6,5},{7,8},{8,7},{9,10},{10,... | collective-permute-start | bytes 307208 | tf_op jit(solution)/shard_map/ppermute | solution.py:583
  24.6 6.2 %collective-permute-start.3 = (f32[100,256]{1,0:T(8,128)S(1)}, f32[100,256]{1,0:T(8,128)S(1)}, u32[]{:S(2)}, u32[]{:S(2)}) collective-permute-start(f32[100,256]{1,0:T(8,128)S(1)} %get-tuple-element.54), channel_id=1, source_target_pairs={{0,1},{1,0},{2,3},{3,2},{4,5},{5,4},{6,7},{7,6},{8,9},{9,8},{10,11... | collective-permute-start | bytes 307208 | tf_op jit(solution)/shard_map/ppermute | solution.py:582
  31.9 9.9 %collective-permute-start.4 = (f32[12,256]{1,0:T(8,128)S(1)}, f32[12,256]{1,0:T(8,128)S(1)}, u32[]{:S(2)}, u32[]{:S(2)}) collective-permute-start(f32[12,256]{1,0:T(8,128)S(1)} %get-tuple-element.62), channel_id=1, source_target_pairs={{0,480},{32,64},{64,32},{96,128},{128,96},{160,192},{192,160},{224... | collective-permute-start | bytes 36872 | tf_op jit(solution)/shard_map/ppermute | solution.py:583
  35.3 6.5 %collective-permute-start.5 = (f32[12,256]{1,0:T(8,128)S(1)}, f32[12,256]{1,0:T(8,128)S(1)}, u32[]{:S(2)}, u32[]{:S(2)}) collective-permute-start(f32[12,256]{1,0:T(8,128)S(1)} %get-tuple-element.63), channel_id=1, source_target_pairs={{0,32},{32,0},{64,96},{96,64},{128,160},{160,128},{192,224},{224,1... | collective-permute-start | bytes 36872 | tf_op jit(solution)/shard_map/ppermute | solution.py:582
  42.1 10.4 %collective-permute-start.6 = (f32[12,256]{1,0:T(8,128)S(1)}, f32[12,256]{1,0:T(8,128)S(1)}, u32[]{:S(2)}, u32[]{:S(2)}) collective-permute-start(f32[12,256]{1,0:T(8,128)S(1)} %get-tuple-element.70), channel_id=1, source_target_pairs={{0,480},{32,64},{64,32},{96,128},{128,96},{160,192},{192,160},{224... | collective-permute-start | bytes 36872 | tf_op jit(solution)/shard_map/ppermute | solution.py:583
  48.8 6.5 %collective-permute-start.7 = (f32[12,256]{1,0:T(8,128)S(1)}, f32[12,256]{1,0:T(8,128)S(1)}, u32[]{:S(2)}, u32[]{:S(2)}) collective-permute-start(f32[12,256]{1,0:T(8,128)S(1)} %get-tuple-element.71), channel_id=1, source_target_pairs={{0,32},{32,0},{64,96},{96,64},{128,160},{160,128},{192,224},{224,1... | collective-permute-start | bytes 36872 | tf_op jit(solution)/shard_map/ppermute | solution.py:582
  55.4 7.5 %collective-permute-start.8 = (f32[42,256]{1,0:T(8,128)S(1)}, f32[42,256]{1,0:T(8,128)S(1)}, u32[]{:S(2)}, u32[]{:S(2)}) collective-permute-start(f32[42,256]{1,0:T(8,128)S(1)} %get-tuple-element.76), channel_id=1, source_target_pairs={{0,31},{1,2},{2,1},{3,4},{4,3},{5,6},{6,5},{7,8},{8,7},{9,10},{10,... | collective-permute-start | bytes 129032 | tf_op jit(solution)/shard_map/ppermute | solution.py:583
  57.3 5.6 %collective-permute-start.9 = (f32[42,256]{1,0:T(8,128)S(1)}, f32[42,256]{1,0:T(8,128)S(1)}, u32[]{:S(2)}, u32[]{:S(2)}) collective-permute-start(f32[42,256]{1,0:T(8,128)S(1)} %get-tuple-element.77), channel_id=1, source_target_pairs={{0,1},{1,0},{2,3},{3,2},{4,5},{5,4},{6,7},{7,6},{8,9},{9,8},{10,11... | collective-permute-start | bytes 129032 | tf_op jit(solution)/shard_map/ppermute | solution.py:582
  63.2 9.8 %collective-permute-start.10 = (f32[12,256]{1,0:T(8,128)S(1)}, f32[12,256]{1,0:T(8,128)S(1)}, u32[]{:S(2)}, u32[]{:S(2)}) collective-permute-start(f32[12,256]{1,0:T(8,128)S(1)} %get-tuple-element.83), channel_id=1, source_target_pairs={{0,480},{32,64},{64,32},{96,128},{128,96},{160,192},{192,160},{224... | collective-permute-start | bytes 36872 | tf_op jit(solution)/shard_map/ppermute | solution.py:583
  66.6 6.5 %collective-permute-start.11 = (f32[12,256]{1,0:T(8,128)S(1)}, f32[12,256]{1,0:T(8,128)S(1)}, u32[]{:S(2)}, u32[]{:S(2)}) collective-permute-start(f32[12,256]{1,0:T(8,128)S(1)} %get-tuple-element.84), channel_id=1, source_target_pairs={{0,32},{32,0},{64,96},{96,64},{128,160},{160,128},{192,224},{224,1... | collective-permute-start | bytes 36872 | tf_op jit(solution)/shard_map/ppermute | solution.py:582
